TPU v7x, 32 devices: a whole 2x2x4 slice. The times are simulated.
32 devices in a mesh: groups: 2 (over y), shard: 8 (over z, x), sub: 2 (over core).
Axes of the slice: x: 2, y: 2, z: 4, core: 2. Of those that a mesh axis runs over, the one named last changes fastest.
Arguments:
- query_hidden_states: bfloat16 [384, 32, 4096], P(('groups', 'shard'), None, 'sub'), parts along dimension 0, may hold values from -6 to 6
- passage_hidden_states: bfloat16 [32, 256, 4096], P(('groups', 'shard'), None, 'sub'), parts along dimension 0, may hold values from -6 to 6
- projection_matrix: bfloat16 [4096, 128], P('sub'), may hold values from -0.09375 to 0.09375
- adapter_down_weight: bfloat16 [4096, 16], P('sub'), may hold values from -0.09375 to 0.09375
- adapter_up_weight: bfloat16 [16, 128], replicated, may hold values from -1.5 to 1.5
- passage_pair_index: int32 [384, 9], P(('groups', 'shard')), parts along dimension 0, may hold values from 0 to 15, as said below
- passage_row_table: int32 [32], P('groups'), parts along dimension 0, may hold values from 0 to 15, as said below
Outputs:
- query_loss: float32 [384], P(('groups', 'shard', 'sub')), parts along dimension 0
- grad_down: float32 [8192, 16], P(('groups', 'sub')), parts along dimension 0
- grad_up: float32 [32, 128], P('groups'), parts along dimension 0
There are 2 independent parts, one for each index of `groups`. A program takes and returns all parts, laid end to end along the dimension named above; an argument that names none is the same for every part. Nothing has to cross between parts.
Inputs may be any that keep to these rules, and one draw needn't show every extreme that they name: A permutation: passage id p is stored in row passage_row_table[p] of passage_hidden_states. `passage_pair_index`: query rows form aligned blocks of 12; among the 108 candidates of one block, at most 14 are stored in one owner's rows (rows r with the same r // 2), and in every block some owner holds exactly 14 of them. Candidates of one query may repeat.
All inputs are finite; a program needn't handle non-finite values.
Results may differ from a plain program's by a relative error of at most 0.012.
The roundings to bfloat16 on the way count: a program that leaves them out, or rounds other values in their place, can miss the bound.
Values may be sent and summed in bfloat16 or wider, within the bound.
No kernel may reach another device: no remote copies, remote signals or barrier semaphores. Data moves between devices by JAX's collectives and lax.ppermute only.
A program may use at most 128 MiB of HBM per device.

v0:
```python
import math

import jax
import jax.numpy as jnp
from jax import lax
from jax.sharding import PartitionSpec as P

pool_temp = 0.05
loss_temp = 0.05
norm_eps = 1e-06


def finish_vectors(frozen_output, adapter_output, adapter_up_weight):
    adapter_output_brain = adapter_output.astype(jnp.bfloat16)
    combined_output = frozen_output + jnp.dot(
        adapter_output_brain, adapter_up_weight, preferred_element_type=jnp.float32
    )
    factor = lax.rsqrt(
        jnp.sum(combined_output * combined_output, axis=-1, keepdims=True) + norm_eps
    )
    return (adapter_output_brain, combined_output, (combined_output * factor).astype(jnp.bfloat16))


def unnormalize(combined_output, grad):
    factor = lax.rsqrt(
        jnp.sum(combined_output * combined_output, axis=-1, keepdims=True) + norm_eps
    )
    inner = jnp.sum(combined_output * grad, axis=-1, keepdims=True)
    return factor * grad - factor * factor * factor * inner * combined_output


def per_device(
    query_hidden_states,
    passage_hidden_states,
    projection_matrix,
    adapter_down_weight,
    adapter_up_weight,
    passage_pair_index,
    passage_row_table,
):
    nshard = lax.axis_size("shard")
    nsub = lax.axis_size("sub")
    core = lax.axis_index("sub")
    qdev, qlen, dhalf = query_hidden_states.shape
    pdev, plen, unused_width = passage_hidden_states.shape
    width = projection_matrix.shape[1]
    cands = passage_pair_index.shape[1]
    half = qdev // nsub
    pairs = half * cands
    cap = max(2, (pairs + nshard - 1) // nshard)
    slots = nshard * cap
    per_block = cap * math.gcd(nshard, max(1, 32 // cap))
    nblocks = slots // per_block
    query_flat_rows = query_hidden_states.reshape(qdev * qlen, dhalf)
    passage_flat_rows = passage_hidden_states.reshape(pdev * plen, dhalf)
    frozen_query = jnp.dot(query_flat_rows, projection_matrix, preferred_element_type=jnp.float32)
    adapter_query = jnp.dot(
        query_flat_rows, adapter_down_weight, preferred_element_type=jnp.float32
    )
    frozen_passage = jnp.dot(
        passage_flat_rows, projection_matrix, preferred_element_type=jnp.float32
    )
    adapter_passage = jnp.dot(
        passage_flat_rows, adapter_down_weight, preferred_element_type=jnp.float32
    )
    frozen_query, adapter_query, frozen_passage, adapter_passage = lax.psum(
        (frozen_query, adapter_query, frozen_passage, adapter_passage), "sub"
    )
    adapter_query_brain, combined_query, query_token_vectors = finish_vectors(
        frozen_query, adapter_query, adapter_up_weight
    )
    adapter_passage_brain, combined_passage, passage_token_vectors = finish_vectors(
        frozen_passage, adapter_passage, adapter_up_weight
    )
    mine = lax.dynamic_slice_in_dim(
        query_token_vectors.reshape(qdev, qlen * width), core * half, half, 0
    )
    my_ids = lax.dynamic_slice_in_dim(passage_pair_index, core * half, half, 0)
    rows = passage_row_table[my_ids].reshape(pairs)
    owner = rows // pdev
    local = rows % pdev
    member = (owner[:, None] == jnp.arange(nshard, dtype=jnp.int32)[None, :]).astype(jnp.int32)
    earlier = jnp.cumsum(member, axis=0) - member
    rank = jnp.sum(earlier * member, axis=1)
    slot = owner * cap + rank
    asker = jnp.arange(pairs, dtype=jnp.int32) // cands
    send_vec = jnp.zeros((slots, qlen * width), jnp.bfloat16).at[slot].set(mine[asker])
    send_loc = jnp.full((slots,), pdev, jnp.bfloat16).at[slot].set(local.astype(jnp.bfloat16))
    recv_vec, recv_loc = (
        lax.all_to_all(send_vec, "shard", split_axis=0, concat_axis=0, tiled=True),
        lax.all_to_all(send_loc, "shard", split_axis=0, concat_axis=0, tiled=True),
    )
    loc_int = recv_loc.astype(jnp.int32)
    select = (loc_int[:, None] == jnp.arange(pdev, dtype=jnp.int32)[None, :]).astype(jnp.float32)
    bank3 = passage_token_vectors.reshape(pdev, plen, width)
    incoming = recv_vec.reshape(nblocks, per_block, qlen, width)
    select_blocks = select.reshape(nblocks, per_block, pdev)

    def forward(item):
        inc, sel = item
        chosen = jnp.einsum(
            "sp,pje->sje", sel.astype(jnp.bfloat16), bank3, preferred_element_type=jnp.float32
        ).astype(jnp.bfloat16)
        sims = jnp.einsum("sie,sje->sij", inc, chosen, preferred_element_type=jnp.float32)
        expo = jnp.exp(sims / pool_temp)
        total = jnp.sum(expo, axis=-1)
        live = jnp.sum(sel, axis=1)
        score = pool_temp * jnp.mean(jnp.log(total), axis=1) * live
        weights = (expo / total[..., None] * live[:, None, None]).astype(jnp.bfloat16)
        unit = (
            jnp.einsum("sij,sje->sie", weights, chosen, preferred_element_type=jnp.float32) / qlen
        ).astype(jnp.bfloat16)
        return (score, unit, weights)

    score, unit, weights = lax.map(forward, (incoming, select_blocks))
    score = score.reshape(slots)
    unit = unit.reshape(slots, qlen * width)
    back_scores = lax.all_to_all(score, "shard", split_axis=0, concat_axis=0, tiled=True)
    logits = back_scores[slot].reshape(half, cands) / loss_temp
    summed = jnp.sum(jnp.exp(logits), axis=-1)
    query_loss = jnp.log(summed) - logits[:, 0]
    first = (jnp.arange(cands) == 0).astype(jnp.float32)
    dscore = (jnp.exp(logits) / summed[:, None] - first[None, :]) / loss_temp
    send_grad = jnp.zeros((slots,), jnp.float32).at[slot].set(dscore.reshape(pairs))
    recv_grad = lax.all_to_all(send_grad, "shard", split_axis=0, concat_axis=0, tiled=True)
    back_unit = lax.all_to_all(unit, "shard", split_axis=0, concat_axis=0, tiled=True)

    def backward(acc, item):
        inc, sel, wts, grads = item
        gradw = (wts * (grads / qlen)[:, None, None]).astype(jnp.bfloat16)
        contrib = jnp.einsum("sij,sie->sje", gradw, inc, preferred_element_type=jnp.float32)
        added = jnp.einsum("sp,sje->pje", sel, contrib, precision=lax.Precision.HIGHEST)
        return (acc + added, None)

    grad_bank, unused_out = lax.scan(
        backward,
        jnp.zeros((pdev, plen, width), jnp.float32),
        (incoming, select_blocks, weights, recv_grad.reshape(nblocks, per_block)),
    )
    grad_bank = grad_bank.reshape(pdev * plen, width)
    per_pair = back_unit[slot].astype(jnp.float32) * dscore.reshape(pairs)[:, None]
    grad_mine = jnp.sum(per_pair.reshape(half, cands, qlen * width), axis=1)
    padded = lax.dynamic_update_slice_in_dim(
        jnp.zeros((qdev, qlen * width), jnp.float32), grad_mine, core * half, 0
    )
    grad_vq, grad_vp = lax.psum((padded, grad_bank), "sub")
    dfull_q = unnormalize(combined_query, grad_vq.reshape(qdev * qlen, width))
    dfull_p = unnormalize(combined_passage, grad_vp)
    up_weight_float = adapter_up_weight.astype(jnp.float32)
    grad_up = jnp.dot(
        adapter_query_brain.astype(jnp.float32).T, dfull_q, precision=lax.Precision.HIGHEST
    )
    grad_up = grad_up + jnp.dot(
        adapter_passage_brain.astype(jnp.float32).T, dfull_p, precision=lax.Precision.HIGHEST
    )
    dlow_q = jnp.dot(dfull_q, up_weight_float.T, precision=lax.Precision.HIGHEST).astype(
        jnp.bfloat16
    )
    dlow_p = jnp.dot(dfull_p, up_weight_float.T, precision=lax.Precision.HIGHEST).astype(
        jnp.bfloat16
    )
    grad_down = lax.dot_general(
        query_flat_rows, dlow_q, (((0,), (0,)), ((), ())), preferred_element_type=jnp.float32
    )
    grad_down = grad_down + lax.dot_general(
        passage_flat_rows, dlow_p, (((0,), (0,)), ((), ())), preferred_element_type=jnp.float32
    )
    grad_down, grad_up = lax.psum((grad_down, grad_up), "shard")
    return (query_loss, grad_down, grad_up)


def solution(mesh):
    placed = (
        P(("groups", "shard"), None, "sub"),
        P(("groups", "shard"), None, "sub"),
        P("sub", None),
        P("sub", None),
        P(),
        P(("groups", "shard"), None),
        P("groups"),
    )
    return jax.shard_map(
        per_device,
        mesh=mesh,
        in_specs=placed,
        out_specs=(P(("groups", "shard", "sub")), P(("groups", "sub"), None), P("groups", None)),
        check_vma=False,
    )
```

profile of v0, /device:TPU:0, one launch (start us, length us, event | category | flops | bytes accessed | tf_op | source)
XLA Modules:
  0.0 351.9 jit_solution(8618136964948613834)
XLA Ops:
  11.9 7.3 %all-to-all-start.1 = ((bf16[8,14,1]{1,2,0:T(2,128)(2,1)}), bf16[8,14,1]{1,2,0:T(2,128)(2,1)S(1)}, u32[]{:S(2)}, u32[]{:S(2)}) async-start(bf16[8,14,1]{1,2,0:T(2,128)(2,1)} %all_to_all.46), calls=%async_computation.1 | async-start | bytes 8192 | tf_op jit(solution)/shard_map/all_to_all | solution.py:91
  19.3 2.9 fusion.51
  23.7 2.2 fusion.54
  26.8 4.2 %all-reduce = (bf16[768,16]{0,1:T(8,128)(2,1)}, bf16[512,16]{0,1:T(8,128)(2,1)}) all-reduce(f32[768,16]{0,1:T(8,128)S(1)} %fusion.52, f32[512,16]{0,1:T(8,128)S(1)} %fusion.54), channel_id=1, replica_groups=mesh['groups'=2,'shard'=8,'sub'=2] {'sub'}, use_global_device_ids=true, to_apply=%region_3.0 | all-reduce | flops 20480 | bytes 122880 | tf_op jit(solution)/shard_map/psum | solution.py:66
  31.1 13.1 %all-reduce.11.cloned.1.call-done = (f32[768,128]{1,0:T(8,128)}, f32[512,128]{1,0:T(8,128)}) async-done(((f32[768,128]{1,0:T(8,128)}, f32[512,128]{1,0:T(8,128)}), (f32[768,128]{1,0:T(8,128)}, f32[512,128]{1,0:T(8,128)})) %all-reduce.11.cloned.1.call-update) | async-done | bytes 655376 | tf_op jit(solution)/shard_map/psum | solution.py:66
  47.6 1.7 reshape.317
  50.9 6.9 %scatter_custom_fusion = bf16[112,4096]{1,0:T(8,128)(2,1)} fusion(s32[108]{0:T(128)S(1)} %get-tuple-element.220, bf16[12,4096]{1,0:T(8,128)(2,1)} %constant_dynamic-slice_fusion.2, s32[1024]{0:T(1024)S(1)} %pad_clamp_fusion.1, bf16[]{:T(256)} %constant.124.clone.1), kind=kCustom, calls=%fused_computation.52 | custom fusion | bytes 918016 | tf_op jit(solution)/shard_map/scatter | solution.py:87
  57.8 2.5 all_to_all.34
  60.3 5.8 %all-to-all-start = ((bf16[8,14,4096]{2,1,0:T(8,128)(2,1)}), bf16[8,14,4096]{2,1,0:T(8,128)(2,1)}, u32[]{:S(2)}, u32[]{:S(2)}) async-start(bf16[8,14,4096]{2,1,0:T(8,128)(2,1)} %all_to_all.34), calls=%async_computation | async-start | bytes 2097152 | tf_op jit(solution)/shard_map/all_to_all | solution.py:90
  69.8 22.6 %all-to-all-done = bf16[8,14,4096]{2,1,0:T(8,128)(2,1)} async-done(((bf16[8,14,4096]{2,1,0:T(8,128)(2,1)}), bf16[8,14,4096]{2,1,0:T(8,128)(2,1)}, u32[]{:S(2)}, u32[]{:S(2)}) %all-to-all-start) | async-done | bytes 917536 | tf_op jit(solution)/shard_map/all_to_all | solution.py:90
  92.4 2.7 reshape.318
  95.1 51.4 %while.27 = (s32[]{:T(128)}, f32[4,28]{1,0:T(4,128)}, bf16[4,28,32,128]{3,2,1,0:T(8,128)(2,1)}, bf16[4,28,32,256]{3,2,1,0:T(8,128)(2,1)}, bf16[4,28,32,128]{3,2,...) while((s32[]{:T(128)}, f32[4,28]{1,0:T(4,128)}, ...), condition=%wide.region_14.15_spmd, body=%wide.region_10.14_spmd.sunk | while | flops 123174968 | bytes 20636092 | solution.py:115
  95.1 1.7 fusion.93
  98.1 3.0 fusion.94
  103.1 3.8 %fusion.95 = bf16[4,28,32,128]{3,2,1,0:T(8,128)(2,1)} fusion(bf16[4,28,32,128]{3,2,1,0:T(8,128)(2,1)} %get-tuple-element.316, s32[]{:T(128)S(6)} %copy.66, bf16[28,256,128]{2,0,1:T(8,128)(2,1)} %copy-done.2, f32[28,32,256]{2,1,0:T(8,128)} %get-tuple-element.298, f32[28]{0:T(128)S(1)} %fusion.92, f32[28,32]{1,0:T(8,128)} %copy-done.9), kind=kOutput, calls=%fused_computation.13.clone.1 | convolution fusion | flops 59637760 | bytes 3260532 | tf_op jit(solution)/shard_map/while/body/eval_jaxpr/sij,sje->sie/dot_general | solution.py:111
  107.9 1.7 fusion.93
  111.0 3.0 fusion.94
  116.0 3.8 %fusion.95 = bf16[4,28,32,128]{3,2,1,0:T(8,128)(2,1)} fusion(bf16[4,28,32,128]{3,2,1,0:T(8,128)(2,1)} %get-tuple-element.316, s32[]{:T(128)S(6)} %copy.66, bf16[28,256,128]{2,0,1:T(8,128)(2,1)} %copy-done.2, f32[28,32,256]{2,1,0:T(8,128)} %get-tuple-element.298, f32[28]{0:T(128)S(1)} %fusion.92, f32[28,32]{1,0:T(8,128)} %copy-done.9), kind=kOutput, calls=%fused_computation.13.clone.1 | convolution fusion | flops 59637760 | bytes 3260532 | tf_op jit(solution)/shard_map/while/body/eval_jaxpr/sij,sje->sie/dot_general | solution.py:111
  120.8 1.7 fusion.93
  123.8 3.0 fusion.94
  128.9 3.8 %fusion.95 = bf16[4,28,32,128]{3,2,1,0:T(8,128)(2,1)} fusion(bf16[4,28,32,128]{3,2,1,0:T(8,128)(2,1)} %get-tuple-element.316, s32[]{:T(128)S(6)} %copy.66, bf16[28,256,128]{2,0,1:T(8,128)(2,1)} %copy-done.2, f32[28,32,256]{2,1,0:T(8,128)} %get-tuple-element.298, f32[28]{0:T(128)S(1)} %fusion.92, f32[28,32]{1,0:T(8,128)} %copy-done.9), kind=kOutput, calls=%fused_computation.13.clone.1 | convolution fusion | flops 59637760 | bytes 3260532 | tf_op jit(solution)/shard_map/while/body/eval_jaxpr/sij,sje->sie/dot_general | solution.py:111
  136.7 3.0 fusion.94
  141.7 3.8 %fusion.95 = bf16[4,28,32,128]{3,2,1,0:T(8,128)(2,1)} fusion(bf16[4,28,32,128]{3,2,1,0:T(8,128)(2,1)} %get-tuple-element.316, s32[]{:T(128)S(6)} %copy.66, bf16[28,256,128]{2,0,1:T(8,128)(2,1)} %copy-done.2, f32[28,32,256]{2,1,0:T(8,128)} %get-tuple-element.298, f32[28]{0:T(128)S(1)} %fusion.92, f32[28,32]{1,0:T(8,128)} %copy-done.9), kind=kOutput, calls=%fused_computation.13.clone.1 | convolution fusion | flops 59637760 | bytes 3260532 | tf_op jit(solution)/shard_map/while/body/eval_jaxpr/sij,sje->sie/dot_general | solution.py:111
  147.8 3.6 %all-to-all-start.2 = ((f32[8,14,1]{1,2,0:T(1,128)}), f32[8,14,1]{1,2,0:T(1,128)S(1)}, u32[]{:S(2)}, u32[]{:S(2)}) async-start(f32[8,14,1]{1,2,0:T(1,128)} %bitcast.13), calls=%async_computation.2 | async-start | bytes 8192 | tf_op jit(solution)/shard_map/all_to_all | solution.py:118
  153.2 2.5 all_to_all.41
  155.7 2.2 all-to-all-done.2
  166.2 3.8 %all-to-all-start.4 = ((f32[8,14,1]{1,2,0:T(1,128)}), f32[8,14,1]{1,2,0:T(1,128)S(1)}, u32[]{:S(2)}, u32[]{:S(2)}) async-start(f32[8,14,1]{1,2,0:T(1,128)} %bitcast.111), calls=%async_computation.4 | async-start | bytes 8192 | tf_op jit(solution)/shard_map/all_to_all | solution.py:125
  171.3 5.1 %all-to-all-done.4 = f32[8,14,1]{1,2,0:T(1,128)S(1)} async-done(((f32[8,14,1]{1,2,0:T(1,128)}), f32[8,14,1]{1,2,0:T(1,128)S(1)}, u32[]{:S(2)}, u32[]{:S(2)}) %all-to-all-start.4) | async-done | bytes 480 | tf_op jit(solution)/shard_map/all_to_all | solution.py:125
  176.4 4.2 %all-to-all-start.3 = ((bf16[8,14,4096]{2,1,0:T(8,128)(2,1)}), bf16[8,14,4096]{2,1,0:T(8,128)(2,1)}, u32[]{:S(2)}, u32[]{:S(2)}) async-start(bf16[8,14,4096]{2,1,0:T(8,128)(2,1)} %all_to_all.41), calls=%async_computation.3 | async-start | bytes 2097152 | tf_op jit(solution)/shard_map/all_to_all | solution.py:126
  182.9 42.4 %while.28 = (s32[]{:T(128)}, f32[2,256,128]{2,0,1:T(2,128)}, f32[4,28,2]{1,2,0:T(2,128)S(1)}, bf16[4,28,32,256]{3,2,1,0:T(8,128)(2,1)}, f32[4,28]{1,0:T(4,128)S(...) while((s32[]{:T(128)}, f32[2,256,128]{2,0,1:T(2,128)}, ...), condition=%wide.region_21.22_spmd.clone, body=%wide.region_20.21_spmd.clone.sunk | while | flops 81559584 | bytes 8554943 | solution.py:135
  182.9 3.8 %fusion.101 = f32[28,256,128]{2,1,0:T(8,128)} fusion(f32[28]{0:T(128)S(1)} %fusion.100, bf16[4,28,32,256]{3,2,1,0:T(8,128)(2,1)} %get-tuple-element.351, s32[]{:T(128)S(6)} %copy.77, bf16[4,28,32,128]{3,2,1,0:T(8,128)(2,1)} %get-tuple-element.353), kind=kOutput, calls=%fused_computation.31.clone.1 | convolution fusion | flops 59408384 | bytes 4359280 | tf_op jit(solution)/shard_map/while/body/eval_jaxpr/sij,sie->sje/dot_general | solution.py:131
  186.7 6.8 %fusion.102 = f32[2,256,128]{2,0,1:T(2,128)} fusion(f32[28,256,128]{2,1,0:T(8,128)} %fusion.101, f32[2,256,128]{2,0,1:T(2,128)} %get-tuple-element.341, pred[]{:T(512)S(6)} %compare.18, f32[4,28,2]{1,2,0:T(2,128)S(1)} %get-tuple-element.350, s32[]{:T(128)S(6)} %copy.77), kind=kOutput, calls=%fused_computation.28.clone.1 | convolution fusion | flops 22151168 | bytes 4195333 | tf_op jit(solution)/shard_map/while/body/eval_jaxpr/sp,sje->pje/dot_general | solution.py:132
  193.5 3.8 %fusion.101 = f32[28,256,128]{2,1,0:T(8,128)} fusion(f32[28]{0:T(128)S(1)} %fusion.100, bf16[4,28,32,256]{3,2,1,0:T(8,128)(2,1)} %get-tuple-element.351, s32[]{:T(128)S(6)} %copy.77, bf16[4,28,32,128]{3,2,1,0:T(8,128)(2,1)} %get-tuple-element.353), kind=kOutput, calls=%fused_computation.31.clone.1 | convolution fusion | flops 59408384 | bytes 4359280 | tf_op jit(solution)/shard_map/while/body/eval_jaxpr/sij,sie->sje/dot_general | solution.py:131
  197.3 6.8 %fusion.102 = f32[2,256,128]{2,0,1:T(2,128)} fusion(f32[28,256,128]{2,1,0:T(8,128)} %fusion.101, f32[2,256,128]{2,0,1:T(2,128)} %get-tuple-element.341, pred[]{:T(512)S(6)} %compare.18, f32[4,28,2]{1,2,0:T(2,128)S(1)} %get-tuple-element.350, s32[]{:T(128)S(6)} %copy.77), kind=kOutput, calls=%fused_computation.28.clone.1 | convolution fusion | flops 22151168 | bytes 4195333 | tf_op jit(solution)/shard_map/while/body/eval_jaxpr/sp,sje->pje/dot_general | solution.py:132
  204.1 3.8 %fusion.101 = f32[28,256,128]{2,1,0:T(8,128)} fusion(f32[28]{0:T(128)S(1)} %fusion.100, bf16[4,28,32,256]{3,2,1,0:T(8,128)(2,1)} %get-tuple-element.351, s32[]{:T(128)S(6)} %copy.77, bf16[4,28,32,128]{3,2,1,0:T(8,128)(2,1)} %get-tuple-element.353), kind=kOutput, calls=%fused_computation.31.clone.1 | convolution fusion | flops 59408384 | bytes 4359280 | tf_op jit(solution)/shard_map/while/body/eval_jaxpr/sij,sie->sje/dot_general | solution.py:131
  207.9 6.8 %fusion.102 = f32[2,256,128]{2,0,1:T(2,128)} fusion(f32[28,256,128]{2,1,0:T(8,128)} %fusion.101, f32[2,256,128]{2,0,1:T(2,128)} %get-tuple-element.341, pred[]{:T(512)S(6)} %compare.18, f32[4,28,2]{1,2,0:T(2,128)S(1)} %get-tuple-element.350, s32[]{:T(128)S(6)} %copy.77), kind=kOutput, calls=%fused_computation.28.clone.1 | convolution fusion | flops 22151168 | bytes 4195333 | tf_op jit(solution)/shard_map/while/body/eval_jaxpr/sp,sje->pje/dot_general | solution.py:132
  214.8 3.8 %fusion.101 = f32[28,256,128]{2,1,0:T(8,128)} fusion(f32[28]{0:T(128)S(1)} %fusion.100, bf16[4,28,32,256]{3,2,1,0:T(8,128)(2,1)} %get-tuple-element.351, s32[]{:T(128)S(6)} %copy.77, bf16[4,28,32,128]{3,2,1,0:T(8,128)(2,1)} %get-tuple-element.353), kind=kOutput, calls=%fused_computation.31.clone.1 | convolution fusion | flops 59408384 | bytes 4359280 | tf_op jit(solution)/shard_map/while/body/eval_jaxpr/sij,sie->sje/dot_general | solution.py:131
  218.6 6.8 %fusion.102 = f32[2,256,128]{2,0,1:T(2,128)} fusion(f32[28,256,128]{2,1,0:T(8,128)} %fusion.101, f32[2,256,128]{2,0,1:T(2,128)} %get-tuple-element.341, pred[]{:T(512)S(6)} %compare.18, f32[4,28,2]{1,2,0:T(2,128)S(1)} %get-tuple-element.350, s32[]{:T(128)S(6)} %copy.77), kind=kOutput, calls=%fused_computation.28.clone.1 | convolution fusion | flops 22151168 | bytes 4195333 | tf_op jit(solution)/shard_map/while/body/eval_jaxpr/sp,sje->pje/dot_general | solution.py:132
  227.0 2.4 all_to_all.43
  229.4 4.3 %gather_fusion.2 = bf16[108,4096]{1,0:T(8,128)(2,1)} fusion(bf16[112,4096]{1,0:T(8,128)(2,1)} %all_to_all.43, s32[1024]{0:T(1024)} %pad_clamp_fusion), kind=kCustom, calls=%fused_computation.3 | custom fusion | bytes 1769904 | tf_op jit(solution)/shard_map/gather | solution.py:141
  233.7 2.9 reshape.326
  236.6 3.3 multiply_reduce_fusion
  240.7 1.8 dynamic_update_slice.24
  242.5 1.8 reshape.321
  245.6 18.9 %all-reduce.9.cloned.1.call-done = (f32[768,128]{1,0:T(8,128)}, f32[512,128]{1,0:T(8,128)}) async-done(((f32[768,128]{1,0:T(8,128)}, f32[512,128]{1,0:T(8,128)}), (f32[768,128]{1,0:T(8,128)}, f32[512,128]{1,0:T(8,128)})) %all-reduce.9.cloned.1.call-update) | async-done | bytes 655376 | tf_op jit(solution)/shard_map/psum | solution.py:146
  267.9 2.1 fusion.36
  274.1 22.5 %psum.63 = f32[16,128]{1,0:T(8,128)} all-reduce(f32[16,128]{1,0:T(8,128)S(1)} %convolution_add_fusion.3), channel_id=1, replica_groups=mesh['groups'=2,'shard'=8,'sub'=2] {'shard'}, use_global_device_ids=true, to_apply=%region_25.26 | all-reduce | flops 2048 | bytes 16384 | tf_op jit(solution)/shard_map/psum | solution.py:168
  296.6 47.2 %all-reduce.7.cloned.1.call-done = f32[2048,16]{0,1:T(8,128)} async-done(((f32[2048,16]{0,1:T(8,128)}), f32[2048,16]{0,1:T(8,128)}) %all-reduce.7.cloned.1.call-update) | async-done | bytes 131088 | tf_op jit(solution)/shard_map/psum | solution.py:168
  (177 shorter events, 62.4 us)
Async XLA Ops:
  7.2 12.1 %copy-start = (bf16[24,32,2048]{2,1,0:T(8,128)(2,1)S(1)}, bf16[24,32,2048]{2,1,0:T(8,128)(2,1)}, u32[]{:S(2)}) copy-start(bf16[24,32,2048]{2,1,0:T(8,128)(2,1)} %param.11) | copy-start | bytes 9437188
  7.2 1.1 copy-start.1
  10.0 56.1 %copy-start.26 = (s32[108]{0:T(128)}, s32[108]{0:T(128)S(1)}, u32[]{:S(2)}) copy-start(s32[108]{0:T(128)S(1)} %get-tuple-element.220) | copy-start | bytes 1300
  11.9 48.4 %all-to-all-start.1 = ((bf16[8,14,1]{1,2,0:T(2,128)(2,1)}), bf16[8,14,1]{1,2,0:T(2,128)(2,1)S(1)}, u32[]{:S(2)}, u32[]{:S(2)}) async-start(bf16[8,14,1]{1,2,0:T(2,128)(2,1)} %all_to_all.46), calls=%async_computation.1 | async-start | bytes 8192 | tf_op jit(solution)/shard_map/all_to_all | solution.py:91
  19.2 25.0 %all-reduce.11.cloned.1.call-start = ((), (), s32[]{:S(2)}) async-start(), calls=%async_computation.7 | async-start | bytes 1310720 | tf_op jit(solution)/shard_map/psum | solution.py:66
  19.3 2.9 copy-start.4
  19.3 2.9 copy-start.12
  22.2 1.5 copy-start.13
  25.9 18.3 %copy-start.14 = (bf16[16,128]{1,0:T(8,128)(2,1)S(1)}, bf16[16,128]{1,0:T(8,128)(2,1)}, u32[]{:S(2)}) copy-start(bf16[16,128]{1,0:T(8,128)(2,1)} %param.15) | copy-start | bytes 12292
  45.6 0.6 copy-start.19
  46.2 0.6 copy-start.16
  60.3 32.1 %all-to-all-start = ((bf16[8,14,4096]{2,1,0:T(8,128)(2,1)}), bf16[8,14,4096]{2,1,0:T(8,128)(2,1)}, u32[]{:S(2)}, u32[]{:S(2)}) async-start(bf16[8,14,4096]{2,1,0:T(8,128)(2,1)} %all_to_all.34), calls=%async_computation | async-start | bytes 2097152 | tf_op jit(solution)/shard_map/all_to_all | solution.py:90
  68.1 0.7 copy-start.6
  68.2 26.9 %copy-start.23 = (f32[512]{0:T(512)}, f32[512]{0:T(512)S(1)}, u32[]{:S(2)}) copy-start(f32[512]{0:T(512)S(1)} %get-tuple-element.217) | copy-start | bytes 6148
  68.2 26.9 %copy-start.21 = (f32[512]{0:T(512)}, f32[512]{0:T(512)S(1)}, u32[]{:S(2)}) copy-start(f32[512]{0:T(512)S(1)} %add_rsqrt_fusion.1) | copy-start | bytes 6148
  96.8 1.4 copy-start.2
  101.1 0.6 copy-start.9
  103.1 3.8 %copy-start.3 = (f32[28,32,256]{2,1,0:T(8,128)S(1)}, f32[28,32,256]{2,1,0:T(8,128)}, u32[]{:S(2)}) copy-start(f32[28,32,256]{2,1,0:T(8,128)} %get-tuple-element.298) | copy-start | bytes 2752516 | tf_op jit(solution)/shard_map/while
  103.1 3.8 %copy-start.10 = (f32[28,32]{1,0:T(8,128)S(1)}, f32[28,32]{1,0:T(8,128)}, u32[]{:S(2)}) copy-start(f32[28,32]{1,0:T(8,128)} %copy-done.9) | copy-start | bytes 10756 | tf_op jit(solution)/shard_map/while
  109.6 1.4 copy-start.2
  114.0 0.6 copy-start.9
  116.0 3.8 %copy-start.3 = (f32[28,32,256]{2,1,0:T(8,128)S(1)}, f32[28,32,256]{2,1,0:T(8,128)}, u32[]{:S(2)}) copy-start(f32[28,32,256]{2,1,0:T(8,128)} %get-tuple-element.298) | copy-start | bytes 2752516 | tf_op jit(solution)/shard_map/while
  116.0 3.8 %copy-start.10 = (f32[28,32]{1,0:T(8,128)S(1)}, f32[28,32]{1,0:T(8,128)}, u32[]{:S(2)}) copy-start(f32[28,32]{1,0:T(8,128)} %copy-done.9) | copy-start | bytes 10756 | tf_op jit(solution)/shard_map/while
  122.5 1.4 copy-start.2
  126.8 0.6 copy-start.9
  128.9 3.8 %copy-start.3 = (f32[28,32,256]{2,1,0:T(8,128)S(1)}, f32[28,32,256]{2,1,0:T(8,128)}, u32[]{:S(2)}) copy-start(f32[28,32,256]{2,1,0:T(8,128)} %get-tuple-element.298) | copy-start | bytes 2752516 | tf_op jit(solution)/shard_map/while
  128.9 3.8 %copy-start.10 = (f32[28,32]{1,0:T(8,128)S(1)}, f32[28,32]{1,0:T(8,128)}, u32[]{:S(2)}) copy-start(f32[28,32]{1,0:T(8,128)} %copy-done.9) | copy-start | bytes 10756 | tf_op jit(solution)/shard_map/while
  135.3 1.4 copy-start.2
  139.7 0.6 copy-start.9
  141.7 3.8 %copy-start.3 = (f32[28,32,256]{2,1,0:T(8,128)S(1)}, f32[28,32,256]{2,1,0:T(8,128)}, u32[]{:S(2)}) copy-start(f32[28,32,256]{2,1,0:T(8,128)} %get-tuple-element.298) | copy-start | bytes 2752516 | tf_op jit(solution)/shard_map/while
  141.7 3.8 %copy-start.10 = (f32[28,32]{1,0:T(8,128)S(1)}, f32[28,32]{1,0:T(8,128)}, u32[]{:S(2)}) copy-start(f32[28,32]{1,0:T(8,128)} %copy-done.9) | copy-start | bytes 10756 | tf_op jit(solution)/shard_map/while
  147.8 10.0 %all-to-all-start.2 = ((f32[8,14,1]{1,2,0:T(1,128)}), f32[8,14,1]{1,2,0:T(1,128)S(1)}, u32[]{:S(2)}, u32[]{:S(2)}) async-start(f32[8,14,1]{1,2,0:T(1,128)} %bitcast.13), calls=%async_computation.2 | async-start | bytes 8192 | tf_op jit(solution)/shard_map/all_to_all | solution.py:118
  160.5 0.6 copy-start.27
  161.3 0.5 copy-start.25
  166.2 10.2 %all-to-all-start.4 = ((f32[8,14,1]{1,2,0:T(1,128)}), f32[8,14,1]{1,2,0:T(1,128)S(1)}, u32[]{:S(2)}, u32[]{:S(2)}) async-start(f32[8,14,1]{1,2,0:T(1,128)} %bitcast.111), calls=%async_computation.4 | async-start | bytes 8192 | tf_op jit(solution)/shard_map/all_to_all | solution.py:125
  176.4 50.6 %all-to-all-start.3 = ((bf16[8,14,4096]{2,1,0:T(8,128)(2,1)}), bf16[8,14,4096]{2,1,0:T(8,128)(2,1)}, u32[]{:S(2)}, u32[]{:S(2)}) async-start(bf16[8,14,4096]{2,1,0:T(8,128)(2,1)} %all_to_all.41), calls=%async_computation.3 | async-start | bytes 2097152 | tf_op jit(solution)/shard_map/all_to_all | solution.py:126
  180.6 83.9 %all-reduce.9.cloned.1.call-start = ((), (), s32[]{:S(2)}) async-start(), calls=%async_computation.6 | async-start | bytes 1310720 | tf_op jit(solution)/shard_map/psum | solution.py:146
  239.9 26.5 %copy-start.15 = (bf16[16,128]{1,0:T(8,128)(2,1)S(1)}, bf16[16,128]{1,0:T(8,128)(2,1)}, u32[]{:S(2)}) copy-start(bf16[16,128]{1,0:T(8,128)(2,1)} %param.15) | copy-start | bytes 12292
  239.9 26.5 %copy-start.17 = (f32[768]{0:T(1024)S(1)}, f32[768]{0:T(1024)}, u32[]{:S(2)}) copy-start(f32[768]{0:T(1024)} %copy-done.16) | copy-start | bytes 9220
  244.4 99.4 %all-reduce.7.cloned.1.call-start = ((), (), s32[]{:S(2)}) async-start(), calls=%async_computation.5 | async-start | bytes 262144 | tf_op jit(solution)/shard_map/psum | solution.py:168
  267.9 2.7 copy-start.7
  267.9 2.7 copy-start.11
  270.1 0.7 copy-start.24
  270.1 0.7 copy-start.22
  270.1 1.6 copy-start.5
  270.6 2.1 copy-start.8
  270.6 2.2 copy-start.18
  270.6 2.2 copy-start.20
Sparse Core Ops, SparseCore 0:
  23.8 20.3 all-reduce.10
  244.5 20.0 all-reduce.8
  272.8 70.8 all-reduce.6
where the time goes:
time: 354 us; the launch traced here: 352 us
  waiting for transfers between devices  109 us (31%)
  matrix products  93.2 us (26%)
  local copies, waits for them, and re-layouts  64.4 us (18%)
  blocking collectives  26.7 us (8%)
  starting transfers between devices  25.1 us (7%)
  other arithmetic  19 us (5%)
  between operations  14.1 us (4%)
    psum x1, waiting for transfers between devices, per_device(): grad_down, grad_up = lax.psum((grad_down, grad_up), 'shard')  47.2 us
    dot_general x4, matrix products, backward(): jnp.einsum('sp,sje->pje', sel, contrib, precision=lax.Precision.HIGHEST)  27.2 us
    all_to_all x1, waiting for transfers between devices, per_device(): lax.all_to_all(send_vec, 'shard', split_axis=0, concat_axis=0, tiled=True)  22.6 us
    psum x1, blocking collectives, per_device(): grad_down, grad_up = lax.psum((grad_down, grad_up), 'shard')  22.5 us
    psum x1, waiting for transfers between devices, per_device(): grad_vq, grad_vp = lax.psum((padded, grad_bank), 'sub')  18.9 us
    dot_general x4, matrix products, backward(): jnp.einsum('sij,sie->sje', gradw, inc, preferred_element_type=jnp.float32)  15.2 us
    dot_general x4, matrix products, forward(): jnp.einsum('sij,sje->sie', weights, chosen, preferred_element_type=jnp.fl...  15.1 us
    psum x1, waiting for transfers between devices, per_device(): lax.psum((frozen_query, adapter_query, frozen_passage, adapter_passage),...  13.1 us
  transfers between devices with their start and end apart: 8, of which 6 were waited for; matrix products, arithmetic and copies ran while one was open for 21% of the time, Pallas kernels for 0%

commit v1 on v0

v1 whole, which is shorter than its diff:
```python
import functools
import math

import jax
import jax.numpy as jnp
from jax import lax
from jax.experimental import pallas as pl
from jax.experimental.pallas import tpu as pltpu
from jax.sharding import PartitionSpec as P

pool_temp = 0.05
loss_temp = 0.05
norm_eps = 1e-06
bf16 = jnp.bfloat16
f32 = jnp.float32
LANES = 128
EXP_SCALE = math.log2(math.e) / pool_temp
VMEM = pl.BlockSpec(memory_space=pltpu.VMEM)
SMEM = pl.BlockSpec(memory_space=pltpu.SMEM)


def dot(a, b, contract, precision=None):
    return lax.dot_general(
        a, b, ((contract[0], contract[1]), ((), ())), precision=precision, preferred_element_type=f32
    )


NN = ((1,), (0,))
NT = ((1,), (1,))
TN = ((0,), (0,))


def split_dot(exact, wide, contract):
    high = wide.astype(bf16)
    low = (wide - high.astype(f32)).astype(bf16)
    return dot(exact, high, contract) + dot(exact, low, contract)


def project_kernel(core_ref, x_ref, proj_ref, down_ref, send_ref, keep_ref):
    x = x_ref[...]
    base = dot(x, proj_ref[...], NN)
    low = dot(x, down_ref[...], NN)

    def put(ref):
        ref[:, :LANES] = base
        ref[:, LANES:] = low

    pl.when(pl.program_id(0) == 0)(lambda: put(send_ref))
    pl.when(pl.program_id(0) == 1)(lambda: put(keep_ref))


def project(core, rows, projection, down):
    half, width = rows.shape[0] // 2, rows.shape[1]
    shape = jax.ShapeDtypeStruct((half, 2 * LANES), f32)
    return pl.pallas_call(
        project_kernel,
        grid_spec=pltpu.PrefetchScalarGridSpec(
            num_scalar_prefetch=1,
            grid=(2,),
            in_specs=[
                pl.BlockSpec((half, width), lambda j, core: (lax.rem(core[0] + 1 + j, 2), 0)),
                pl.BlockSpec((width, LANES), lambda j, core: (0, 0)),
                pl.BlockSpec((width, LANES), lambda j, core: (0, 0)),
            ],
            out_specs=[
                pl.BlockSpec((half, 2 * LANES), lambda j, core: (0, 0)),
                pl.BlockSpec((half, 2 * LANES), lambda j, core: (0, 0)),
            ],
        ),
        out_shape=(shape, shape),
        name="project",
    )(core, rows, projection, down)


def finish(keep_ref, recv_ref, up):
    rank = up.shape[0]
    low_bf = (keep_ref[:, LANES : LANES + rank] + recv_ref[:, LANES : LANES + rank]).astype(bf16)
    full = keep_ref[:, :LANES] + recv_ref[:, :LANES] + dot(low_bf, up, NN)
    r = lax.rsqrt(jnp.sum(full * full, axis=1, keepdims=True) + norm_eps)
    return low_bf, full * r, r


def pad_lanes(x):
    return jnp.concatenate([x, jnp.zeros((x.shape[0], LANES - x.shape[1]), x.dtype)], axis=1)


def pack_kernel(keep_ref, recv_ref, up_ref, pack_ref, r_ref):
    up = up_ref[...]
    rank, tokens = up.shape[0], keep_ref.shape[0]
    low_bf, vn, r = finish(keep_ref, recv_ref, up)
    pack_ref[:tokens, :] = vn.astype(bf16)
    scaled = jnp.transpose(pad_lanes(low_bf.astype(f32) * r))
    for t in range(tokens // LANES):
        at = tokens + t * rank
        pack_ref[at : at + rank, :] = scaled[:rank, t * LANES : (t + 1) * LANES].astype(bf16)
    r_ref[...] = jnp.transpose(jnp.broadcast_to(r, (tokens, LANES)))[:8, :]


def pack_passage(keep, recv, up):
    tokens, rank = keep.shape[0], up.shape[0]
    return pl.pallas_call(
        pack_kernel,
        in_specs=[VMEM] * 3,
        out_specs=[VMEM] * 2,
        out_shape=(
            jax.ShapeDtypeStruct((tokens + tokens // LANES * rank, LANES), bf16),
            jax.ShapeDtypeStruct((8, tokens), f32),
        ),
        name="pack_passage",
    )(keep, recv, up)


def score_kernel(queries, store, n_packs, *refs):
    packs = refs[:n_packs]
    (owner_ref, keep_ref, recv_ref, up_ref, mult_ref, first_ref) = refs[n_packs : n_packs + 6]
    loss_ref, dlow_q_ref, part_ref, gup_ref = refs[n_packs + 6 : n_packs + 10]
    expo_ref, total_ref, scale_ref, dvq_ref = refs[n_packs + 10 :]
    up = up_ref[...]
    rank = up.shape[0]
    ntok = keep_ref.shape[0]
    qlen = ntok // queries
    plen = part_ref.shape[-1]
    low_bf, vn, r = finish(keep_ref, recv_ref, up)
    vq = vn.astype(bf16)
    vqt = jnp.transpose(vn).astype(bf16)

    def expo_of(pack, p):
        sims = dot(pack[p, :plen, :], vqt, NN)
        return jnp.exp2(sims * EXP_SCALE)

    def over(body):
        at = 0
        for pack in packs:
            n = pack.shape[0]
            if n <= 8:
                for p in range(n):
                    body(pack, p, at + p)
            else:
                lax.fori_loop(0, n, lambda p, c, pack=pack, at=at: (body(pack, p, at + p), c)[1], 0)
            at += n

    def forward(pack, p, pos):
        expo = expo_of(pack, p)
        total_ref[pl.ds(pos, 1), :] = jnp.sum(expo, axis=0, keepdims=True)
        if store:
            expo_ref[pos] = expo.astype(bf16)

    over(forward)

    total = total_ref[...]
    token_query = lax.broadcasted_iota(jnp.int32, (ntok, LANES), 0) // qlen
    same = (token_query == lax.broadcasted_iota(jnp.int32, (ntok, LANES), 1)).astype(f32)
    logits = dot(jnp.log(total), same, NN, lax.Precision.HIGHEST) * (1.0 / qlen)
    mult, first = mult_ref[...], first_ref[...]
    weighted = mult * jnp.exp(logits)
    summed = jnp.sum(weighted, axis=0, keepdims=True)
    live = lax.broadcasted_iota(jnp.int32, summed.shape, 1) < queries
    summed = jnp.where(live, summed, 1.0)
    positive = jnp.sum(first * logits, axis=0, keepdims=True)
    loss_ref[...] = jnp.broadcast_to(jnp.log(summed) - positive, loss_ref.shape)
    dscore = (weighted / summed - first) * (1.0 / loss_temp)
    scale_ref[...] = dot(dscore, same, NT, lax.Precision.HIGHEST) / (total * qlen)

    dvq_ref[...] = jnp.zeros_like(dvq_ref)
    gup_ref[...] = jnp.zeros_like(gup_ref)

    def backward(pack, p, pos):
        vp = pack[p, :plen, :]
        expo = expo_ref[pos].astype(f32) if store else expo_of(pack, p)
        gradw = (expo * scale_ref[pl.ds(pos, 1), :]).astype(bf16)
        dv = dot(gradw, vq, NN)
        dvq_ref[...] += dot(vp, gradw, TN)
        vpf = vp.astype(f32)
        dv = dv - vpf * jnp.sum(vpf * dv, axis=1, keepdims=True)
        part_ref[owner_ref[0, pos], owner_ref[1, pos]] = split_dot(up, dv, NT).astype(bf16)
        for t in range(plen // LANES):
            scaled = pack[p, plen + t * rank : plen + (t + 1) * rank, :]
            gup_ref[...] += split_dot(scaled, dv[t * LANES : (t + 1) * LANES, :], NN)

    over(backward)

    dvq = jnp.transpose(dvq_ref[...])
    dfull = r * (dvq - vn * jnp.sum(vn * dvq, axis=1, keepdims=True))
    dlow_q_ref[...] = split_dot(up, dfull, NT).astype(bf16)
    low_t = jnp.transpose(pad_lanes(low_bf.astype(f32)))[:rank, :].astype(bf16)
    gup_ref[...] += split_dot(low_t, dfull, NN)


def score(packs, owners, keep, recv, up, mult, first, queries, nshard, plen):
    npos, rank, ntok = mult.shape[0], up.shape[0], keep.shape[0]
    store = npos * plen * ntok * 2 <= 12 * 2**20
    return pl.pallas_call(
        functools.partial(score_kernel, queries, store, len(packs)),
        in_specs=[VMEM] * len(packs) + [SMEM] + [VMEM] * 5,
        out_specs=[VMEM] * 4,
        out_shape=(
            jax.ShapeDtypeStruct((8, LANES), f32),
            jax.ShapeDtypeStruct((rank, ntok), bf16),
            jax.ShapeDtypeStruct((nshard, 2, rank, plen), bf16),
            jax.ShapeDtypeStruct((rank, LANES), f32),
        ),
        scratch_shapes=[
            pltpu.VMEM((npos if store else 1, plen, ntok), bf16),
            pltpu.VMEM((npos, ntok), f32),
            pltpu.VMEM((npos, ntok), f32),
            pltpu.VMEM((LANES, ntok), f32),
        ],
        compiler_params=pltpu.CompilerParams(vmem_limit_bytes=48 * 2**20),
        name="score",
    )(*packs, owners, keep, recv, up, mult, first)


def grad_down_kernel(core_ref, x_ref, dlow_ref, out_ref):
    @pl.when(pl.program_id(0) == 0)
    def _():
        out_ref[...] = jnp.zeros_like(out_ref)

    out_ref[...] += dot(dlow_ref[...], x_ref[...], NN)


def grad_down_of(core, rows, mine, other):
    half, width = rows.shape[0] // 2, rows.shape[1]
    rank = mine.shape[0]
    both = jnp.concatenate([mine, other], axis=1)
    return pl.pallas_call(
        grad_down_kernel,
        grid_spec=pltpu.PrefetchScalarGridSpec(
            num_scalar_prefetch=1,
            grid=(2,),
            in_specs=[
                pl.BlockSpec((half, width), lambda j, core: (lax.rem(core[0] + j, 2), 0)),
                pl.BlockSpec((rank, half), lambda j, core: (0, j)),
            ],
            out_specs=pl.BlockSpec((rank, width), lambda j, core: (0, 0)),
        ),
        out_shape=jax.ShapeDtypeStruct((rank, width), f32),
        name="grad_down",
    )(core, rows, both)


def swap(x):
    return lax.ppermute(x, "sub", [(0, 1), (1, 0)])


def across(x, nshard, step):
    return lax.ppermute(x, "shard", [(i, i ^ step) for i in range(nshard)])


def gather_packs(pack, nshard, shard, core):
    if nshard == 8:
        near = jnp.stack([pack] + [across(pack, nshard, k) for k in (2, 4, 6)])
        far = across(near, nshard, 1)
        packs = [near, far, swap(near), swap(far)]
        shards = jnp.bitwise_xor(shard, jnp.array([0, 2, 4, 6, 1, 3, 5, 7], jnp.int32))
    else:
        mine = lax.all_gather(pack, "shard")
        packs = [mine, swap(mine)]
        shards = jnp.arange(nshard, dtype=jnp.int32)
    cores = jnp.repeat(jnp.stack([core, 1 - core]), nshard)
    return packs, jnp.stack([jnp.tile(shards, 2), cores]).astype(jnp.int32)


def sum_over_shards(x, nshard):
    x = x.astype(bf16)
    if nshard != 8:
        return lax.psum(x.astype(f32), "shard")
    x = (x.astype(f32) + across(x, nshard, 1).astype(f32)).astype(bf16)
    a, b, c = (across(x, nshard, k).astype(f32) for k in (2, 4, 6))
    return (x.astype(f32) + a) + (b + c)


def per_device(
    query_hidden_states,
    passage_hidden_states,
    projection_matrix,
    adapter_down_weight,
    adapter_up_weight,
    passage_pair_index,
    passage_row_table,
):
    nshard = lax.axis_size("shard")
    core = lax.axis_index("sub").astype(jnp.int32)
    shard = lax.axis_index("shard").astype(jnp.int32)
    qdev, qlen, width = query_hidden_states.shape
    pdev, plen, _ = passage_hidden_states.shape
    rank = adapter_up_weight.shape[0]
    half = qdev // 2
    core1 = core.reshape(1)
    query_rows = query_hidden_states.reshape(qdev * qlen, width)
    passage_rows = passage_hidden_states.reshape(pdev * plen, width)
    down = jnp.pad(adapter_down_weight, ((0, 0), (0, LANES - rank)))

    send_p, keep_p = project(core1, passage_rows, projection_matrix, down)
    recv_p = swap(send_p)
    send_q, keep_q = project(core1, query_rows, projection_matrix, down)
    recv_q = swap(send_q)
    pack, r_p = pack_passage(keep_p, recv_p, adapter_up_weight)
    packs, owners = gather_packs(pack, nshard, shard, core)

    ids = lax.dynamic_slice_in_dim(passage_pair_index, core * half, half, 0)
    rows = passage_row_table[ids]
    places = owners[0] * pdev + owners[1]
    hits = (places[:, None, None] == rows[None]).astype(f32)
    lanes = ((0, 0), (0, LANES - half))
    mult = jnp.pad(jnp.sum(hits, axis=2), lanes)
    first = jnp.pad(hits[:, :, 0], lanes)

    loss, dlow_q, part, gup = score(
        packs, owners, keep_q, recv_q, adapter_up_weight, mult, first, half, nshard, plen
    )
    query_loss = loss[0, :half]
    parts = lax.all_to_all(part, "shard", split_axis=0, concat_axis=0, tiled=True)
    grad_q = grad_down_of(core1, query_rows, dlow_q, swap(dlow_q))
    gup = gup + swap(gup)
    r_both = jnp.where(core == 0, jnp.stack([r_p, swap(r_p)]), jnp.stack([swap(r_p), r_p]))[:, :1]
    total = jnp.sum(parts.astype(f32), axis=0)
    total = total + swap(total)
    dlow_p = (total * r_both).astype(bf16)
    mine = lax.dynamic_index_in_dim(dlow_p, core, 0, False)
    other = lax.dynamic_index_in_dim(dlow_p, 1 - core, 0, False)
    grad_p = grad_down_of(core1, passage_rows, mine, other)
    summed = sum_over_shards(jnp.concatenate([grad_q + grad_p, gup], axis=1), nshard)
    return (query_loss, jnp.transpose(summed[:, :width]), summed[:, width:])


def solution(mesh):
    placed = (
        P(("groups", "shard"), None, "sub"),
        P(("groups", "shard"), None, "sub"),
        P("sub", None),
        P("sub", None),
        P(),
        P(("groups", "shard"), None),
        P("groups"),
    )
    return jax.shard_map(
        per_device,
        mesh=mesh,
        in_specs=placed,
        out_specs=(P(("groups", "shard", "sub")), P(("groups", "sub"), None), P("groups", None)),
        check_vma=False,
    )
```

time: 354 us -> 78.5 us (0.22)
  matrix products: 93.2 us -> 0 us
  waiting for transfers between devices: 109 us -> 26.3 us
  local copies, waits for them, and re-layouts: 64.4 us -> 6.46 us
  blocking collectives: 26.7 us -> 0 us
  Pallas kernels: 0 us -> 23.6 us
  other arithmetic: 19 us -> 2.74 us
  between operations: 14.1 us -> 0.86 us
  starting transfers between devices: 25.1 us -> 18.1 us
    dot_general x32 -> x0, matrix products: 93.2 us -> none  [the longest x4 27.2 us: backward(): jnp.einsum('sp,sje->pje', sel, contrib, precision=lax.Precision.HIGHEST)]
    psum x3 -> x0, waiting for transfers between devices: 79.3 us -> none  [the longest x1 47.2 us: per_device(): grad_down, grad_up = lax.psum((grad_down, grad_up), 'shard')]
    psum x2 -> x0, blocking collectives: 26.7 us -> none  [the longest x1 22.5 us: per_device(): grad_down, grad_up = lax.psum((grad_down, grad_up), 'shard')]
    all_to_all x5 -> x1, waiting for transfers between devices: 29.9 us -> 6.17 us  [per_device(): lax.all_to_all(part, 'shard', split_axis=0, concat_axis=0, tiled=True)]
    pallas_call x0 -> x6, Pallas kernels: none -> 23.6 us  [the longest x2 8.38 us: project(): pl.pallas_call(project_kernel, grid_spec=pltpu.PrefetchScalarGridSpec(num...]
    all_to_all x5 -> x1, starting transfers between devices: 24.7 us -> 4.43 us  [per_device(): lax.all_to_all(part, 'shard', split_axis=0, concat_axis=0, tiled=True)]
    ppermute x0 -> x16, waiting for transfers between devices: none -> 20.2 us  [the longest x8 18.6 us: across(): return lax.ppermute(x, 'shard', [(i, i ^ step) for i in range(nshard)])]
    ppermute x0 -> x16, starting transfers between devices: none -> 13.7 us  [the longest x8 12.1 us: across(): return lax.ppermute(x, 'shard', [(i, i ^ step) for i in range(nshard)])]
  transfers between devices with their start and end apart: 8 -> 17, of which waited for: 6 -> 9; matrix products, arithmetic and copies ran while one was open for 21% -> 4% of each run, Pallas kernels for 0% -> 22%
where the time goes in v1:
time: 78.5 us; the launch traced here: 78.1 us
  waiting for transfers between devices  26.3 us (34%)
  Pallas kernels  23.6 us (30%)
  starting transfers between devices  18.1 us (23%)
  local copies, waits for them, and re-layouts  6.46 us (8%)
  other arithmetic  2.74 us (3%)
  between operations  0.86 us (1%)
    ppermute x8, waiting for transfers between devices, across(): return lax.ppermute(x, 'shard', [(i, i ^ step) for i in range(nshard)])  18.6 us
    ppermute x8, starting transfers between devices, across(): return lax.ppermute(x, 'shard', [(i, i ^ step) for i in range(nshard)])  12.1 us
    pallas_call x2, Pallas kernels, project(): pl.pallas_call(project_kernel, grid_spec=pltpu.PrefetchScalarGridSpec(num...  8.38 us
    pallas_call x1, Pallas kernels, score(): pl.pallas_call(functools.partial(score_kernel, queries, store, len(packs)...  7.92 us
    all_to_all x1, waiting for transfers between devices, per_device(): lax.all_to_all(part, 'shard', split_axis=0, concat_axis=0, tiled=True)  6.17 us
    pallas_call x2, Pallas kernels, grad_down_of(): pl.pallas_call(grad_down_kernel, grid_spec=pltpu.PrefetchScalarGridSpec(n...  5.34 us
    all_to_all x1, starting transfers between devices, per_device(): lax.all_to_all(part, 'shard', split_axis=0, concat_axis=0, tiled=True)  4.43 us
    pallas_call x1, Pallas kernels, pack_passage(): pl.pallas_call(pack_kernel, in_specs=[VMEM] * 3, out_specs=[VMEM] * 2, ou...  1.96 us
  transfers between devices with their start and end apart: 17, of which 9 were waited for; matrix products, arithmetic and copies ran while one was open for 4% of the time, Pallas kernels for 22%

profile of v1, /device:TPU:0, one launch (start us, length us, event | category | flops | bytes accessed | tf_op | source)
XLA Modules:
  0.0 78.1 jit_solution(14065161890070698417)
XLA Ops:
  0.7 1.1 %copy.14 = bf16[2048,16]{1,0:T(8,128)(2,1)S(1)} copy(bf16[2048,16]{0,1:T(8,128)(2,1)} %param.11) | data formatting | bytes 131072 | tf_op args[3]
  1.8 0.9 %pad.11.down_ref = bf16[2048,128]{1,0:T(8,128)(2,1)} pad(bf16[2048,16]{1,0:T(8,128)(2,1)S(1)} %copy.14, bf16[]{:T(256)} %constant.13.clone.1), padding=0_0x0_112 | pad | bytes 589826 | tf_op jit(solution)/shard_map/jit(_pad)/pad | solution.py:291
  2.7 3.8 %project.2 = (f32[256,256]{1,0:T(8,128)}, f32[256,256]{1,0:T(8,128)}) custom-call(s32[1]{0:T(128)} %bitcast.core_ref, bf16[512,2048]{1,0:T(8,128)(2,1)} %bitcast.25, bf16[2048,128]{1,0:T(8,128)(2,1)} %proj_ref.3, bf16[2048,128]{1,0:T(8,128)(2,1)} %pad.11.down_ref), custom_call_target="tpu_custom_call" | custom-call | tf_op jit(solution)/shard_map/project/pallas_call | solution.py:55
  6.5 0.5 collective-permute-start
  6.9 4.6 %project.3 = (f32[384,256]{1,0:T(8,128)}, f32[384,256]{1,0:T(8,128)}) custom-call(s32[1]{0:T(128)} %bitcast.core_ref, bf16[768,2048]{1,0:T(8,128)(2,1)} %bitcast.23, bf16[2048,128]{1,0:T(8,128)(2,1)} %proj_ref.3, bf16[2048,128]{1,0:T(8,128)(2,1)} %pad.11.down_ref), custom_call_target="tpu_custom_call" | custom-call | tf_op jit(solution)/shard_map/project/pallas_call | solution.py:55
  11.6 0.1 pad_add_fusion.1
  11.7 0.1 broadcast_add_fusion
  11.7 0.1 add.55
  11.8 0.1 compare_select_fusion
  11.9 0.1 copy.15
  12.0 0.1 reshape.35
  12.1 0.7 copy-done.3
  12.8 2.0 %pack_passage.1 = (bf16[288,128]{1,0:T(8,128)(2,1)}, f32[8,256]{1,0:T(8,128)}) custom-call(f32[256,256]{1,0:T(8,128)} %get-tuple-element.13.keep_ref, f32[256,256]{1,0:T(8,128)} %copy-done.3, bf16[16,128]{1,0:T(8,128)(2,1)} %refs_7_.1), custom_call_target="tpu_custom_call" | custom-call | tf_op jit(solution)/shard_map/pack_passage/pallas_call | solution.py:101
  14.8 5.1 %collective-permute-start.3 = (bf16[288,128]{1,0:T(8,128)(2,1)}, bf16[288,128]{1,0:T(8,128)(2,1)S(1)}, u32[]{:S(2)}, u32[]{:S(2)}) collective-permute-start(bf16[288,128]{1,0:T(8,128)(2,1)} %get-tuple-element.15), channel_id=1, source_target_pairs={{0,12},{2,14},{4,8},{6,10},{8,4},{10,6},{12,0},{14,2},{1,13},{3,15... | collective-permute-start | bytes 221192 | tf_op jit(solution)/shard_map/ppermute | solution.py:246
  19.8 0.6 collective-permute-start.1
  20.4 1.2 %gather_fusion = s32[108]{0:T(128)S(1)} fusion(s32[16]{0:T(128)S(1)} %copy-done, s32[1024]{0:T(1024)S(1)} %pad_clamp_fusion), kind=kCustom, calls=%fused_computation | custom fusion | bytes 1296 | tf_op jit(solution)/shard_map/gather | solution.py:301
  21.7 0.1 reshape.34
  21.7 0.1 copy.16
  21.8 1.0 %collective-permute-done.3 = bf16[288,128]{1,0:T(8,128)(2,1)S(1)} collective-permute-done((bf16[288,128]{1,0:T(8,128)(2,1)}, bf16[288,128]{1,0:T(8,128)(2,1)S(1)}, u32[]{:S(2)}, u32[]{:S(2)}) %collective-permute-start.3) | collective-permute-done | bytes 73760 | tf_op jit(solution)/shard_map/ppermute | solution.py:246
  22.8 3.6 %collective-permute-done.2 = bf16[288,128]{1,0:T(8,128)(2,1)S(1)} collective-permute-done((bf16[288,128]{1,0:T(8,128)(2,1)}, bf16[288,128]{1,0:T(8,128)(2,1)S(1)}, u32[]{:S(2)}, u32[]{:S(2)}) %collective-permute-start.2) | collective-permute-done | bytes 73760 | tf_op jit(solution)/shard_map/ppermute | solution.py:246
  26.5 1.6 %collective-permute-start.4 = (bf16[4,288,128]{2,1,0:T(8,128)(2,1)S(1)}, bf16[4,288,128]{2,1,0:T(8,128)(2,1)S(1)}, u32[]{:S(2)}, u32[]{:S(2)}) collective-permute-start(bf16[4,288,128]{2,1,0:T(8,128)(2,1)S(1)} %pad_maximum_fusion.refs_0_), channel_id=1, source_target_pairs={{0,2},{2,0},{4,6},{6,4},{8,10},{10,8},{12,14},{14,12},{1,3},{3,1},... | collective-permute-start | bytes 884744 | tf_op jit(solution)/shard_map/ppermute | solution.py:246
  28.0 0.1 compare_convert_fusion
  28.1 0.1 fusion
  28.2 0.1 stack_reshape.3
  28.3 0.1 stack_tile.3
  28.4 6.4 %collective-permute-done.4.refs_1_ = bf16[4,288,128]{2,1,0:T(8,128)(2,1)S(1)} collective-permute-done((bf16[4,288,128]{2,1,0:T(8,128)(2,1)S(1)}, bf16[4,288,128]{2,1,0:T(8,128)(2,1)S(1)}, u32[]{:S(2)}, u32[]{:S(2)}) %collective-permute-start.4) | collective-permute-done | bytes 294944 | tf_op jit(solution)/shard_map/ppermute | solution.py:246
  34.9 0.5 collective-permute-start.10
  35.4 1.0 %collective-permute-done.6.refs_3_ = bf16[4,288,128]{2,1,0:T(8,128)(2,1)S(1)} collective-permute-done((bf16[4,288,128]{2,1,0:T(8,128)(2,1)S(1)}, bf16[4,288,128]{2,1,0:T(8,128)(2,1)S(1)}, u32[]{:S(2)}, u32[]{:S(2)}) %collective-permute-start.6) | collective-permute-done | bytes 294944 | tf_op jit(solution)/shard_map/ppermute | solution.py:242
  36.4 7.9 %score.1 = (f32[8,128]{1,0:T(8,128)S(1)}, bf16[16,384]{1,0:T(8,128)(2,1)S(1)}, bf16[8,2,16,256]{3,2,1,0:T(8,128)(2,1)}, f32[16,128]{1,0:T(8,128)S(1)}) custom-call(bf16[4,288,128]{2,1,0:T(8,128)(2,1)S(1)} %pad_maximum_fusion.refs_0_, bf16[4,288,128]{2,1,0:T(8,128)(2,1)S(1)} %collective-permute-done.4.refs_1_, ...), custom_call_target="tpu_custom_call" | custom-call | tf_op jit(solution)/shard_map/score/pallas_call | solution.py:192
  44.4 4.4 %all-to-all-start = ((bf16[8,2,16,256]{3,2,1,0:T(8,128)(2,1)}), bf16[8,2,16,256]{3,2,1,0:T(8,128)(2,1)S(1)}, u32[]{:S(2)}, u32[]{:S(2)}) async-start(bf16[8,2,16,256]{3,2,1,0:T(8,128)(2,1)} %get-tuple-element.20), calls=%async_computation | async-start | bytes 262144 | tf_op jit(solution)/shard_map/all_to_all | solution.py:312
  48.8 0.5 collective-permute-start.8
  49.4 0.6 collective-permute-done.11
  50.0 6.2 %all-to-all-done = bf16[8,2,16,256]{3,2,1,0:T(8,128)(2,1)S(1)} async-done(((bf16[8,2,16,256]{3,2,1,0:T(8,128)(2,1)}), bf16[8,2,16,256]{3,2,1,0:T(8,128)(2,1)S(1)}, u32[]{:S(2)}, u32[]{:S(2)}) %all-to-all-start) | async-done | bytes 131104 | tf_op jit(solution)/shard_map/all_to_all | solution.py:312
  56.3 0.6 pad_maximum_fusion.2.dlow_ref
  56.9 2.9 %grad_down.2 = f32[16,2048]{1,0:T(8,128)} custom-call(s32[1]{0:T(128)} %bitcast.core_ref, bf16[768,2048]{1,0:T(8,128)(2,1)} %bitcast.24, bf16[16,768]{1,0:T(8,128)(2,1)} %pad_maximum_fusion.2.dlow_ref), custom_call_target="tpu_custom_call" | custom-call | tf_op jit(solution)/shard_map/grad_down/pallas_call | solution.py:225
  59.8 0.6 pad_maximum_fusion.3.dlow_ref
  60.4 2.5 %grad_down.3 = f32[16,2048]{1,0:T(8,128)} custom-call(s32[1]{0:T(128)} %bitcast.core_ref, bf16[512,2048]{1,0:T(8,128)(2,1)} %bitcast.26, bf16[16,512]{1,0:T(8,128)(2,1)} %pad_maximum_fusion.3.dlow_ref), custom_call_target="tpu_custom_call" | custom-call | tf_op jit(solution)/shard_map/grad_down/pallas_call | solution.py:225
  62.9 1.0 %add_convert_fusion.1 = bf16[16,2048]{1,0:T(8,128)(2,1)S(1)} fusion(f32[16,2048]{1,0:T(8,128)} %grad_down.2, f32[16,2048]{1,0:T(8,128)} %grad_down.3), kind=kLoop, calls=%fused_computation.6 | loop fusion | flops 65536 | bytes 327680 | tf_op jit(solution)/shard_map/convert
  63.9 0.4 collective-permute-start.12
  64.3 4.2 %collective-permute-done.12 = bf16[16,2176]{1,0:T(8,128)(2,1)S(1)} collective-permute-done((bf16[16,2176]{1,0:T(8,128)(2,1)S(1)}, bf16[16,2176]{1,0:T(8,128)(2,1)S(1)}, u32[]{:S(2)}, u32[]{:S(2)}) %collective-permute-start.12) | collective-permute-done | bytes 69664 | tf_op jit(solution)/shard_map/ppermute | solution.py:246
  68.5 0.8 %collective-permute-start.15 = (bf16[16,2176]{1,0:T(8,128)(2,1)S(1)}, bf16[16,2176]{1,0:T(8,128)(2,1)S(1)}, u32[]{:S(2)}, u32[]{:S(2)}) collective-permute-start(bf16[16,2176]{1,0:T(8,128)(2,1)S(1)} %add_convert_fusion), channel_id=1, source_target_pairs={{0,12},{2,14},{4,8},{6,10},{8,4},{10,6},{12,0},{14,2},{1,13},{3,15... | collective-permute-start | bytes 208904 | tf_op jit(solution)/shard_map/ppermute | solution.py:246
  69.3 0.7 collective-permute-start.14
  70.1 2.9 %collective-permute-start.13 = (bf16[16,2176]{1,0:T(8,128)(2,1)S(1)}, bf16[16,2176]{1,0:T(8,128)(2,1)S(1)}, u32[]{:S(2)}, u32[]{:S(2)}) collective-permute-start(bf16[16,2176]{1,0:T(8,128)(2,1)S(1)} %add_convert_fusion), channel_id=1, source_target_pairs={{0,4},{2,6},{4,0},{6,2},{8,12},{10,14},{12,8},{14,10},{1,5},{3,7},... | collective-permute-start | bytes 208904 | tf_op jit(solution)/shard_map/ppermute | solution.py:246
  73.0 0.5 slice_bitcast_fusion.2
  73.5 2.1 %collective-permute-done.15 = bf16[16,2176]{1,0:T(8,128)(2,1)S(1)} collective-permute-done((bf16[16,2176]{1,0:T(8,128)(2,1)S(1)}, bf16[16,2176]{1,0:T(8,128)(2,1)S(1)}, u32[]{:S(2)}, u32[]{:S(2)}) %collective-permute-start.15) | collective-permute-done | bytes 69664 | tf_op jit(solution)/shard_map/ppermute | solution.py:246
  75.6 1.3 %collective-permute-done.14 = bf16[16,2176]{1,0:T(8,128)(2,1)S(1)} collective-permute-done((bf16[16,2176]{1,0:T(8,128)(2,1)S(1)}, bf16[16,2176]{1,0:T(8,128)(2,1)S(1)}, u32[]{:S(2)}, u32[]{:S(2)}) %collective-permute-start.14) | collective-permute-done | bytes 69664 | tf_op jit(solution)/shard_map/ppermute | solution.py:246
  76.9 0.6 slice.24
  77.5 0.7 slice_bitcast_fusion
  (47 shorter events, 0.5 us)
Async XLA Ops:
  0.6 19.7 %copy-start = (s32[16]{0:T(128)S(1)}, s32[16]{0:T(128)}, u32[]{:S(2)}) copy-start(s32[16]{0:T(128)} %param.14) | copy-start | bytes 196
  2.7 9.0 %copy-start.7 = (s32[8]{0:T(128)S(1)}, s32[8]{0:T(128)}, u32[]{:S(2)}) copy-start(s32[8]{0:T(128)} %constant.36.clone) | copy-start | bytes 100
  2.7 9.1 %copy-start.6 = (s32[24,9]{0,1:T(8,128)S(1)}, s32[24,9]{0,1:T(8,128)}, u32[]{:S(2)}) copy-start(s32[24,9]{0,1:T(8,128)} %param.13) | copy-start | bytes 2596
  6.5 5.6 %collective-permute-start = (f32[256,256]{1,0:T(8,128)}, f32[256,256]{1,0:T(8,128)S(1)}, u32[]{:S(2)}, u32[]{:S(2)}) collective-permute-start(f32[256,256]{1,0:T(8,128)} %get-tuple-element.14), channel_id=1, source_target_pairs={{0,1},{1,0},{2,3},{3,2},{4,5},{5,4},{6,7},{7,6},{8,9},{9,8},{10,11... | collective-permute-start | bytes 786440 | tf_op jit(solution)/shard_map/ppermute | solution.py:242
  11.5 23.9 %collective-permute-start.7 = (f32[384,256]{1,0:T(8,128)}, f32[384,256]{1,0:T(8,128)S(1)}, u32[]{:S(2)}, u32[]{:S(2)}) collective-permute-start(f32[384,256]{1,0:T(8,128)} %get-tuple-element.17), channel_id=1, source_target_pairs={{0,1},{1,0},{2,3},{3,2},{4,5},{5,4},{6,7},{7,6},{8,9},{9,8},{10,11... | collective-permute-start | bytes 1179656 | tf_op jit(solution)/shard_map/ppermute | solution.py:242
  12.1 0.7 copy-start.3
  14.8 8.1 %collective-permute-start.3 = (bf16[288,128]{1,0:T(8,128)(2,1)}, bf16[288,128]{1,0:T(8,128)(2,1)S(1)}, u32[]{:S(2)}, u32[]{:S(2)}) collective-permute-start(bf16[288,128]{1,0:T(8,128)(2,1)} %get-tuple-element.15), channel_id=1, source_target_pairs={{0,12},{2,14},{4,8},{6,10},{8,4},{10,6},{12,0},{14,2},{1,13},{3,15... | collective-permute-start | bytes 221192 | tf_op jit(solution)/shard_map/ppermute | solution.py:246
  19.8 6.6 %collective-permute-start.2 = (bf16[288,128]{1,0:T(8,128)(2,1)}, bf16[288,128]{1,0:T(8,128)(2,1)S(1)}, u32[]{:S(2)}, u32[]{:S(2)}) collective-permute-start(bf16[288,128]{1,0:T(8,128)(2,1)} %get-tuple-element.15), channel_id=1, source_target_pairs={{0,8},{2,10},{4,12},{6,14},{8,0},{10,2},{12,4},{14,6},{1,9},{3,11}... | collective-permute-start | bytes 221192 | tf_op jit(solution)/shard_map/ppermute | solution.py:246
  19.8 6.6 %collective-permute-start.1 = (bf16[288,128]{1,0:T(8,128)(2,1)}, bf16[288,128]{1,0:T(8,128)(2,1)S(1)}, u32[]{:S(2)}, u32[]{:S(2)}) collective-permute-start(bf16[288,128]{1,0:T(8,128)(2,1)} %get-tuple-element.15), channel_id=1, source_target_pairs={{0,4},{2,6},{4,0},{6,2},{8,12},{10,14},{12,8},{14,10},{1,5},{3,7},... | collective-permute-start | bytes 221192 | tf_op jit(solution)/shard_map/ppermute | solution.py:246
  20.4 6.0 %copy-start.4 = (bf16[288,128]{1,0:T(8,128)(2,1)S(1)}, bf16[288,128]{1,0:T(8,128)(2,1)}, u32[]{:S(2)}) copy-start(bf16[288,128]{1,0:T(8,128)(2,1)} %get-tuple-element.15) | copy-start | bytes 221188
  20.4 14.5 %copy-start.5 = (f32[8,256]{1,0:T(8,128)S(1)}, f32[8,256]{1,0:T(8,128)}, u32[]{:S(2)}) copy-start(f32[8,256]{1,0:T(8,128)} %get-tuple-element.21) | copy-start | bytes 24580
  20.4 16.0 %copy-start.1 = (f32[384,256]{1,0:T(8,128)S(1)}, f32[384,256]{1,0:T(8,128)}, u32[]{:S(2)}) copy-start(f32[384,256]{1,0:T(8,128)} %get-tuple-element.16.refs_5_) | copy-start | bytes 1179652
  20.4 16.0 %copy-start.2 = (bf16[16,128]{1,0:T(8,128)(2,1)S(1)}, bf16[16,128]{1,0:T(8,128)(2,1)}, u32[]{:S(2)}) copy-start(bf16[16,128]{1,0:T(8,128)(2,1)} %refs_7_.1) | copy-start | bytes 12292
  26.5 8.4 %collective-permute-start.4 = (bf16[4,288,128]{2,1,0:T(8,128)(2,1)S(1)}, bf16[4,288,128]{2,1,0:T(8,128)(2,1)S(1)}, u32[]{:S(2)}, u32[]{:S(2)}) collective-permute-start(bf16[4,288,128]{2,1,0:T(8,128)(2,1)S(1)} %pad_maximum_fusion.refs_0_), channel_id=1, source_target_pairs={{0,2},{2,0},{4,6},{6,4},{8,10},{10,8},{12,14},{14,12},{1,3},{3,1},... | collective-permute-start | bytes 884744 | tf_op jit(solution)/shard_map/ppermute | solution.py:246
  28.4 7.0 %collective-permute-start.5 = (bf16[4,288,128]{2,1,0:T(8,128)(2,1)S(1)}, bf16[4,288,128]{2,1,0:T(8,128)(2,1)S(1)}, u32[]{:S(2)}, u32[]{:S(2)}) collective-permute-start(bf16[4,288,128]{2,1,0:T(8,128)(2,1)S(1)} %pad_maximum_fusion.refs_0_), channel_id=1, source_target_pairs={{0,1},{1,0},{2,3},{3,2},{4,5},{5,4},{6,7},{7,6},{8,9},{9,8},{10,11... | collective-permute-start | bytes 884744 | tf_op jit(solution)/shard_map/ppermute | solution.py:242
  34.9 1.6 %collective-permute-start.6 = (bf16[4,288,128]{2,1,0:T(8,128)(2,1)S(1)}, bf16[4,288,128]{2,1,0:T(8,128)(2,1)S(1)}, u32[]{:S(2)}, u32[]{:S(2)}) collective-permute-start(bf16[4,288,128]{2,1,0:T(8,128)(2,1)S(1)} %collective-permute-done.4.refs_1_), channel_id=1, source_target_pairs={{0,1},{1,0},{2,3},{3,2},{4,5},{5,4},{6,7},{7,6},{8,9},{9,8},{10,11... | collective-permute-start | bytes 884744 | tf_op jit(solution)/shard_map/ppermute | solution.py:242
  34.9 13.9 %collective-permute-start.10 = (f32[8,256]{1,0:T(8,128)S(1)}, f32[8,256]{1,0:T(8,128)S(1)}, u32[]{:S(2)}, u32[]{:S(2)}) collective-permute-start(f32[8,256]{1,0:T(8,128)S(1)} %copy-done.5), channel_id=1, source_target_pairs={{0,1},{1,0},{2,3},{3,2},{4,5},{5,4},{6,7},{7,6},{8,9},{9,8},{10,11... | collective-permute-start | bytes 24584 | tf_op jit(solution)/shard_map/ppermute | solution.py:242
  44.4 11.8 %all-to-all-start = ((bf16[8,2,16,256]{3,2,1,0:T(8,128)(2,1)}), bf16[8,2,16,256]{3,2,1,0:T(8,128)(2,1)S(1)}, u32[]{:S(2)}, u32[]{:S(2)}) async-start(bf16[8,2,16,256]{3,2,1,0:T(8,128)(2,1)} %get-tuple-element.20), calls=%async_computation | async-start | bytes 262144 | tf_op jit(solution)/shard_map/all_to_all | solution.py:312
  48.8 1.2 %collective-permute-start.11 = (f32[16,128]{1,0:T(8,128)S(1)}, f32[16,128]{1,0:T(8,128)S(1)}, u32[]{:S(2)}, u32[]{:S(2)}) collective-permute-start(f32[16,128]{1,0:T(8,128)S(1)} %get-tuple-element.22), channel_id=1, source_target_pairs={{0,1},{1,0},{2,3},{3,2},{4,5},{5,4},{6,7},{7,6},{8,9},{9,8},{10,11... | collective-permute-start | bytes 24584 | tf_op jit(solution)/shard_map/ppermute | solution.py:242
  48.8 7.4 %collective-permute-start.8 = (bf16[16,384]{1,0:T(8,128)(2,1)S(1)}, bf16[16,384]{1,0:T(8,128)(2,1)S(1)}, u32[]{:S(2)}, u32[]{:S(2)}) collective-permute-start(bf16[16,384]{1,0:T(8,128)(2,1)S(1)} %get-tuple-element.19), channel_id=1, source_target_pairs={{0,1},{1,0},{2,3},{3,2},{4,5},{5,4},{6,7},{7,6},{8,9},{9,8},{10,11... | collective-permute-start | bytes 36872 | tf_op jit(solution)/shard_map/ppermute | solution.py:242
  56.2 3.6 %collective-permute-start.9 = (f32[2,16,256]{2,1,0:T(8,128)S(1)}, f32[2,16,256]{2,1,0:T(8,128)S(1)}, u32[]{:S(2)}, u32[]{:S(2)}) collective-permute-start(f32[2,16,256]{2,1,0:T(8,128)S(1)} %convert_reduce_fusion), channel_id=1, source_target_pairs={{0,1},{1,0},{2,3},{3,2},{4,5},{5,4},{6,7},{7,6},{8,9},{9,8},{10,11... | collective-permute-start | bytes 98312 | tf_op jit(solution)/shard_map/ppermute | solution.py:242
  63.9 4.6 %collective-permute-start.12 = (bf16[16,2176]{1,0:T(8,128)(2,1)S(1)}, bf16[16,2176]{1,0:T(8,128)(2,1)S(1)}, u32[]{:S(2)}, u32[]{:S(2)}) collective-permute-start(bf16[16,2176]{1,0:T(8,128)(2,1)S(1)} %pad_maximum_fusion.1), channel_id=1, source_target_pairs={{0,2},{2,0},{4,6},{6,4},{8,10},{10,8},{12,14},{14,12},{1,3},{3,1},... | collective-permute-start | bytes 208904 | tf_op jit(solution)/shard_map/ppermute | solution.py:246
  68.5 7.0 %collective-permute-start.15 = (bf16[16,2176]{1,0:T(8,128)(2,1)S(1)}, bf16[16,2176]{1,0:T(8,128)(2,1)S(1)}, u32[]{:S(2)}, u32[]{:S(2)}) collective-permute-start(bf16[16,2176]{1,0:T(8,128)(2,1)S(1)} %add_convert_fusion), channel_id=1, source_target_pairs={{0,12},{2,14},{4,8},{6,10},{8,4},{10,6},{12,0},{14,2},{1,13},{3,15... | collective-permute-start | bytes 208904 | tf_op jit(solution)/shard_map/ppermute | solution.py:246
  69.3 7.5 %collective-permute-start.14 = (bf16[16,2176]{1,0:T(8,128)(2,1)S(1)}, bf16[16,2176]{1,0:T(8,128)(2,1)S(1)}, u32[]{:S(2)}, u32[]{:S(2)}) collective-permute-start(bf16[16,2176]{1,0:T(8,128)(2,1)S(1)} %add_convert_fusion), channel_id=1, source_target_pairs={{0,8},{2,10},{4,12},{6,14},{8,0},{10,2},{12,4},{14,6},{1,9},{3,11}... | collective-permute-start | bytes 208904 | tf_op jit(solution)/shard_map/ppermute | solution.py:246
  70.1 6.8 %collective-permute-start.13 = (bf16[16,2176]{1,0:T(8,128)(2,1)S(1)}, bf16[16,2176]{1,0:T(8,128)(2,1)S(1)}, u32[]{:S(2)}, u32[]{:S(2)}) collective-permute-start(bf16[16,2176]{1,0:T(8,128)(2,1)S(1)} %add_convert_fusion), channel_id=1, source_target_pairs={{0,4},{2,6},{4,0},{6,2},{8,12},{10,14},{12,8},{14,10},{1,5},{3,7},... | collective-permute-start | bytes 208904 | tf_op jit(solution)/shard_map/ppermute | solution.py:246

commit v2 on v0

v2 whole, which is shorter than its diff:
```python
import functools
import math

import jax
import jax.numpy as jnp
from jax import lax
from jax.experimental import pallas as pl
from jax.experimental.pallas import tpu as pltpu
from jax.sharding import PartitionSpec as P

pool_temp = 0.05
loss_temp = 0.05
norm_eps = 1e-06
bf16 = jnp.bfloat16
f32 = jnp.float32
LANES = 128
EXP_SCALE = math.log2(math.e) / pool_temp
VMEM = pl.BlockSpec(memory_space=pltpu.VMEM)
SMEM = pl.BlockSpec(memory_space=pltpu.SMEM)
HBM = pl.BlockSpec(memory_space=pltpu.HBM)


def dot(a, b, contract, precision=None):
    return lax.dot_general(
        a, b, ((contract[0], contract[1]), ((), ())), precision=precision, preferred_element_type=f32
    )


NN = ((1,), (0,))
NT = ((1,), (1,))
TN = ((0,), (0,))


def project_kernel(info_ref, p_hbm, q_hbm, proj_hbm, down_hbm, send_ref, keep_ref, x_ref, weight_ref, down_ref, sems):
    core = info_ref[2]
    weights = [
        pltpu.make_async_copy(down_hbm, down_ref, sems.at[0]),
        pltpu.make_async_copy(proj_hbm, weight_ref.at[:, :LANES], sems.at[1]),
    ]
    loads = []
    for i, (owner, out) in enumerate(((1 - core, send_ref), (core, keep_ref))):
        at = 0
        for j, source in enumerate((p_hbm, q_hbm)):
            half = source.shape[0] // 2
            rows = pl.ds(pl.multiple_of(owner * half, LANES), half)
            to = slice(at, at + half)
            copy = pltpu.make_async_copy(source.at[rows, :], x_ref.at[i, to, :], sems.at[2 + 2 * i + j])
            loads.append((copy, out, i, to))
            at += half
    for copy in weights:
        copy.start()
    for copy, _, _, _ in loads[:2]:
        copy.start()
    weights[0].wait()
    rank, width = down_ref.shape
    low = jnp.concatenate([down_ref[...].astype(f32), jnp.zeros((LANES - rank, width), f32)], axis=0)
    weight_ref[:, LANES:] = jnp.transpose(low).astype(bf16)
    weights[1].wait()
    for copy, _, _, _ in loads[2:]:
        copy.start()
    for copy, out, i, to in loads:
        copy.wait()
        out[to, :] = dot(x_ref[i, to, :], weight_ref[...], NN)


def project(info, passage_rows, query_rows, projection, down):
    half, width = (passage_rows.shape[0] + query_rows.shape[0]) // 2, query_rows.shape[1]
    rank = down.shape[0]
    shape = jax.ShapeDtypeStruct((half, 2 * LANES), f32)
    operands = (passage_rows, query_rows, projection, down)
    operands = [pltpu.with_memory_space_constraint(x, pltpu.HBM) for x in operands]
    return pl.pallas_call(
        project_kernel,
        in_specs=[SMEM] + [HBM] * 4,
        out_specs=[VMEM] * 2,
        out_shape=(shape, shape),
        scratch_shapes=[
            pltpu.VMEM((2, half, width), bf16),
            pltpu.VMEM((width, 2 * LANES), bf16),
            pltpu.VMEM((rank, width), bf16),
            pltpu.SemaphoreType.DMA((6,)),
        ],
        compiler_params=pltpu.CompilerParams(vmem_limit_bytes=12 * 2**20),
        name="project",
    )(info, *operands)


def finish(keep, recv, up):
    rank = up.shape[0]
    low_bf = (keep[:, LANES : LANES + rank] + recv[:, LANES : LANES + rank]).astype(bf16)
    full = keep[:, :LANES] + recv[:, :LANES] + dot(low_bf, up, NN)
    r = lax.rsqrt(jnp.sum(full * full, axis=1, keepdims=True) + norm_eps)
    return low_bf, full * r, r


def pad_lanes(x):
    return jnp.concatenate([x, jnp.zeros((x.shape[0], LANES - x.shape[1]), x.dtype)], axis=1)


def pack_kernel(sizes, info_ref, table_ref, ids_ref, keep_ref, recv_ref, up_ref, p_ref, q_ref, r_ref):
    up = up_ref[...]
    rank = up.shape[0]
    low_bf, vn, r = finish(keep_ref[...], recv_ref[...], up)
    scaled = jnp.transpose(pad_lanes(low_bf.astype(f32) * r))[:rank, :].astype(bf16)
    vn = vn.astype(bf16)
    start = 0
    for ref, tokens in zip((p_ref, q_ref), sizes, strict=True):
        ref[:tokens, :] = vn[start : start + tokens, :]
        for t in range(tokens // LANES):
            at = start + t * LANES
            ref[tokens + t * rank : tokens + (t + 1) * rank, :] = scaled[:, at : at + LANES]
        start += tokens
    r_ref[...] = jnp.transpose(jnp.broadcast_to(r, (start, LANES)))[:8, :]
    ids = ids_ref[...]
    cands, qdev = ids.shape
    n_ids = table_ref.shape[0]
    if n_ids <= 16:
        rows = jnp.zeros(ids.shape, jnp.int32)
        for i in range(n_ids):
            rows = jnp.where(ids == i, table_ref[i], rows)
    else:
        rows = lax.fori_loop(
            0, n_ids, lambda i, c: jnp.where(ids == i, table_ref[i], c), jnp.zeros(ids.shape, jnp.int32)
        )
    half = qdev // 2
    wide = jnp.concatenate([pad_lanes(rows.astype(f32)), jnp.full((16 - cands, LANES), -1.0, f32)], axis=0)
    place = info_ref[0] * half
    wide = pltpu.roll(wide, lax.rem(place - info_ref[2] * half + LANES, LANES), 1)
    lane = lax.broadcasted_iota(jnp.int32, wide.shape, 1)
    wide = jnp.where((lane >= place) & (lane < place + half), wide, -1.0)
    q_ref[q_ref.shape[0] - 16 :, :] = wide.astype(bf16)


def pack_tokens(info, table, ids, keep, recv, up, ptok, qtok):
    rank = up.shape[0]
    return pl.pallas_call(
        functools.partial(pack_kernel, (ptok, qtok)),
        in_specs=[SMEM] * 2 + [VMEM] * 4,
        out_specs=[VMEM] * 3,
        out_shape=(
            jax.ShapeDtypeStruct((ptok + ptok // LANES * rank, LANES), bf16),
            jax.ShapeDtypeStruct((qtok + qtok // LANES * rank + 16, LANES), bf16),
            jax.ShapeDtypeStruct((8, ptok + qtok), f32),
        ),
        compiler_params=pltpu.CompilerParams(vmem_limit_bytes=8 * 2**20),
        name="pack_tokens",
    )(info, table, ids, keep, recv, up)


def both_queries(lo, mine_ref, other_ref, at):
    mine, other = mine_ref[at, :], other_ref[at, :]
    return jnp.where(lo == 0, mine, other), jnp.where(lo == 0, other, mine)


def over_packs(packs, body):
    at = 0
    for pack in packs:
        n = pack.shape[0]
        if n <= 8:
            for p in range(n):
                body(pack, p, at + p)
        else:
            lax.fori_loop(0, n, lambda p, c, pack=pack, at=at: (body(pack, p, at + p), c)[1], 0)
        at += n


def same_query(shape, dim, qlen):
    token = lax.broadcasted_iota(jnp.int32, shape, dim) // qlen
    return (token == lax.broadcasted_iota(jnp.int32, shape, 1 - dim)).astype(bf16)


def parts_of(wide, n):
    parts = []
    for _ in range(n):
        parts.append(wide.astype(bf16))
        wide = wide - parts[-1].astype(f32)
    return parts


def expo_of(vp, vqt):
    return jnp.exp2(dot(vp, vqt, NN) * EXP_SCALE)


def forward_kernel(cfg, *refs):
    qlen, qtok, plen, store, where, n_packs = cfg
    packs = refs[:n_packs]
    info_ref, mine_ref, other_ref = refs[n_packs : n_packs + 3]
    stats_ref, total_ref, sums_ref, expo_ref, vqt_ref = refs[n_packs + 3 :]
    lo = info_ref[0]
    first_half, second_half = both_queries(lo, mine_ref, other_ref, slice(0, qtok))
    vqt_ref[:, :qtok] = jnp.transpose(first_half.astype(f32)).astype(bf16)
    vqt_ref[:, qtok:] = jnp.transpose(second_half.astype(f32)).astype(bf16)
    tail = slice(mine_ref.shape[0] - 16, mine_ref.shape[0])
    rows = jnp.maximum(mine_ref[tail, :].astype(f32), other_ref[tail, :].astype(f32))

    def forward(pack, p, pos):
        expo = expo_of(pack[p, :plen, :], vqt_ref[...])
        total_ref[pl.ds(pos, 1), :] = jnp.sum(expo, axis=0, keepdims=True)
        if store:
            expo_ref[pos] = expo.astype(bf16)
        hi, core = where(info_ref, pos)
        here = (rows == ((hi * 2 + lo) * 2 + core).astype(f32)).astype(f32)
        stats_ref[1, pl.ds(pos, 1), :] = jnp.sum(here, axis=0, keepdims=True)
        stats_ref[2, pl.ds(pos, 1), :] = here[:1, :]

    over_packs(packs, forward)
    same = same_query((2 * qtok, LANES), 0, qlen)
    logits = sum(dot(part, same, NN) for part in parts_of(jnp.log(total_ref[...]), 3)) * (1.0 / qlen)
    stats_ref[0] = logits
    sums_ref[...] = jnp.zeros_like(sums_ref)
    sums_ref[:1, :] = jnp.sum(stats_ref[1] * jnp.exp(logits), axis=0, keepdims=True)
    sums_ref[1:2, :] = jnp.sum(stats_ref[2] * logits, axis=0, keepdims=True)


def backward_kernel(cfg, *refs):
    qlen, qtok, plen, store, where, n_packs = cfg
    packs = refs[:n_packs]
    info_ref, mine_ref, other_ref, up_ref, stats_ref, total_ref, sums_ref, recv_ref, expo_ref, vqt_ref = refs[
        n_packs : n_packs + 10
    ]
    refs = refs[n_packs + 10 :]
    n_parts = n_packs // 2 if store else 1
    part_refs, (dmine_ref, dother_ref, gup_ref, loss_ref) = refs[:n_parts], refs[n_parts : n_parts + 4]
    scale_ref, dvqt_ref, grad_ref, dv_ref, dvb_ref = refs[n_parts + 4 :]
    up = up_ref[...]
    rank = up.shape[0]
    lo = info_ref[0]
    vq = jnp.concatenate(both_queries(lo, mine_ref, other_ref, slice(0, qtok)), axis=0)
    logits, mult, first = stats_ref[0], stats_ref[1], stats_ref[2]
    summed = sums_ref[:1, :] + recv_ref[:1, :]
    live = lax.broadcasted_iota(jnp.int32, summed.shape, 1) < 2 * qtok // qlen
    summed = jnp.where(live, summed, 1.0)
    loss_ref[...] = jnp.broadcast_to(jnp.log(summed) - (sums_ref[1:2, :] + recv_ref[1:2, :]), loss_ref.shape)
    dscore = (mult * jnp.exp(logits) / summed - first) * (1.0 / loss_temp)
    same = same_query((LANES, 2 * qtok), 1, qlen)
    scale_ref[...] = sum(dot(part, same, NN) for part in parts_of(dscore, 2)) / (total_ref[...] * qlen)

    def scaled_low(pack, p):
        blocks = range(plen, plen + plen // LANES * rank, rank)
        return jnp.concatenate([pack[p, at : at + rank, :] for at in blocks], axis=1)

    def project_out(vp, dv):
        vpf = vp.astype(f32)
        return (dv - vpf * jnp.sum(vpf * dv, axis=1, keepdims=True)).astype(bf16)

    if store:
        for pos in range(n_packs):
            rows = slice(pos * plen, (pos + 1) * plen)
            grad_ref[rows, :] = (expo_ref[pos].astype(f32) * scale_ref[pos : pos + 1, :]).astype(bf16)
        dv_ref[...] = dot(grad_ref[...], vq, NN)
        for pos, pack in enumerate(packs):
            rows = slice(pos * plen, (pos + 1) * plen)
            vp = pack[0, :plen, :]
            dvqt = dot(vp, grad_ref[rows, :], TN)
            dvqt_ref[...] = dvqt if pos == 0 else dvqt_ref[...] + dvqt
            dv = project_out(vp, dv_ref[rows, :])
            dvb_ref[rows, :] = dv
            part_refs[pos % n_parts][where(info_ref, pos)[1]] = dot(up, dv, NT).astype(bf16)
        lows = jnp.concatenate([scaled_low(pack, 0) for pack in packs], axis=1)
        gup = dot(lows, dvb_ref[...], NN)
    else:
        dvqt_ref[...] = jnp.zeros_like(dvqt_ref)
        gup_ref[...] = jnp.zeros_like(gup_ref)

        def backward(pack, p, pos):
            vp = pack[p, :plen, :]
            grad = (expo_of(vp, vqt_ref[...]) * scale_ref[pl.ds(pos, 1), :]).astype(bf16)
            dvqt_ref[...] += dot(vp, grad, TN)
            dv = project_out(vp, dot(grad, vq, NN))
            hi, core = where(info_ref, pos)
            part_refs[0][hi, core] = dot(up, dv, NT).astype(bf16)
            gup_ref[...] += dot(scaled_low(pack, p), dv, NN)

        over_packs(packs, backward)
        gup = gup_ref[...]

    vqt = vqt_ref[...].astype(f32)
    dvqt = dvqt_ref[...]
    dvqt = (dvqt - vqt * jnp.sum(vqt * dvqt, axis=0, keepdims=True)).astype(bf16)
    dlow = dot(up, dvqt, NN)
    dmine_ref[...] = jnp.where(lo == 0, dlow[:, :qtok], dlow[:, qtok:])
    dother_ref[...] = jnp.where(lo == 0, dlow[:, qtok:], dlow[:, :qtok])
    lows = [
        both_queries(lo, mine_ref, other_ref, slice(at, at + rank))
        for at in range(qtok, qtok + qtok // LANES * rank, rank)
    ]
    lows = jnp.concatenate([low[0] for low in lows] + [low[1] for low in lows], axis=1)
    gup_ref[...] = gup + dot(lows, dvqt, NT)


def places(steps):
    def where(info_ref, pos):
        n = len(steps)
        if n <= 8:
            return jnp.bitwise_xor(info_ref[1], steps[pos % n]), info_ref[2] if pos < n else 1 - info_ref[2]
        return lax.rem(pos, n), jnp.where(pos < n, info_ref[2], 1 - info_ref[2])

    return where


def score_forward(packs, steps, info, mine, other, qlen, qtok, plen):
    npos = 2 * len(steps)
    store = len(packs) == npos
    cfg = (qlen, qtok, plen, store, places(steps), len(packs))
    return pl.pallas_call(
        functools.partial(forward_kernel, cfg),
        in_specs=[VMEM] * len(packs) + [SMEM] + [VMEM] * 2,
        out_specs=[VMEM] * 5,
        out_shape=(
            jax.ShapeDtypeStruct((3, npos, LANES), f32),
            jax.ShapeDtypeStruct((npos, 2 * qtok), f32),
            jax.ShapeDtypeStruct((8, LANES), f32),
            jax.ShapeDtypeStruct((npos, plen, 2 * qtok) if store else (1, 16, LANES), bf16),
            jax.ShapeDtypeStruct((LANES, 2 * qtok), bf16),
        ),
        compiler_params=pltpu.CompilerParams(vmem_limit_bytes=(16 if store else 40) * 2**20),
        name="score_forward",
    )(*packs, info, mine, other)


def score_backward(packs, steps, info, mine, other, up, stats, total, sums, recv, expo, vqt, qlen, qtok, plen):
    npos, rank = 2 * len(steps), up.shape[0]
    store = len(packs) == npos
    cfg = (qlen, qtok, plen, store, places(steps), len(packs))
    part = jax.ShapeDtypeStruct((2, rank, plen), bf16)
    whole = jax.ShapeDtypeStruct((len(steps), 2, rank, plen), bf16)
    kept = npos * plen if store else 16
    parts = (part,) * len(steps) if store else (whole,)
    return pl.pallas_call(
        functools.partial(backward_kernel, cfg),
        in_specs=[VMEM] * len(packs) + [SMEM] + [VMEM] * 9,
        out_specs=[VMEM] * (len(parts) + 4),
        out_shape=(
            *parts,
            jax.ShapeDtypeStruct((rank, qtok), f32),
            jax.ShapeDtypeStruct((rank, qtok), f32),
            jax.ShapeDtypeStruct((rank, LANES), f32),
            jax.ShapeDtypeStruct((8, LANES), f32),
        ),
        scratch_shapes=[
            pltpu.VMEM((npos, 2 * qtok), f32),
            pltpu.VMEM((LANES, 2 * qtok), f32),
            pltpu.VMEM((kept, 2 * qtok), bf16),
            pltpu.VMEM((kept, LANES), f32),
            pltpu.VMEM((kept, LANES), bf16),
        ],
        compiler_params=pltpu.CompilerParams(vmem_limit_bytes=(20 if store else 40) * 2**20),
        name="score_backward",
    )(*packs, info, mine, other, up, stats, total, sums, recv, expo, vqt)


def collect_kernel(n, *refs):
    parts, (mine_ref, recv_ref, r_ref, up_ref, out_ref) = refs[:n], refs[n:]
    _, _, plen = parts[0].shape
    qtok = mine_ref.shape[1]
    for i in range(2):
        out_ref[:, i * plen : (i + 1) * plen] = sum(part[i].astype(f32) for part in parts)
    out_ref[:, 2 * plen : 2 * plen + qtok] = (mine_ref[...] + recv_ref[...]) * r_ref[:1, plen:]
    out_ref[:, 2 * plen + qtok :] = up_ref[...]


def collect(parts, mine, recv, r, up):
    rank, qtok = mine.shape
    plen = parts[0].shape[2]
    return pl.pallas_call(
        functools.partial(collect_kernel, len(parts)),
        in_specs=[VMEM] * (len(parts) + 4),
        out_specs=VMEM,
        out_shape=jax.ShapeDtypeStruct((rank, 2 * plen + qtok + LANES), f32),
        compiler_params=pltpu.CompilerParams(vmem_limit_bytes=4 * 2**20),
        name="collect",
    )(*parts, mine, recv, r, up)


def grad_kernel(plen, qtok, info_ref, p_ref, q_ref, mine_ref, other_ref, r_mine_ref, r_other_ref, out_ref):
    core = info_ref[2]
    width = p_ref.shape[1]
    queries = slice(2 * plen, 2 * plen + qtok)
    q_mine, q_other = mine_ref[:, queries].astype(bf16), other_ref[:, queries].astype(bf16)
    q_dlow = [jnp.where(core == i, q_mine, q_other) for i in range(2)]
    p_dlow = []
    for i in range(2):
        r = jnp.where(core == i, r_mine_ref[:1, :plen], r_other_ref[:1, :plen])
        rows = slice(i * plen, (i + 1) * plen)
        p_dlow.append(((mine_ref[:, rows] + other_ref[:, rows]) * r).astype(bf16))
    total = dot(jnp.concatenate(q_dlow, axis=1), q_ref[...], NN)
    total += dot(jnp.concatenate(p_dlow, axis=1), p_ref[...], NN)
    out_ref[:, :width] = total.astype(bf16)
    out_ref[:, width:] = (mine_ref[:, 2 * plen + qtok :] + other_ref[:, 2 * plen + qtok :]).astype(bf16)


def grad_all(info, passage_rows, query_rows, mine, other, r_mine, r_other, plen, qtok):
    rank, width = mine.shape[0], passage_rows.shape[1]
    return pl.pallas_call(
        functools.partial(grad_kernel, plen, qtok),
        in_specs=[SMEM] + [VMEM] * 6,
        out_specs=VMEM,
        out_shape=jax.ShapeDtypeStruct((rank, width + LANES), bf16),
        compiler_params=pltpu.CompilerParams(vmem_limit_bytes=4 * 2**20),
        name="grad_all",
    )(info, passage_rows, query_rows, mine, other, r_mine, r_other)


def add_kernel(a_ref, b_ref, c_ref, d_ref, down_ref, up_ref):
    total = (a_ref[...].astype(f32) + b_ref[...].astype(f32)) + (
        c_ref[...].astype(f32) + d_ref[...].astype(f32)
    )
    width = down_ref.shape[1]
    down_ref[...] = total[:, :width]
    up_ref[...] = total[:, width:]


def add_four(parts, width):
    rank = parts[0].shape[0]
    return pl.pallas_call(
        add_kernel,
        in_specs=[VMEM] * 4,
        out_specs=[VMEM] * 2,
        out_shape=(
            jax.ShapeDtypeStruct((rank, width), f32),
            jax.ShapeDtypeStruct((rank, LANES), f32),
        ),
        compiler_params=pltpu.CompilerParams(vmem_limit_bytes=4 * 2**20),
        name="add_four",
    )(*parts)


def swap(x):
    return lax.ppermute(x, "sub", [(0, 1), (1, 0)])


def across(x, nshard, step):
    return lax.ppermute(x, "shard", [(i, i ^ step) for i in range(nshard)])


def gather_packs(pack, nshard, groups):
    if nshard == 8:
        pack = pack[None]
        near = [pack] + [across(pack, nshard, k) for k in (6, 4, 2)]
        return near + [swap(piece) for piece in near], (0, 3, 2, 1)
    near = lax.all_gather(pack, "shard", axis_index_groups=groups)
    return [near, swap(near)], tuple(range(nshard // 2))


def exchange_parts(parts, steps, nshard, groups):
    if len(parts) == 1:
        parts = lax.all_to_all(parts[0], "shard", split_axis=0, concat_axis=0, tiled=True, axis_index_groups=groups)
        return [jnp.sum(parts.astype(f32), axis=0)]
    return [parts[0]] + [across(part, nshard, 2 * step) for part, step in zip(parts[1:], steps[1:], strict=True)]


def sum_over_shards(x, nshard, width):
    if nshard != 8:
        x = lax.psum(x.astype(f32), "shard")
        return x[:, :width], x[:, width:]
    x = (x.astype(f32) + across(x, nshard, 1).astype(f32)).astype(bf16)
    return add_four([x] + [across(x, nshard, k) for k in (2, 4, 6)], width)


def per_device(
    query_hidden_states,
    passage_hidden_states,
    projection_matrix,
    adapter_down_weight,
    adapter_up_weight,
    passage_pair_index,
    passage_row_table,
):
    nshard = lax.axis_size("shard")
    core = lax.axis_index("sub").astype(jnp.int32)
    shard = lax.axis_index("shard").astype(jnp.int32)
    info = jnp.stack([shard % 2, shard // 2, core])
    groups = [list(range(parity, nshard, 2)) for parity in range(2)]
    qdev, qlen, width = query_hidden_states.shape
    pdev, plen, _ = passage_hidden_states.shape
    half = qdev // 2
    qtok = half * qlen
    query_rows = query_hidden_states.reshape(qdev * qlen, width)
    passage_rows = passage_hidden_states.reshape(pdev * plen, width)

    send, keep = project(info, passage_rows, query_rows, projection_matrix, jnp.transpose(adapter_down_weight))
    ppack, mine, r = pack_tokens(
        info, passage_row_table, jnp.transpose(passage_pair_index), keep, swap(send), adapter_up_weight, plen, qtok
    )
    other = across(mine, nshard, 1)
    packs, steps = gather_packs(ppack, nshard, groups)
    r_other = swap(r)

    stats, total, sums, expo, vqt = score_forward(packs, steps, info, mine, other, qlen, qtok, plen)
    *parts, dlow_mine, dlow_other, gup, loss = score_backward(
        packs,
        steps,
        info,
        mine,
        other,
        adapter_up_weight,
        stats,
        total,
        sums,
        across(sums, nshard, 1),
        expo,
        vqt,
        qlen,
        qtok,
        plen,
    )
    parts = exchange_parts(parts, steps, nshard, groups)
    collected = collect(parts, dlow_mine, across(dlow_other, nshard, 1), r, gup)
    grads = grad_all(info, passage_rows, query_rows, collected, swap(collected), r, r_other, plen, qtok)
    query_loss = lax.dynamic_slice_in_dim(loss[0], info[0] * half, half, 0)
    down_sum, up_sum = sum_over_shards(grads, nshard, width)
    return (query_loss, jnp.transpose(down_sum), up_sum)


def solution(mesh):
    placed = (
        P(("groups", "shard"), None, "sub"),
        P(("groups", "shard"), None, "sub"),
        P("sub", None),
        P("sub", None),
        P(),
        P(("groups", "shard"), None),
        P("groups"),
    )
    return jax.shard_map(
        per_device,
        mesh=mesh,
        in_specs=placed,
        out_specs=(P(("groups", "shard", "sub")), P(("groups", "sub"), None), P("groups", None)),
        check_vma=False,
    )
```

time: 354 us -> 56.8 us (0.16)
  matrix products: 93.2 us -> 0 us
  waiting for transfers between devices: 109 us -> 20.5 us
  local copies, waits for them, and re-layouts: 64.4 us -> 0.6 us
  blocking collectives: 26.7 us -> 0 us
  other arithmetic: 19 us -> 0.1 us
  Pallas kernels: 0 us -> 13.4 us
  between operations: 14.1 us -> 0.75 us
  starting transfers between devices: 25.1 us -> 21.4 us
    dot_general x32 -> x0, matrix products: 93.2 us -> none  [the longest x4 27.2 us: backward(): jnp.einsum('sp,sje->pje', sel, contrib, precision=lax.Precision.HIGHEST)]
    psum x3 -> x0, waiting for transfers between devices: 79.3 us -> none  [the longest x1 47.2 us: per_device(): grad_down, grad_up = lax.psum((grad_down, grad_up), 'shard')]
    all_to_all x5 -> x0, waiting for transfers between devices: 29.9 us -> none  [the longest x1 22.6 us: per_device(): lax.all_to_all(send_vec, 'shard', split_axis=0, concat_axis=0, tiled=True)]
    psum x2 -> x0, blocking collectives: 26.7 us -> none  [the longest x1 22.5 us: per_device(): grad_down, grad_up = lax.psum((grad_down, grad_up), 'shard')]
    all_to_all x5 -> x0, starting transfers between devices: 24.7 us -> none  [the longest x1 7.25 us: per_device(): lax.all_to_all(send_loc, 'shard', split_axis=0, concat_axis=0, tiled=True)]
    ppermute x0 -> x20, starting transfers between devices: none -> 21.4 us  [the longest x13 19.8 us: across(): return lax.ppermute(x, 'shard', [(i, i ^ step) for i in range(nshard)])]
    ppermute x0 -> x20, waiting for transfers between devices: none -> 20.5 us  [the longest x13 17 us: across(): return lax.ppermute(x, 'shard', [(i, i ^ step) for i in range(nshard)])]
    pallas_call x0 -> x7, Pallas kernels: none -> 13.4 us  [the longest x1 5.06 us: project(): pl.pallas_call(project_kernel, in_specs=[SMEM] + [HBM] * 4, out_specs=[VM...]
  transfers between devices with their start and end apart: 8 -> 20, of which waited for: 6 -> 11; matrix products, arithmetic and copies ran while one was open for 21% -> 1% of each run, Pallas kernels for 0% -> 0%
where the time goes in v2:
time: 56.8 us; the launch traced here: 56.7 us
  starting transfers between devices  21.4 us (38%)
  waiting for transfers between devices  20.5 us (36%)
  Pallas kernels  13.4 us (24%)
  between operations  0.75 us (1%)
  local copies, waits for them, and re-layouts  0.6 us (1%)
    ppermute x13, starting transfers between devices, across(): return lax.ppermute(x, 'shard', [(i, i ^ step) for i in range(nshard)])  19.8 us
    ppermute x13, waiting for transfers between devices, across(): return lax.ppermute(x, 'shard', [(i, i ^ step) for i in range(nshard)])  17 us
    pallas_call x1, Pallas kernels, project(): pl.pallas_call(project_kernel, in_specs=[SMEM] + [HBM] * 4, out_specs=[VM...  5.06 us
    ppermute x7, waiting for transfers between devices, swap(): return lax.ppermute(x, 'sub', [(0, 1), (1, 0)])  3.48 us
    pallas_call x1, Pallas kernels, score_backward(): pl.pallas_call(functools.partial(backward_kernel, cfg), in_specs=[VMEM] *...  3.44 us
    pallas_call x1, Pallas kernels, score_forward(): pl.pallas_call(functools.partial(forward_kernel, cfg), in_specs=[VMEM] *...  1.88 us
    ppermute x7, starting transfers between devices, swap(): return lax.ppermute(x, 'sub', [(0, 1), (1, 0)])  1.6 us
    pallas_call x1, Pallas kernels, grad_all(): pl.pallas_call(functools.partial(grad_kernel, plen, qtok), in_specs=[SMEM...  1.33 us
  transfers between devices with their start and end apart: 20, of which 11 were waited for; matrix products, arithmetic and copies ran while one was open for 1% of the time, Pallas kernels for 0%

profile of v2, /device:TPU:0, one launch (start us, length us, event | category | flops | bytes accessed | tf_op | source)
XLA Modules:
  0.0 56.7 jit_solution(16014171004105511740)
XLA Ops:
  0.7 0.1 pad_add_fusion.info_ref.refs_8_
  0.8 5.1 %project.1 = (f32[640,256]{1,0:T(8,128)S(1)}, f32[640,256]{1,0:T(8,128)S(1)}) custom-call(s32[3]{0:T(128)S(1)} %pad_add_fusion.info_ref.refs_8_, bf16[512,2048]{1,0:T(8,128)(2,1)} %bitcast.13, bf16[768,2048]{1,0:T(8,128)(2,1)} %bitcast.11, bf16[2048,128]{1,0:T(8,128)(2,1)} %proj_hbm.1, bf16[16,2048]{1,0:T(8,128)(2,1)} %bitcast.22), custom_call_target="tpu_custom_call" | custom-call | tf_op jit(solution)/shard_map/project/pallas_call | solution.py:72
  5.8 0.5 collective-permute-start
  6.3 1.7 %collective-permute-done.recv_ref = f32[640,256]{1,0:T(8,128)S(1)} collective-permute-done((f32[640,256]{1,0:T(8,128)S(1)}, f32[640,256]{1,0:T(8,128)S(1)}, u32[]{:S(2)}, u32[]{:S(2)}) %collective-permute-start) | collective-permute-done | bytes 655392 | tf_op jit(solution)/shard_map/ppermute | solution.py:429
  8.1 0.0 copy-start.1
  8.1 1.0 %pack_tokens.1 = (bf16[288,128]{1,0:T(8,128)(2,1)S(1)}, bf16[448,128]{1,0:T(8,128)(2,1)S(1)}, f32[8,640]{1,0:T(8,128)S(1)}) custom-call(s32[3]{0:T(128)S(1)} %pad_add_fusion.info_ref.refs_8_, s32[16]{0:T(128)S(1)} %copy-done.4, s32[9,24]{1,0:T(8,128)S(1)} %bitcast.21, f32[640,256]{1,0:T(8,128)S(1)} %get-tuple-element.23.keep_ref, ...), custom_call_target="tpu_custom_call" | custom-call | tf_op jit(solution)/shard_map/pack_tokens/pallas_call | solution.py:136
  9.1 5.0 %collective-permute-start.1 = (bf16[1,288,128]{2,1,0:T(8,128)(2,1)S(1)}, bf16[1,288,128]{2,1,0:T(8,128)(2,1)S(1)}, u32[]{:S(2)}, u32[]{:S(2)}) collective-permute-start(bf16[1,288,128]{2,1,0:T(8,128)(2,1)S(1)} %bitcast.15), channel_id=1, source_target_pairs={{0,12},{2,14},{4,8},{6,10},{8,4},{10,6},{12,0},{14,2},{1,13},{3,15... | collective-permute-start | bytes 221192 | tf_op jit(solution)/shard_map/ppermute | solution.py:433
  14.1 0.0 collective-permute-start.2
  14.1 0.6 %collective-permute-start.3 = (bf16[1,288,128]{2,1,0:T(8,128)(2,1)S(1)}, bf16[1,288,128]{2,1,0:T(8,128)(2,1)S(1)}, u32[]{:S(2)}, u32[]{:S(2)}) collective-permute-start(bf16[1,288,128]{2,1,0:T(8,128)(2,1)S(1)} %bitcast.17), channel_id=1, source_target_pairs={{0,4},{2,6},{4,0},{6,2},{8,12},{10,14},{12,8},{14,10},{1,5},{3,7},... | collective-permute-start | bytes 221192 | tf_op jit(solution)/shard_map/ppermute | solution.py:433
  14.7 1.6 %collective-permute-start.8 = (bf16[448,128]{1,0:T(8,128)(2,1)S(1)}, bf16[448,128]{1,0:T(8,128)(2,1)S(1)}, u32[]{:S(2)}, u32[]{:S(2)}) collective-permute-start(bf16[448,128]{1,0:T(8,128)(2,1)S(1)} %get-tuple-element.26.refs_9_), channel_id=1, source_target_pairs={{0,2},{2,0},{4,6},{6,4},{8,10},{10,8},{12,14},{14,12},{1,3},{3,1},... | collective-permute-start | bytes 344072 | tf_op jit(solution)/shard_map/ppermute | solution.py:433
  16.4 0.0 collective-permute-start.4
  16.4 0.7 %collective-permute-done.1.refs_1_ = bf16[1,288,128]{2,1,0:T(8,128)(2,1)S(1)} collective-permute-done((bf16[1,288,128]{2,1,0:T(8,128)(2,1)S(1)}, bf16[1,288,128]{2,1,0:T(8,128)(2,1)S(1)}, u32[]{:S(2)}, u32[]{:S(2)}) %collective-permute-start.1) | collective-permute-done | bytes 73760 | tf_op jit(solution)/shard_map/ppermute | solution.py:433
  17.1 0.0 collective-permute-start.5
  17.1 3.5 %collective-permute-done.2.refs_2_ = bf16[1,288,128]{2,1,0:T(8,128)(2,1)S(1)} collective-permute-done((bf16[1,288,128]{2,1,0:T(8,128)(2,1)S(1)}, bf16[1,288,128]{2,1,0:T(8,128)(2,1)S(1)}, u32[]{:S(2)}, u32[]{:S(2)}) %collective-permute-start.2) | collective-permute-done | bytes 73760 | tf_op jit(solution)/shard_map/ppermute | solution.py:433
  20.6 0.0 collective-permute-start.6
  20.6 0.0 collective-permute-done.3.refs_3_
  20.6 0.5 collective-permute-start.7
  21.1 0.0 collective-permute-done.4.refs_4_
  21.1 0.0 collective-permute-done.8.refs_10_
  21.1 0.0 collective-permute-done.5.refs_5_
  21.1 0.7 %collective-permute-done.6.refs_6_ = bf16[1,288,128]{2,1,0:T(8,128)(2,1)S(1)} collective-permute-done((bf16[1,288,128]{2,1,0:T(8,128)(2,1)S(1)}, bf16[1,288,128]{2,1,0:T(8,128)(2,1)S(1)}, u32[]{:S(2)}, u32[]{:S(2)}) %collective-permute-start.6) | collective-permute-done | bytes 73760 | tf_op jit(solution)/shard_map/ppermute | solution.py:429
  21.9 0.2 collective-permute-done.7.refs_7_
  22.0 1.9 %score_forward.1 = (f32[3,8,128]{2,1,0:T(8,128)S(1)}, f32[8,768]{1,0:T(8,128)S(1)}, f32[8,128]{1,0:T(8,128)S(1)}, bf16[8,256,768]{2,1,0:T(8,128)(2,1)S(1)}, bf16[128,768]{1,0:T(8,128)(2,1)S(1)}) custom-call(bf16[1,288,128]{2,1,0:T(8,128)(2,1)S(1)} %bitcast.19, bf16[1,288,128]{2,1,0:T(8,128)(2,1)S(1)} %collective-permute-done.1.refs_1_, ...), custom_call_target="tpu_custom_call" | custom-call | tf_op jit(solution)/shard_map/score_forward/pallas_call | solution.py:305
  23.9 1.6 %collective-permute-start.9 = (f32[8,128]{1,0:T(8,128)S(1)}, f32[8,128]{1,0:T(8,128)S(1)}, u32[]{:S(2)}, u32[]{:S(2)}) collective-permute-start(f32[8,128]{1,0:T(8,128)S(1)} %get-tuple-element.29.refs_14_), channel_id=1, source_target_pairs={{0,2},{2,0},{4,6},{6,4},{8,10},{10,8},{12,14},{14,12},{1,3},{3,1},... | collective-permute-start | bytes 12296 | tf_op jit(solution)/shard_map/ppermute | solution.py:433
  25.5 2.1 %collective-permute-done.9.refs_15_ = f32[8,128]{1,0:T(8,128)S(1)} collective-permute-done((f32[8,128]{1,0:T(8,128)S(1)}, f32[8,128]{1,0:T(8,128)S(1)}, u32[]{:S(2)}, u32[]{:S(2)}) %collective-permute-start.9) | collective-permute-done | bytes 4128 | tf_op jit(solution)/shard_map/ppermute | solution.py:433
  27.6 3.4 %score_backward.1 = (bf16[2,16,256]{2,1,0:T(8,128)(2,1)S(1)}, bf16[2,16,256]{2,1,0:T(8,128)(2,1)S(1)}, bf16[2,16,256]{2,1,0:T(8,128)(2,1)S(1)}, bf16[2,16,256]{2...) custom-call(bf16[1,288,128]{2,1,0:T(8,128)(2,1)S(1)} %bitcast.20, ...), custom_call_target="tpu_custom_call" | custom-call | tf_op jit(solution)/shard_map/score_backward/pallas_call | solution.py:329
  31.0 1.5 %collective-permute-start.13 = (f32[16,384]{1,0:T(8,128)S(1)}, f32[16,384]{1,0:T(8,128)S(1)}, u32[]{:S(2)}, u32[]{:S(2)}) collective-permute-start(f32[16,384]{1,0:T(8,128)S(1)} %get-tuple-element.38), channel_id=1, source_target_pairs={{0,2},{2,0},{4,6},{6,4},{8,10},{10,8},{12,14},{14,12},{1,3},{3,1},... | collective-permute-start | bytes 73736 | tf_op jit(solution)/shard_map/ppermute | solution.py:433
  32.6 2.5 %collective-permute-start.10 = (bf16[2,16,256]{2,1,0:T(8,128)(2,1)S(1)}, bf16[2,16,256]{2,1,0:T(8,128)(2,1)S(1)}, u32[]{:S(2)}, u32[]{:S(2)}) collective-permute-start(bf16[2,16,256]{2,1,0:T(8,128)(2,1)S(1)} %get-tuple-element.34), channel_id=1, source_target_pairs={{0,12},{2,14},{4,8},{6,10},{8,4},{10,6},{12,0},{14,2},{1,13},{3,15... | collective-permute-start | bytes 49160 | tf_op jit(solution)/shard_map/ppermute | solution.py:433
  35.1 0.0 collective-permute-start.11
  35.1 1.9 %collective-permute-start.12 = (bf16[2,16,256]{2,1,0:T(8,128)(2,1)S(1)}, bf16[2,16,256]{2,1,0:T(8,128)(2,1)S(1)}, u32[]{:S(2)}, u32[]{:S(2)}) collective-permute-start(bf16[2,16,256]{2,1,0:T(8,128)(2,1)S(1)} %get-tuple-element.36), channel_id=1, source_target_pairs={{0,4},{2,6},{4,0},{6,2},{8,12},{10,14},{12,8},{14,10},{1,5},{3,7},... | collective-permute-start | bytes 49160 | tf_op jit(solution)/shard_map/ppermute | solution.py:433
  37.0 1.1 %collective-permute-done.10.refs_1_ = bf16[2,16,256]{2,1,0:T(8,128)(2,1)S(1)} collective-permute-done((bf16[2,16,256]{2,1,0:T(8,128)(2,1)S(1)}, bf16[2,16,256]{2,1,0:T(8,128)(2,1)S(1)}, u32[]{:S(2)}, u32[]{:S(2)}) %collective-permute-start.10) | collective-permute-done | bytes 16416 | tf_op jit(solution)/shard_map/ppermute | solution.py:433
  38.1 1.6 %collective-permute-done.11.refs_2_ = bf16[2,16,256]{2,1,0:T(8,128)(2,1)S(1)} collective-permute-done((bf16[2,16,256]{2,1,0:T(8,128)(2,1)S(1)}, bf16[2,16,256]{2,1,0:T(8,128)(2,1)S(1)}, u32[]{:S(2)}, u32[]{:S(2)}) %collective-permute-start.11) | collective-permute-done | bytes 16416 | tf_op jit(solution)/shard_map/ppermute | solution.py:433
  39.7 0.0 collective-permute-done.12.refs_3_
  39.7 0.0 collective-permute-done.13.refs_5_
  39.7 0.1 collective-permute-start.14
  39.8 0.5 collective-permute-start.15
  40.3 0.8 %collective-permute-done.15.r_other_ref = f32[8,640]{1,0:T(8,128)S(1)} collective-permute-done((f32[8,640]{1,0:T(8,128)S(1)}, f32[8,640]{1,0:T(8,128)S(1)}, u32[]{:S(2)}, u32[]{:S(2)}) %collective-permute-start.15) | collective-permute-done | bytes 20512 | tf_op jit(solution)/shard_map/ppermute | solution.py:429
  41.1 0.0 collective-permute-done.14.other_ref
  41.1 1.3 %grad_all.1 = bf16[16,2176]{1,0:T(8,128)(2,1)S(1)} custom-call(s32[3]{0:T(128)S(1)} %pad_add_fusion.info_ref.refs_8_, bf16[512,2048]{1,0:T(8,128)(2,1)S(1)} %bitcast.14, bf16[768,2048]{1,0:T(8,128)(2,1)S(1)} %bitcast.12, f32[16,1024]{1,0:T(8,128)S(1)} %collect.1.mine_ref, f32[16,1024]{1,0:T(8,128)S(1)} %collective-permute-done.14.other_ref, ...), custom_call_target="tpu_custom_call" | custom-call | tf_op jit(solution)/shard_map/grad_all/pallas_call | solution.py:394
  42.5 0.6 collective-permute-start.16
  43.0 3.9 %collective-permute-done.16 = bf16[16,2176]{1,0:T(8,128)(2,1)S(1)} collective-permute-done((bf16[16,2176]{1,0:T(8,128)(2,1)S(1)}, bf16[16,2176]{1,0:T(8,128)(2,1)S(1)}, u32[]{:S(2)}, u32[]{:S(2)}) %collective-permute-start.16) | collective-permute-done | bytes 69664 | tf_op jit(solution)/shard_map/ppermute | solution.py:433
  46.9 1.1 %collective-permute-start.17 = (bf16[16,2176]{1,0:T(8,128)(2,1)S(1)}, bf16[16,2176]{1,0:T(8,128)(2,1)S(1)}, u32[]{:S(2)}, u32[]{:S(2)}) collective-permute-start(bf16[16,2176]{1,0:T(8,128)(2,1)S(1)} %add_convert_fusion.a_ref), channel_id=1, source_target_pairs={{0,4},{2,6},{4,0},{6,2},{8,12},{10,14},{12,8},{14,10},{1,5},{3,7},... | collective-permute-start | bytes 208904 | tf_op jit(solution)/shard_map/ppermute | solution.py:433
  48.0 1.1 %collective-permute-start.18 = (bf16[16,2176]{1,0:T(8,128)(2,1)S(1)}, bf16[16,2176]{1,0:T(8,128)(2,1)S(1)}, u32[]{:S(2)}, u32[]{:S(2)}) collective-permute-start(bf16[16,2176]{1,0:T(8,128)(2,1)S(1)} %add_convert_fusion.a_ref), channel_id=1, source_target_pairs={{0,8},{2,10},{4,12},{6,14},{8,0},{10,2},{12,4},{14,6},{1,9},{3,11}... | collective-permute-start | bytes 208904 | tf_op jit(solution)/shard_map/ppermute | solution.py:433
  49.1 2.3 %collective-permute-start.19 = (bf16[16,2176]{1,0:T(8,128)(2,1)S(1)}, bf16[16,2176]{1,0:T(8,128)(2,1)S(1)}, u32[]{:S(2)}, u32[]{:S(2)}) collective-permute-start(bf16[16,2176]{1,0:T(8,128)(2,1)S(1)} %add_convert_fusion.a_ref), channel_id=1, source_target_pairs={{0,12},{2,14},{4,8},{6,10},{8,4},{10,6},{12,0},{14,2},{1,13},{3,15... | collective-permute-start | bytes 208904 | tf_op jit(solution)/shard_map/ppermute | solution.py:433
  51.4 0.6 %dynamic-slice_bitcast_fusion = f32[12]{0:T(128)} fusion(f32[1,128]{1,0:T(1,128)S(1)} %slice.3, s32[]{:T(128)S(6)} %select_n.16), kind=kLoop, calls=%fused_computation.2 | loop fusion | bytes 100 | tf_op jit(solution)/shard_map/dynamic_slice | solution.py:510
  52.0 0.0 collective-permute-done.17.b_ref
  52.0 4.0 %collective-permute-done.18.c_ref = bf16[16,2176]{1,0:T(8,128)(2,1)S(1)} collective-permute-done((bf16[16,2176]{1,0:T(8,128)(2,1)S(1)}, bf16[16,2176]{1,0:T(8,128)(2,1)S(1)}, u32[]{:S(2)}, u32[]{:S(2)}) %collective-permute-start.18) | collective-permute-done | bytes 69664 | tf_op jit(solution)/shard_map/ppermute | solution.py:433
  56.0 0.7 %add_four.1 = (f32[16,2048]{1,0:T(8,128)}, f32[16,128]{1,0:T(8,128)}) custom-call(bf16[16,2176]{1,0:T(8,128)(2,1)S(1)} %add_convert_fusion.a_ref, bf16[16,2176]{1,0:T(8,128)(2,1)S(1)} %collective-permute-done.17.b_ref, bf16[16,2176]{1,0:T(8,128)(2,1)S(1)} %collective-permute-done.18.c_ref, bf16[16,2176]{1,0:T(8,128)(2,1)S(1)} %collective-permute-done.19.d_ref), custom_call_target="tpu_custom_call" | custom-call | tf_op jit(solution)/shard_map/add_four/pallas_call | solution.py:415
  (13 shorter events, 0.1 us)
Async XLA Ops:
  0.6 7.4 %copy-start.3 = (s32[24,9]{0,1:T(8,128)S(1)}, s32[24,9]{0,1:T(8,128)}, u32[]{:S(2)}) copy-start(s32[24,9]{0,1:T(8,128)} %param.12) | copy-start | bytes 2596
  0.6 7.4 %copy-start.2 = (bf16[16,128]{1,0:T(8,128)(2,1)S(1)}, bf16[16,128]{1,0:T(8,128)(2,1)}, u32[]{:S(2)}) copy-start(bf16[16,128]{1,0:T(8,128)(2,1)} %refs_11_.1) | copy-start | bytes 12292
  0.7 7.4 %copy-start.4 = (s32[16]{0:T(128)S(1)}, s32[16]{0:T(128)}, u32[]{:S(2)}) copy-start(s32[16]{0:T(128)} %table_ref.1) | copy-start | bytes 196
  5.8 2.2 %collective-permute-start = (f32[640,256]{1,0:T(8,128)S(1)}, f32[640,256]{1,0:T(8,128)S(1)}, u32[]{:S(2)}, u32[]{:S(2)}) collective-permute-start(f32[640,256]{1,0:T(8,128)S(1)} %get-tuple-element.24), channel_id=1, source_target_pairs={{0,1},{1,0},{2,3},{3,2},{4,5},{5,4},{6,7},{7,6},{8,9},{9,8},{10,11... | collective-permute-start | bytes 1966088 | tf_op jit(solution)/shard_map/ppermute | solution.py:429
  8.1 33.1 %copy-start = (bf16[24,32,2048]{2,1,0:T(8,128)(2,1)S(1)}, bf16[24,32,2048]{2,1,0:T(8,128)(2,1)}, u32[]{:S(2)}) copy-start(bf16[24,32,2048]{2,1,0:T(8,128)(2,1)} %param.7) | copy-start | bytes 9437188
  8.1 33.1 %copy-start.1 = (bf16[2,256,2048]{2,1,0:T(8,128)(2,1)S(1)}, bf16[2,256,2048]{2,1,0:T(8,128)(2,1)}, u32[]{:S(2)}) copy-start(bf16[2,256,2048]{2,1,0:T(8,128)(2,1)} %param.8) | copy-start | bytes 6291460
  9.1 8.0 %collective-permute-start.1 = (bf16[1,288,128]{2,1,0:T(8,128)(2,1)S(1)}, bf16[1,288,128]{2,1,0:T(8,128)(2,1)S(1)}, u32[]{:S(2)}, u32[]{:S(2)}) collective-permute-start(bf16[1,288,128]{2,1,0:T(8,128)(2,1)S(1)} %bitcast.15), channel_id=1, source_target_pairs={{0,12},{2,14},{4,8},{6,10},{8,4},{10,6},{12,0},{14,2},{1,13},{3,15... | collective-permute-start | bytes 221192 | tf_op jit(solution)/shard_map/ppermute | solution.py:433
  14.1 6.5 %collective-permute-start.2 = (bf16[1,288,128]{2,1,0:T(8,128)(2,1)S(1)}, bf16[1,288,128]{2,1,0:T(8,128)(2,1)S(1)}, u32[]{:S(2)}, u32[]{:S(2)}) collective-permute-start(bf16[1,288,128]{2,1,0:T(8,128)(2,1)S(1)} %bitcast.16), channel_id=1, source_target_pairs={{0,8},{2,10},{4,12},{6,14},{8,0},{10,2},{12,4},{14,6},{1,9},{3,11}... | collective-permute-start | bytes 221192 | tf_op jit(solution)/shard_map/ppermute | solution.py:433
  14.1 6.5 %collective-permute-start.3 = (bf16[1,288,128]{2,1,0:T(8,128)(2,1)S(1)}, bf16[1,288,128]{2,1,0:T(8,128)(2,1)S(1)}, u32[]{:S(2)}, u32[]{:S(2)}) collective-permute-start(bf16[1,288,128]{2,1,0:T(8,128)(2,1)S(1)} %bitcast.17), channel_id=1, source_target_pairs={{0,4},{2,6},{4,0},{6,2},{8,12},{10,14},{12,8},{14,10},{1,5},{3,7},... | collective-permute-start | bytes 221192 | tf_op jit(solution)/shard_map/ppermute | solution.py:433
  14.7 6.4 %collective-permute-start.8 = (bf16[448,128]{1,0:T(8,128)(2,1)S(1)}, bf16[448,128]{1,0:T(8,128)(2,1)S(1)}, u32[]{:S(2)}, u32[]{:S(2)}) collective-permute-start(bf16[448,128]{1,0:T(8,128)(2,1)S(1)} %get-tuple-element.26.refs_9_), channel_id=1, source_target_pairs={{0,2},{2,0},{4,6},{6,4},{8,10},{10,8},{12,14},{14,12},{1,3},{3,1},... | collective-permute-start | bytes 344072 | tf_op jit(solution)/shard_map/ppermute | solution.py:433
  16.4 4.7 %collective-permute-start.4 = (bf16[1,288,128]{2,1,0:T(8,128)(2,1)S(1)}, bf16[1,288,128]{2,1,0:T(8,128)(2,1)S(1)}, u32[]{:S(2)}, u32[]{:S(2)}) collective-permute-start(bf16[1,288,128]{2,1,0:T(8,128)(2,1)S(1)} %bitcast.18), channel_id=1, source_target_pairs={{0,1},{1,0},{2,3},{3,2},{4,5},{5,4},{6,7},{7,6},{8,9},{9,8},{10,11... | collective-permute-start | bytes 221192 | tf_op jit(solution)/shard_map/ppermute | solution.py:429
  17.1 4.1 %collective-permute-start.5 = (bf16[1,288,128]{2,1,0:T(8,128)(2,1)S(1)}, bf16[1,288,128]{2,1,0:T(8,128)(2,1)S(1)}, u32[]{:S(2)}, u32[]{:S(2)}) collective-permute-start(bf16[1,288,128]{2,1,0:T(8,128)(2,1)S(1)} %collective-permute-done.1.refs_1_), channel_id=1, source_target_pairs={{0,1},{1,0},{2,3},{3,2},{4,5},{5,4},{6,7},{7,6},{8,9},{9,8},{10,11... | collective-permute-start | bytes 221192 | tf_op jit(solution)/shard_map/ppermute | solution.py:429
  20.6 1.3 %collective-permute-start.6 = (bf16[1,288,128]{2,1,0:T(8,128)(2,1)S(1)}, bf16[1,288,128]{2,1,0:T(8,128)(2,1)S(1)}, u32[]{:S(2)}, u32[]{:S(2)}) collective-permute-start(bf16[1,288,128]{2,1,0:T(8,128)(2,1)S(1)} %collective-permute-done.2.refs_2_), channel_id=1, source_target_pairs={{0,1},{1,0},{2,3},{3,2},{4,5},{5,4},{6,7},{7,6},{8,9},{9,8},{10,11... | collective-permute-start | bytes 221192 | tf_op jit(solution)/shard_map/ppermute | solution.py:429
  20.6 1.4 %collective-permute-start.7 = (bf16[1,288,128]{2,1,0:T(8,128)(2,1)S(1)}, bf16[1,288,128]{2,1,0:T(8,128)(2,1)S(1)}, u32[]{:S(2)}, u32[]{:S(2)}) collective-permute-start(bf16[1,288,128]{2,1,0:T(8,128)(2,1)S(1)} %collective-permute-done.3.refs_3_), channel_id=1, source_target_pairs={{0,1},{1,0},{2,3},{3,2},{4,5},{5,4},{6,7},{7,6},{8,9},{9,8},{10,11... | collective-permute-start | bytes 221192 | tf_op jit(solution)/shard_map/ppermute | solution.py:429
  23.9 3.7 %collective-permute-start.9 = (f32[8,128]{1,0:T(8,128)S(1)}, f32[8,128]{1,0:T(8,128)S(1)}, u32[]{:S(2)}, u32[]{:S(2)}) collective-permute-start(f32[8,128]{1,0:T(8,128)S(1)} %get-tuple-element.29.refs_14_), channel_id=1, source_target_pairs={{0,2},{2,0},{4,6},{6,4},{8,10},{10,8},{12,14},{14,12},{1,3},{3,1},... | collective-permute-start | bytes 12296 | tf_op jit(solution)/shard_map/ppermute | solution.py:433
  31.0 8.7 %collective-permute-start.13 = (f32[16,384]{1,0:T(8,128)S(1)}, f32[16,384]{1,0:T(8,128)S(1)}, u32[]{:S(2)}, u32[]{:S(2)}) collective-permute-start(f32[16,384]{1,0:T(8,128)S(1)} %get-tuple-element.38), channel_id=1, source_target_pairs={{0,2},{2,0},{4,6},{6,4},{8,10},{10,8},{12,14},{14,12},{1,3},{3,1},... | collective-permute-start | bytes 73736 | tf_op jit(solution)/shard_map/ppermute | solution.py:433
  32.6 5.5 %collective-permute-start.10 = (bf16[2,16,256]{2,1,0:T(8,128)(2,1)S(1)}, bf16[2,16,256]{2,1,0:T(8,128)(2,1)S(1)}, u32[]{:S(2)}, u32[]{:S(2)}) collective-permute-start(bf16[2,16,256]{2,1,0:T(8,128)(2,1)S(1)} %get-tuple-element.34), channel_id=1, source_target_pairs={{0,12},{2,14},{4,8},{6,10},{8,4},{10,6},{12,0},{14,2},{1,13},{3,15... | collective-permute-start | bytes 49160 | tf_op jit(solution)/shard_map/ppermute | solution.py:433
  35.1 4.6 %collective-permute-start.11 = (bf16[2,16,256]{2,1,0:T(8,128)(2,1)S(1)}, bf16[2,16,256]{2,1,0:T(8,128)(2,1)S(1)}, u32[]{:S(2)}, u32[]{:S(2)}) collective-permute-start(bf16[2,16,256]{2,1,0:T(8,128)(2,1)S(1)} %get-tuple-element.35), channel_id=1, source_target_pairs={{0,8},{2,10},{4,12},{6,14},{8,0},{10,2},{12,4},{14,6},{1,9},{3,11}... | collective-permute-start | bytes 49160 | tf_op jit(solution)/shard_map/ppermute | solution.py:433
  35.1 4.6 %collective-permute-start.12 = (bf16[2,16,256]{2,1,0:T(8,128)(2,1)S(1)}, bf16[2,16,256]{2,1,0:T(8,128)(2,1)S(1)}, u32[]{:S(2)}, u32[]{:S(2)}) collective-permute-start(bf16[2,16,256]{2,1,0:T(8,128)(2,1)S(1)} %get-tuple-element.36), channel_id=1, source_target_pairs={{0,4},{2,6},{4,0},{6,2},{8,12},{10,14},{12,8},{14,10},{1,5},{3,7},... | collective-permute-start | bytes 49160 | tf_op jit(solution)/shard_map/ppermute | solution.py:433
  39.7 1.4 %collective-permute-start.14 = (f32[16,1024]{1,0:T(8,128)S(1)}, f32[16,1024]{1,0:T(8,128)S(1)}, u32[]{:S(2)}, u32[]{:S(2)}) collective-permute-start(f32[16,1024]{1,0:T(8,128)S(1)} %collect.1.mine_ref), channel_id=1, source_target_pairs={{0,1},{1,0},{2,3},{3,2},{4,5},{5,4},{6,7},{7,6},{8,9},{9,8},{10,11... | collective-permute-start | bytes 196616 | tf_op jit(solution)/shard_map/ppermute | solution.py:429
  39.8 1.3 %collective-permute-start.15 = (f32[8,640]{1,0:T(8,128)S(1)}, f32[8,640]{1,0:T(8,128)S(1)}, u32[]{:S(2)}, u32[]{:S(2)}) collective-permute-start(f32[8,640]{1,0:T(8,128)S(1)} %get-tuple-element.39.refs_6_.r_mine_ref), channel_id=1, source_target_pairs={{0,1},{1,0},{2,3},{3,2},{4,5},{5,4},{6,7},{7,6},{8,9},{9,8},{10,11... | collective-permute-start | bytes 61448 | tf_op jit(solution)/shard_map/ppermute | solution.py:429
  42.5 4.4 %collective-permute-start.16 = (bf16[16,2176]{1,0:T(8,128)(2,1)S(1)}, bf16[16,2176]{1,0:T(8,128)(2,1)S(1)}, u32[]{:S(2)}, u32[]{:S(2)}) collective-permute-start(bf16[16,2176]{1,0:T(8,128)(2,1)S(1)} %grad_all.1), channel_id=1, source_target_pairs={{0,2},{2,0},{4,6},{6,4},{8,10},{10,8},{12,14},{14,12},{1,3},{3,1},... | collective-permute-start | bytes 208904 | tf_op jit(solution)/shard_map/ppermute | solution.py:433
  46.9 5.1 %collective-permute-start.17 = (bf16[16,2176]{1,0:T(8,128)(2,1)S(1)}, bf16[16,2176]{1,0:T(8,128)(2,1)S(1)}, u32[]{:S(2)}, u32[]{:S(2)}) collective-permute-start(bf16[16,2176]{1,0:T(8,128)(2,1)S(1)} %add_convert_fusion.a_ref), channel_id=1, source_target_pairs={{0,4},{2,6},{4,0},{6,2},{8,12},{10,14},{12,8},{14,10},{1,5},{3,7},... | collective-permute-start | bytes 208904 | tf_op jit(solution)/shard_map/ppermute | solution.py:433
  48.0 8.0 %collective-permute-start.18 = (bf16[16,2176]{1,0:T(8,128)(2,1)S(1)}, bf16[16,2176]{1,0:T(8,128)(2,1)S(1)}, u32[]{:S(2)}, u32[]{:S(2)}) collective-permute-start(bf16[16,2176]{1,0:T(8,128)(2,1)S(1)} %add_convert_fusion.a_ref), channel_id=1, source_target_pairs={{0,8},{2,10},{4,12},{6,14},{8,0},{10,2},{12,4},{14,6},{1,9},{3,11}... | collective-permute-start | bytes 208904 | tf_op jit(solution)/shard_map/ppermute | solution.py:433
  49.1 6.9 %collective-permute-start.19 = (bf16[16,2176]{1,0:T(8,128)(2,1)S(1)}, bf16[16,2176]{1,0:T(8,128)(2,1)S(1)}, u32[]{:S(2)}, u32[]{:S(2)}) collective-permute-start(bf16[16,2176]{1,0:T(8,128)(2,1)S(1)} %add_convert_fusion.a_ref), channel_id=1, source_target_pairs={{0,12},{2,14},{4,8},{6,10},{8,4},{10,6},{12,0},{14,2},{1,13},{3,15... | collective-permute-start | bytes 208904 | tf_op jit(solution)/shard_map/ppermute | solution.py:433

commit v3 on v2

--- a/solution.py
+++ b/solution.py
@@ -20,6 +20,12 @@
 HBM = pl.BlockSpec(memory_space=pltpu.HBM)
 
 
+def cost(microseconds):
+    return pl.CostEstimate(
+        flops=int(microseconds * 1.1e9), bytes_accessed=int(microseconds * 3.5e6), transcendentals=0
+    )
+
+
 def dot(a, b, contract, precision=None):
     return lax.dot_general(
         a, b, ((contract[0], contract[1]), ((), ())), precision=precision, preferred_element_type=f32
@@ -31,86 +37,131 @@
 TN = ((0,), (0,))
 
 
-def project_kernel(info_ref, p_hbm, q_hbm, proj_hbm, down_hbm, send_ref, keep_ref, x_ref, weight_ref, down_ref, sems):
+def put_projection(out_ref, projected, rank):
+    tokens = projected.shape[0]
+    out_ref[:tokens, :] = projected[:, :LANES]
+    low = jnp.transpose(projected[:, LANES:])[:rank, :]
+    for t in range(tokens // LANES):
+        out_ref[tokens + t * rank : tokens + (t + 1) * rank, :] = low[:, t * LANES : (t + 1) * LANES]
+
+
+def project_passages_kernel(
+    info_ref, p_hbm, q_hbm, proj_hbm, down_hbm, send_ref, keep_ref, q_ref, weight_ref, p_ref, down_ref, sems
+):
     core = info_ref[2]
+    half = p_hbm.shape[0] // 2
     weights = [
         pltpu.make_async_copy(down_hbm, down_ref, sems.at[0]),
         pltpu.make_async_copy(proj_hbm, weight_ref.at[:, :LANES], sems.at[1]),
     ]
     loads = []
-    for i, (owner, out) in enumerate(((1 - core, send_ref), (core, keep_ref))):
-        at = 0
-        for j, source in enumerate((p_hbm, q_hbm)):
-            half = source.shape[0] // 2
-            rows = pl.ds(pl.multiple_of(owner * half, LANES), half)
-            to = slice(at, at + half)
-            copy = pltpu.make_async_copy(source.at[rows, :], x_ref.at[i, to, :], sems.at[2 + 2 * i + j])
-            loads.append((copy, out, i, to))
-            at += half
-    for copy in weights:
-        copy.start()
-    for copy, _, _, _ in loads[:2]:
+    for i, owner in enumerate((1 - core, core)):
+        rows = pl.ds(pl.multiple_of(owner * half, LANES), half)
+        loads.append(pltpu.make_async_copy(p_hbm.at[rows, :], p_ref.at[i], sems.at[2 + i]))
+    queries = pltpu.make_async_copy(q_hbm, q_ref, sems.at[4])
+    for copy in weights + loads:
         copy.start()
     weights[0].wait()
     rank, width = down_ref.shape
     low = jnp.concatenate([down_ref[...].astype(f32), jnp.zeros((LANES - rank, width), f32)], axis=0)
     weight_ref[:, LANES:] = jnp.transpose(low).astype(bf16)
     weights[1].wait()
-    for copy, _, _, _ in loads[2:]:
-        copy.start()
-    for copy, out, i, to in loads:
-        copy.wait()
-        out[to, :] = dot(x_ref[i, to, :], weight_ref[...], NN)
-
-
-def project(info, passage_rows, query_rows, projection, down):
-    half, width = (passage_rows.shape[0] + query_rows.shape[0]) // 2, query_rows.shape[1]
+    queries.start()
+    for i, out in enumerate((send_ref, keep_ref)):
+        loads[i].wait()
+        put_projection(out, dot(p_ref[i], weight_ref[...], NN), rank)
+    queries.wait()
+
+
+def project_passages(info, passage_rows, query_rows, projection, down):
+    half, width = passage_rows.shape[0] // 2, passage_rows.shape[1]
     rank = down.shape[0]
-    shape = jax.ShapeDtypeStruct((half, 2 * LANES), f32)
+    shape = jax.ShapeDtypeStruct((half + half // LANES * rank, LANES), f32)
     operands = (passage_rows, query_rows, projection, down)
     operands = [pltpu.with_memory_space_constraint(x, pltpu.HBM) for x in operands]
     return pl.pallas_call(
-        project_kernel,
+        project_passages_kernel,
         in_specs=[SMEM] + [HBM] * 4,
+        out_specs=[VMEM] * 4,
+        out_shape=(
+            shape,
+            shape,
+            pltpu.VMEM(query_rows.shape, bf16),
+            pltpu.VMEM((width, 2 * LANES), bf16),
+        ),
+        scratch_shapes=[
+            pltpu.VMEM((2, half, width), bf16),
+            pltpu.VMEM((rank, width), bf16),
+            pltpu.SemaphoreType.DMA((5,)),
+        ],
+        compiler_params=pltpu.CompilerParams(vmem_limit_bytes=8 * 2**20),
+        cost_estimate=cost(3.7),
+        name="project_passages",
+    )(info, *operands)
+
+
+def project_queries_kernel(rank, info_ref, q_ref, weight_ref, send_ref, keep_ref):
+    half = q_ref.shape[0] // 2
+    for owner, out in ((1 - info_ref[2], send_ref), (info_ref[2], keep_ref)):
+        rows = pl.ds(pl.multiple_of(owner * half, LANES), half)
+        put_projection(out, dot(q_ref[rows, :], weight_ref[...], NN), rank)
+
+
+def project_queries(info, query_rows, weight, rank):
+    half = query_rows.shape[0] // 2
+    shape = jax.ShapeDtypeStruct((half + half // LANES * rank, LANES), f32)
+    return pl.pallas_call(
+        functools.partial(project_queries_kernel, rank),
+        in_specs=[SMEM] + [VMEM] * 2,
         out_specs=[VMEM] * 2,
         out_shape=(shape, shape),
-        scratch_shapes=[
-            pltpu.VMEM((2, half, width), bf16),
-            pltpu.VMEM((width, 2 * LANES), bf16),
-            pltpu.VMEM((rank, width), bf16),
-            pltpu.SemaphoreType.DMA((6,)),
-        ],
-        compiler_params=pltpu.CompilerParams(vmem_limit_bytes=12 * 2**20),
-        name="project",
-    )(info, *operands)
-
-
-def finish(keep, recv, up):
-    rank = up.shape[0]
-    low_bf = (keep[:, LANES : LANES + rank] + recv[:, LANES : LANES + rank]).astype(bf16)
-    full = keep[:, :LANES] + recv[:, :LANES] + dot(low_bf, up, NN)
-    r = lax.rsqrt(jnp.sum(full * full, axis=1, keepdims=True) + norm_eps)
-    return low_bf, full * r, r
+        compiler_params=pltpu.CompilerParams(vmem_limit_bytes=4 * 2**20),
+        cost_estimate=cost(1.5),
+        name="project_queries",
+    )(info, query_rows, weight)
 
 
 def pad_lanes(x):
     return jnp.concatenate([x, jnp.zeros((x.shape[0], LANES - x.shape[1]), x.dtype)], axis=1)
 
 
-def pack_kernel(sizes, info_ref, table_ref, ids_ref, keep_ref, recv_ref, up_ref, p_ref, q_ref, r_ref):
-    up = up_ref[...]
+def pack_rows(keep_ref, recv_ref, up, out_ref, r_ref):
+    rank, tokens = up.shape[0], r_ref.shape[1]
+    for t in range(tokens // LANES):
+        block = slice(t * LANES, (t + 1) * LANES)
+        rows = slice(tokens + t * rank, tokens + (t + 1) * rank)
+        low = (keep_ref[rows, :] + recv_ref[rows, :]).astype(bf16)
+        full = keep_ref[block, :] + recv_ref[block, :] + dot(low, up, TN)
+        r = lax.rsqrt(jnp.sum(full * full, axis=1, keepdims=True) + norm_eps)
+        out_ref[block, :] = (full * r).astype(bf16)
+        r = jnp.transpose(jnp.broadcast_to(r, (LANES, LANES)))
+        out_ref[rows, :] = (low.astype(f32) * r[:rank, :]).astype(bf16)
+        r_ref[:, block] = r[:8, :]
+
+
+def pack_passage_kernel(keep_ref, recv_ref, up_ref, out_ref, r_ref):
+    pack_rows(keep_ref, recv_ref, up_ref[...], out_ref, r_ref)
+
+
+def pack_passage(keep, recv, up):
     rank = up.shape[0]
-    low_bf, vn, r = finish(keep_ref[...], recv_ref[...], up)
-    scaled = jnp.transpose(pad_lanes(low_bf.astype(f32) * r))[:rank, :].astype(bf16)
-    vn = vn.astype(bf16)
-    start = 0
-    for ref, tokens in zip((p_ref, q_ref), sizes, strict=True):
-        ref[:tokens, :] = vn[start : start + tokens, :]
-        for t in range(tokens // LANES):
-            at = start + t * LANES
-            ref[tokens + t * rank : tokens + (t + 1) * rank, :] = scaled[:, at : at + LANES]
-        start += tokens
-    r_ref[...] = jnp.transpose(jnp.broadcast_to(r, (start, LANES)))[:8, :]
+    tokens = keep.shape[0] // (LANES + rank) * LANES
+    return pl.pallas_call(
+        pack_passage_kernel,
+        in_specs=[VMEM] * 3,
+        out_specs=[VMEM] * 2,
+        out_shape=(
+            jax.ShapeDtypeStruct((tokens + tokens // LANES * rank, LANES), bf16),
+            jax.ShapeDtypeStruct((8, tokens), f32),
+        ),
+        compiler_params=pltpu.CompilerParams(vmem_limit_bytes=4 * 2**20),
+        cost_estimate=cost(6),
+        name="pack_passage",
+    )(keep, recv, up)
+
+
+def pack_queries_kernel(info_ref, table_ref, ids_ref, keep_ref, recv_ref, up_ref, out_ref, r_ref):
+    pack_rows(keep_ref, recv_ref, up_ref[...], out_ref, r_ref)
     ids = ids_ref[...]
     cands, qdev = ids.shape
     n_ids = table_ref.shape[0]
@@ -128,22 +179,23 @@
     wide = pltpu.roll(wide, lax.rem(place - info_ref[2] * half + LANES, LANES), 1)
     lane = lax.broadcasted_iota(jnp.int32, wide.shape, 1)
     wide = jnp.where((lane >= place) & (lane < place + half), wide, -1.0)
-    q_ref[q_ref.shape[0] - 16 :, :] = wide.astype(bf16)
-
-
-def pack_tokens(info, table, ids, keep, recv, up, ptok, qtok):
+    out_ref[out_ref.shape[0] - 16 :, :] = wide.astype(bf16)
+
+
+def pack_queries(info, table, ids, keep, recv, up):
     rank = up.shape[0]
-    return pl.pallas_call(
-        functools.partial(pack_kernel, (ptok, qtok)),
+    tokens = keep.shape[0] // (LANES + rank) * LANES
+    return pl.pallas_call(
+        pack_queries_kernel,
         in_specs=[SMEM] * 2 + [VMEM] * 4,
-        out_specs=[VMEM] * 3,
+        out_specs=[VMEM] * 2,
         out_shape=(
-            jax.ShapeDtypeStruct((ptok + ptok // LANES * rank, LANES), bf16),
-            jax.ShapeDtypeStruct((qtok + qtok // LANES * rank + 16, LANES), bf16),
-            jax.ShapeDtypeStruct((8, ptok + qtok), f32),
+            jax.ShapeDtypeStruct((tokens + tokens // LANES * rank + 16, LANES), bf16),
+            jax.ShapeDtypeStruct((8, tokens), f32),
         ),
-        compiler_params=pltpu.CompilerParams(vmem_limit_bytes=8 * 2**20),
-        name="pack_tokens",
+        compiler_params=pltpu.CompilerParams(vmem_limit_bytes=4 * 2**20),
+        cost_estimate=cost(0.9),
+        name="pack_queries",
     )(info, table, ids, keep, recv, up)
 
 
@@ -247,13 +299,12 @@
         for pos in range(n_packs):
             rows = slice(pos * plen, (pos + 1) * plen)
             grad_ref[rows, :] = (expo_ref[pos].astype(f32) * scale_ref[pos : pos + 1, :]).astype(bf16)
-        dv_ref[...] = dot(grad_ref[...], vq, NN)
+            dv_ref[rows, :] = dot(grad_ref[rows, :], vq, NN)
+            dvqt = dot(packs[pos][0, :plen, :], grad_ref[rows, :], TN)
+            dvqt_ref[...] = dvqt if pos == 0 else dvqt_ref[...] + dvqt
         for pos, pack in enumerate(packs):
             rows = slice(pos * plen, (pos + 1) * plen)
-            vp = pack[0, :plen, :]
-            dvqt = dot(vp, grad_ref[rows, :], TN)
-            dvqt_ref[...] = dvqt if pos == 0 else dvqt_ref[...] + dvqt
-            dv = project_out(vp, dv_ref[rows, :])
+            dv = project_out(pack[0, :plen, :], dv_ref[rows, :])
             dvb_ref[rows, :] = dv
             part_refs[pos % n_parts][where(info_ref, pos)[1]] = dot(up, dv, NT).astype(bf16)
         lows = jnp.concatenate([scaled_low(pack, 0) for pack in packs], axis=1)
@@ -279,7 +330,7 @@
     dvqt = (dvqt - vqt * jnp.sum(vqt * dvqt, axis=0, keepdims=True)).astype(bf16)
     dlow = dot(up, dvqt, NN)
     dmine_ref[...] = jnp.where(lo == 0, dlow[:, :qtok], dlow[:, qtok:])
-    dother_ref[...] = jnp.where(lo == 0, dlow[:, qtok:], dlow[:, :qtok])
+    dother_ref[...] = jnp.where(lo == 0, dlow[:, qtok:], dlow[:, :qtok]).astype(bf16)
     lows = [
         both_queries(lo, mine_ref, other_ref, slice(at, at + rank))
         for at in range(qtok, qtok + qtok // LANES * rank, rank)
@@ -314,6 +365,7 @@
             jax.ShapeDtypeStruct((LANES, 2 * qtok), bf16),
         ),
         compiler_params=pltpu.CompilerParams(vmem_limit_bytes=(16 if store else 40) * 2**20),
+        cost_estimate=cost(1.9),
         name="score_forward",
     )(*packs, info, mine, other)
 
@@ -333,7 +385,7 @@
         out_shape=(
             *parts,
             jax.ShapeDtypeStruct((rank, qtok), f32),
-            jax.ShapeDtypeStruct((rank, qtok), f32),
+            jax.ShapeDtypeStruct((rank, qtok), bf16),
             jax.ShapeDtypeStruct((rank, LANES), f32),
             jax.ShapeDtypeStruct((8, LANES), f32),
         ),
@@ -345,6 +397,7 @@
             pltpu.VMEM((kept, LANES), bf16),
         ],
         compiler_params=pltpu.CompilerParams(vmem_limit_bytes=(20 if store else 40) * 2**20),
+        cost_estimate=cost(2.5),
         name="score_backward",
     )(*packs, info, mine, other, up, stats, total, sums, recv, expo, vqt)
 
@@ -355,7 +408,7 @@
     qtok = mine_ref.shape[1]
     for i in range(2):
         out_ref[:, i * plen : (i + 1) * plen] = sum(part[i].astype(f32) for part in parts)
-    out_ref[:, 2 * plen : 2 * plen + qtok] = (mine_ref[...] + recv_ref[...]) * r_ref[:1, plen:]
+    out_ref[:, 2 * plen : 2 * plen + qtok] = (mine_ref[...] + recv_ref[...].astype(f32)) * r_ref[:1, :]
     out_ref[:, 2 * plen + qtok :] = up_ref[...]
 
 
@@ -368,6 +421,7 @@
         out_specs=VMEM,
         out_shape=jax.ShapeDtypeStruct((rank, 2 * plen + qtok + LANES), f32),
         compiler_params=pltpu.CompilerParams(vmem_limit_bytes=4 * 2**20),
+        cost_estimate=cost(0.3),
         name="collect",
     )(*parts, mine, recv, r, up)
 
@@ -397,13 +451,14 @@
         out_specs=VMEM,
         out_shape=jax.ShapeDtypeStruct((rank, width + LANES), bf16),
         compiler_params=pltpu.CompilerParams(vmem_limit_bytes=4 * 2**20),
+        cost_estimate=cost(1.3),
         name="grad_all",
     )(info, passage_rows, query_rows, mine, other, r_mine, r_other)
 
 
 def add_kernel(a_ref, b_ref, c_ref, d_ref, down_ref, up_ref):
-    total = (a_ref[...].astype(f32) + b_ref[...].astype(f32)) + (
-        c_ref[...].astype(f32) + d_ref[...].astype(f32)
+    total = (a_ref[...].astype(f32) + d_ref[...].astype(f32)) + (
+        b_ref[...].astype(f32) + c_ref[...].astype(f32)
     )
     width = down_ref.shape[1]
     down_ref[...] = total[:, :width]
@@ -421,6 +476,7 @@
             jax.ShapeDtypeStruct((rank, LANES), f32),
         ),
         compiler_params=pltpu.CompilerParams(vmem_limit_bytes=4 * 2**20),
+        cost_estimate=cost(0.7),
         name="add_four",
     )(*parts)
 
@@ -454,7 +510,7 @@
         x = lax.psum(x.astype(f32), "shard")
         return x[:, :width], x[:, width:]
     x = (x.astype(f32) + across(x, nshard, 1).astype(f32)).astype(bf16)
-    return add_four([x] + [across(x, nshard, k) for k in (2, 4, 6)], width)
+    return add_four([x] + [across(x, nshard, k) for k in (6, 4, 2)], width)
 
 
 def per_device(
@@ -478,13 +534,17 @@
     query_rows = query_hidden_states.reshape(qdev * qlen, width)
     passage_rows = passage_hidden_states.reshape(pdev * plen, width)
 
-    send, keep = project(info, passage_rows, query_rows, projection_matrix, jnp.transpose(adapter_down_weight))
-    ppack, mine, r = pack_tokens(
-        info, passage_row_table, jnp.transpose(passage_pair_index), keep, swap(send), adapter_up_weight, plen, qtok
+    send_p, keep_p, query_vmem, weight = project_passages(
+        info, passage_rows, query_rows, projection_matrix, jnp.transpose(adapter_down_weight)
+    )
+    send_q, keep_q = project_queries(info, query_vmem, weight, adapter_up_weight.shape[0])
+    ppack, r_p = pack_passage(keep_p, swap(send_p), adapter_up_weight)
+    mine, r_q = pack_queries(
+        info, passage_row_table, jnp.transpose(passage_pair_index), keep_q, swap(send_q), adapter_up_weight
     )
     other = across(mine, nshard, 1)
     packs, steps = gather_packs(ppack, nshard, groups)
-    r_other = swap(r)
+    mine, r_other = lax.optimization_barrier((mine, swap(r_p)))
 
     stats, total, sums, expo, vqt = score_forward(packs, steps, info, mine, other, qlen, qtok, plen)
     *parts, dlow_mine, dlow_other, gup, loss = score_backward(
@@ -505,8 +565,8 @@
         plen,
     )
     parts = exchange_parts(parts, steps, nshard, groups)
-    collected = collect(parts, dlow_mine, across(dlow_other, nshard, 1), r, gup)
-    grads = grad_all(info, passage_rows, query_rows, collected, swap(collected), r, r_other, plen, qtok)
+    collected = collect(parts, dlow_mine, across(dlow_other, nshard, 1), r_q, gup)
+    grads = grad_all(info, passage_rows, query_rows, collected, swap(collected), r_p, r_other, plen, qtok)
     query_loss = lax.dynamic_slice_in_dim(loss[0], info[0] * half, half, 0)
     down_sum, up_sum = sum_over_shards(grads, nshard, width)
     return (query_loss, jnp.transpose(down_sum), up_sum)

time: 56.8 us -> 52.5 us (0.924)
  waiting for transfers between devices: 20.5 us -> 15.4 us
  starting transfers between devices: 21.4 us -> 22.6 us
    ppermute x13, waiting for transfers between devices: 17 us -> 12.1 us  [across(): return lax.ppermute(x, 'shard', [(i, i ^ step) for i in range(nshard)])]
    ppermute x13, starting transfers between devices: 19.8 us -> 20.8 us  [across(): return lax.ppermute(x, 'shard', [(i, i ^ step) for i in range(nshard)])]
    pallas_call x1, Pallas kernels: 3.44 us -> 2.43 us  [score_backward(): pl.pallas_call(functools.partial(backward_kernel, cfg), in_specs=[VMEM] *...]
    pallas_call x2 -> x4, Pallas kernels: 6.03 us -> 6.57 us  [the longest x1 3.71 us: project_passages(): pl.pallas_call(project_passages_kernel, in_specs=[SMEM] + [HBM] * 4, out_...]
    ppermute x7 -> x8, waiting for transfers between devices: 3.48 us -> 3.33 us  [swap(): return lax.ppermute(x, 'sub', [(0, 1), (1, 0)])]
    ppermute x7 -> x8, starting transfers between devices: 1.6 us -> 1.72 us  [swap(): return lax.ppermute(x, 'sub', [(0, 1), (1, 0)])]
  transfers between devices with their start and end apart: 20 -> 21, of which waited for: 11 -> 10; matrix products, arithmetic and copies ran while one was open for 1% -> 1% of each run, Pallas kernels for 0% -> 5%
where the time goes in v3:
time: 52.5 us; the launch traced here: 52.3 us
  starting transfers between devices  22.6 us (43%)
  waiting for transfers between devices  15.4 us (29%)
  Pallas kernels  12.9 us (25%)
  between operations  0.74 us (1%)
  local copies, waits for them, and re-layouts  0.6 us (1%)
    ppermute x13, starting transfers between devices, across(): return lax.ppermute(x, 'shard', [(i, i ^ step) for i in range(nshard)])  20.8 us
    ppermute x13, waiting for transfers between devices, across(): return lax.ppermute(x, 'shard', [(i, i ^ step) for i in range(nshard)])  12.1 us
    pallas_call x1, Pallas kernels, project_passages(): pl.pallas_call(project_passages_kernel, in_specs=[SMEM] + [HBM] * 4, out_...  3.71 us
    ppermute x8, waiting for transfers between devices, swap(): return lax.ppermute(x, 'sub', [(0, 1), (1, 0)])  3.33 us
    pallas_call x1, Pallas kernels, score_backward(): pl.pallas_call(functools.partial(backward_kernel, cfg), in_specs=[VMEM] *...  2.43 us
    pallas_call x1, Pallas kernels, score_forward(): pl.pallas_call(functools.partial(forward_kernel, cfg), in_specs=[VMEM] *...  1.88 us
    ppermute x8, starting transfers between devices, swap(): return lax.ppermute(x, 'sub', [(0, 1), (1, 0)])  1.72 us
    pallas_call x1, Pallas kernels, project_queries(): pl.pallas_call(functools.partial(project_queries_kernel, rank), in_specs=...  1.56 us
  transfers between devices with their start and end apart: 21, of which 10 were waited for; matrix products, arithmetic and copies ran while one was open for 1% of the time, Pallas kernels for 5%

profile of v3, /device:TPU:0, one launch (start us, length us, event | category | flops | bytes accessed | tf_op | source)
XLA Modules:
  0.0 52.3 jit_solution(7312583331826435091)
XLA Ops:
  0.6 0.1 pad_add_fusion.info_ref.refs_8_
  0.7 3.7 %project_passages.1 = (f32[288,128]{1,0:T(8,128)S(1)}, f32[288,128]{1,0:T(8,128)S(1)}, bf16[768,2048]{1,0:T(8,128)(2,1)S(1)}, bf16[2048,256]{1,0:T(8,128)(2,1)S(1)}) custom-call(s32[3]{0:T(128)S(1)} %pad_add_fusion.info_ref.refs_8_, bf16[512,2048]{1,0:T(8,128)(2,1)} %bitcast.13, bf16[768,2048]{1,0:T(8,128)(2,1)} %bitcast.11, bf16[2048,128]{1,0:T(8,128)(2,1)} %proj_hbm.1, ...), custom_call_target="tpu_custom_call" | custom-call | flops 4070000128 | bytes 12950000 | tf_op jit(solution)/shard_map/project_passages/pallas_call | solution.py:82
  4.4 0.0 copy-start.3
  4.5 0.5 collective-permute-start
  5.0 1.6 %project_queries.1 = (f32[432,128]{1,0:T(8,128)S(1)}, f32[432,128]{1,0:T(8,128)S(1)}) custom-call(s32[3]{0:T(128)S(1)} %pad_add_fusion.info_ref.refs_8_, bf16[768,2048]{1,0:T(8,128)(2,1)S(1)} %get-tuple-element.33.q_ref, bf16[2048,256]{1,0:T(8,128)(2,1)S(1)} %get-tuple-element.34.weight_ref), custom_call_target="tpu_custom_call" | custom-call | flops 1650000000 | bytes 5250000 | tf_op jit(solution)/shard_map/project_queries/pallas_call | solution.py:113
  6.5 0.1 collective-permute-start.8
  6.6 0.0 collective-permute-done.recv_ref
  6.7 0.4 pack_passage.1
  7.0 5.1 %collective-permute-start.1 = (bf16[1,288,128]{2,1,0:T(8,128)(2,1)S(1)}, bf16[1,288,128]{2,1,0:T(8,128)(2,1)S(1)}, u32[]{:S(2)}, u32[]{:S(2)}) collective-permute-start(bf16[1,288,128]{2,1,0:T(8,128)(2,1)S(1)} %bitcast.15), channel_id=1, source_target_pairs={{0,12},{2,14},{4,8},{6,10},{8,4},{10,6},{12,0},{14,2},{1,13},{3,15... | collective-permute-start | bytes 221192 | tf_op jit(solution)/shard_map/ppermute | solution.py:489
  12.1 0.0 collective-permute-start.2
  12.1 0.6 %collective-permute-start.3 = (bf16[1,288,128]{2,1,0:T(8,128)(2,1)S(1)}, bf16[1,288,128]{2,1,0:T(8,128)(2,1)S(1)}, u32[]{:S(2)}, u32[]{:S(2)}) collective-permute-start(bf16[1,288,128]{2,1,0:T(8,128)(2,1)S(1)} %bitcast.17), channel_id=1, source_target_pairs={{0,4},{2,6},{4,0},{6,2},{8,12},{10,14},{12,8},{14,10},{1,5},{3,7},... | collective-permute-start | bytes 221192 | tf_op jit(solution)/shard_map/ppermute | solution.py:489
  12.7 0.0 collective-permute-done.8.recv_ref
  12.7 1.0 %pack_queries.1 = (bf16[448,128]{1,0:T(8,128)(2,1)S(1)}, f32[8,384]{1,0:T(8,128)S(1)}) custom-call(s32[3]{0:T(128)S(1)} %pad_add_fusion.info_ref.refs_8_, s32[16]{0:T(128)S(1)} %copy-done.4, s32[9,24]{1,0:T(8,128)S(1)} %bitcast.21, f32[432,128]{1,0:T(8,128)S(1)} %get-tuple-element.35.keep_ref, f32[432,128]{1,0:T(8,128)S(1)} %collective-permute-done.8.recv_ref, ...), custom_call_target="tpu_custom_call" | custom-call | flops 990000000 | bytes 3150000 | tf_op jit(solution)/shard_map/pack_queries/pallas_call | solution.py:188
  13.7 1.7 %collective-permute-start.10 = (bf16[448,128]{1,0:T(8,128)(2,1)S(1)}, bf16[448,128]{1,0:T(8,128)(2,1)S(1)}, u32[]{:S(2)}, u32[]{:S(2)}) collective-permute-start(bf16[448,128]{1,0:T(8,128)(2,1)S(1)} %get-tuple-element.39.refs_9_), channel_id=1, source_target_pairs={{0,2},{2,0},{4,6},{6,4},{8,10},{10,8},{12,14},{14,12},{1,3},{3,1},... | collective-permute-start | bytes 344072 | tf_op jit(solution)/shard_map/ppermute | solution.py:489
  15.4 0.0 collective-permute-start.9
  15.4 1.2 %collective-permute-done.9.r_other_ref = f32[8,256]{1,0:T(8,128)S(1)} collective-permute-done((f32[8,256]{1,0:T(8,128)S(1)}, f32[8,256]{1,0:T(8,128)S(1)}, u32[]{:S(2)}, u32[]{:S(2)}) %collective-permute-start.9) | collective-permute-done | bytes 8224 | tf_op jit(solution)/shard_map/ppermute | solution.py:485
  16.5 0.2 collective-permute-start.4
  16.7 0.0 collective-permute-done.1.refs_1_
  16.7 0.3 collective-permute-start.5
  17.1 1.5 %collective-permute-done.2.refs_2_ = bf16[1,288,128]{2,1,0:T(8,128)(2,1)S(1)} collective-permute-done((bf16[1,288,128]{2,1,0:T(8,128)(2,1)S(1)}, bf16[1,288,128]{2,1,0:T(8,128)(2,1)S(1)}, u32[]{:S(2)}, u32[]{:S(2)}) %collective-permute-start.2) | collective-permute-done | bytes 73760 | tf_op jit(solution)/shard_map/ppermute | solution.py:489
  18.5 0.0 collective-permute-start.6
  18.5 0.0 collective-permute-done.3.refs_3_
  18.5 0.5 collective-permute-start.7
  19.0 0.0 collective-permute-done.4.refs_4_
  19.0 0.0 collective-permute-done.5.refs_5_
  19.0 0.7 %collective-permute-done.6.refs_6_ = bf16[1,288,128]{2,1,0:T(8,128)(2,1)S(1)} collective-permute-done((bf16[1,288,128]{2,1,0:T(8,128)(2,1)S(1)}, bf16[1,288,128]{2,1,0:T(8,128)(2,1)S(1)}, u32[]{:S(2)}, u32[]{:S(2)}) %collective-permute-start.6) | collective-permute-done | bytes 73760 | tf_op jit(solution)/shard_map/ppermute | solution.py:485
  19.8 0.2 collective-permute-done.7.refs_7_
  20.0 1.9 %score_forward.1 = (f32[3,8,128]{2,1,0:T(8,128)S(1)}, f32[8,768]{1,0:T(8,128)S(1)}, f32[8,128]{1,0:T(8,128)S(1)}, bf16[8,256,768]{2,1,0:T(8,128)(2,1)S(1)}, bf16[128,768]{1,0:T(8,128)(2,1)S(1)}) custom-call(bf16[1,288,128]{2,1,0:T(8,128)(2,1)S(1)} %bitcast.19, bf16[1,288,128]{2,1,0:T(8,128)(2,1)S(1)} %collective-permute-done.1.refs_1_, ...), custom_call_target="tpu_custom_call" | custom-call | flops 2090000000 | bytes 6650000 | tf_op jit(solution)/shard_map/score_forward/pallas_call | solution.py:356
  21.8 1.6 %collective-permute-start.11 = (f32[8,128]{1,0:T(8,128)S(1)}, f32[8,128]{1,0:T(8,128)S(1)}, u32[]{:S(2)}, u32[]{:S(2)}) collective-permute-start(f32[8,128]{1,0:T(8,128)S(1)} %get-tuple-element.42.refs_14_), channel_id=1, source_target_pairs={{0,2},{2,0},{4,6},{6,4},{8,10},{10,8},{12,14},{14,12},{1,3},{3,1},... | collective-permute-start | bytes 12296 | tf_op jit(solution)/shard_map/ppermute | solution.py:489
  23.4 2.1 %collective-permute-done.11.refs_15_ = f32[8,128]{1,0:T(8,128)S(1)} collective-permute-done((f32[8,128]{1,0:T(8,128)S(1)}, f32[8,128]{1,0:T(8,128)S(1)}, u32[]{:S(2)}, u32[]{:S(2)}) %collective-permute-start.11) | collective-permute-done | bytes 4128 | tf_op jit(solution)/shard_map/ppermute | solution.py:489
  25.5 2.4 %score_backward.1 = (bf16[2,16,256]{2,1,0:T(8,128)(2,1)S(1)}, bf16[2,16,256]{2,1,0:T(8,128)(2,1)S(1)}, bf16[2,16,256]{2,1,0:T(8,128)(2,1)S(1)}, bf16[2,16,256]{2...) custom-call(bf16[1,288,128]{2,1,0:T(8,128)(2,1)S(1)} %bitcast.20, ...), custom_call_target="tpu_custom_call" | custom-call | flops 2750000128 | bytes 8750000 | tf_op jit(solution)/shard_map/score_backward/pallas_call | solution.py:381
  27.9 2.6 %collective-permute-start.12 = (bf16[2,16,256]{2,1,0:T(8,128)(2,1)S(1)}, bf16[2,16,256]{2,1,0:T(8,128)(2,1)S(1)}, u32[]{:S(2)}, u32[]{:S(2)}) collective-permute-start(bf16[2,16,256]{2,1,0:T(8,128)(2,1)S(1)} %get-tuple-element.47), channel_id=1, source_target_pairs={{0,12},{2,14},{4,8},{6,10},{8,4},{10,6},{12,0},{14,2},{1,13},{3,15... | collective-permute-start | bytes 49160 | tf_op jit(solution)/shard_map/ppermute | solution.py:489
  30.6 1.8 %collective-permute-start.14 = (bf16[2,16,256]{2,1,0:T(8,128)(2,1)S(1)}, bf16[2,16,256]{2,1,0:T(8,128)(2,1)S(1)}, u32[]{:S(2)}, u32[]{:S(2)}) collective-permute-start(bf16[2,16,256]{2,1,0:T(8,128)(2,1)S(1)} %get-tuple-element.49), channel_id=1, source_target_pairs={{0,4},{2,6},{4,0},{6,2},{8,12},{10,14},{12,8},{14,10},{1,5},{3,7},... | collective-permute-start | bytes 49160 | tf_op jit(solution)/shard_map/ppermute | solution.py:489
  32.4 1.5 %collective-permute-start.15 = (bf16[16,384]{1,0:T(8,128)(2,1)S(1)}, bf16[16,384]{1,0:T(8,128)(2,1)S(1)}, u32[]{:S(2)}, u32[]{:S(2)}) collective-permute-start(bf16[16,384]{1,0:T(8,128)(2,1)S(1)} %get-tuple-element.51), channel_id=1, source_target_pairs={{0,2},{2,0},{4,6},{6,4},{8,10},{10,8},{12,14},{14,12},{1,3},{3,1},... | collective-permute-start | bytes 36872 | tf_op jit(solution)/shard_map/ppermute | solution.py:489
  33.9 2.2 %collective-permute-done.15.refs_5_ = bf16[16,384]{1,0:T(8,128)(2,1)S(1)} collective-permute-done((bf16[16,384]{1,0:T(8,128)(2,1)S(1)}, bf16[16,384]{1,0:T(8,128)(2,1)S(1)}, u32[]{:S(2)}, u32[]{:S(2)}) %collective-permute-start.15) | collective-permute-done | bytes 12320 | tf_op jit(solution)/shard_map/ppermute | solution.py:489
  36.1 0.1 collective-permute-start.16
  36.2 1.2 %collective-permute-done.16.other_ref = f32[16,1024]{1,0:T(8,128)S(1)} collective-permute-done((f32[16,1024]{1,0:T(8,128)S(1)}, f32[16,1024]{1,0:T(8,128)S(1)}, u32[]{:S(2)}, u32[]{:S(2)}) %collective-permute-start.16) | collective-permute-done | bytes 65568 | tf_op jit(solution)/shard_map/ppermute | solution.py:485
  37.5 1.3 %grad_all.1 = bf16[16,2176]{1,0:T(8,128)(2,1)S(1)} custom-call(s32[3]{0:T(128)S(1)} %pad_add_fusion.info_ref.refs_8_, bf16[512,2048]{1,0:T(8,128)(2,1)S(1)} %bitcast.14, bf16[768,2048]{1,0:T(8,128)(2,1)S(1)} %bitcast.12, f32[16,1024]{1,0:T(8,128)S(1)} %collect.1.mine_ref, f32[16,1024]{1,0:T(8,128)S(1)} %collective-permute-done.16.other_ref, ...), custom_call_target="tpu_custom_call" | custom-call | flops 1430000000 | bytes 4550000 | tf_op jit(solution)/shard_map/grad_all/pallas_call | solution.py:448
  38.8 1.5 %collective-permute-start.17 = (bf16[16,2176]{1,0:T(8,128)(2,1)S(1)}, bf16[16,2176]{1,0:T(8,128)(2,1)S(1)}, u32[]{:S(2)}, u32[]{:S(2)}) collective-permute-start(bf16[16,2176]{1,0:T(8,128)(2,1)S(1)} %grad_all.1), channel_id=1, source_target_pairs={{0,2},{2,0},{4,6},{6,4},{8,10},{10,8},{12,14},{14,12},{1,3},{3,1},... | collective-permute-start | bytes 208904 | tf_op jit(solution)/shard_map/ppermute | solution.py:489
  40.3 2.8 %collective-permute-done.17 = bf16[16,2176]{1,0:T(8,128)(2,1)S(1)} collective-permute-done((bf16[16,2176]{1,0:T(8,128)(2,1)S(1)}, bf16[16,2176]{1,0:T(8,128)(2,1)S(1)}, u32[]{:S(2)}, u32[]{:S(2)}) %collective-permute-start.17) | collective-permute-done | bytes 69664 | tf_op jit(solution)/shard_map/ppermute | solution.py:489
  43.1 2.6 %collective-permute-start.18 = (bf16[16,2176]{1,0:T(8,128)(2,1)S(1)}, bf16[16,2176]{1,0:T(8,128)(2,1)S(1)}, u32[]{:S(2)}, u32[]{:S(2)}) collective-permute-start(bf16[16,2176]{1,0:T(8,128)(2,1)S(1)} %add_convert_fusion.a_ref), channel_id=1, source_target_pairs={{0,12},{2,14},{4,8},{6,10},{8,4},{10,6},{12,0},{14,2},{1,13},{3,15... | collective-permute-start | bytes 208904 | tf_op jit(solution)/shard_map/ppermute | solution.py:489
  45.7 0.0 collective-permute-start.19
  45.8 1.8 %collective-permute-start.20 = (bf16[16,2176]{1,0:T(8,128)(2,1)S(1)}, bf16[16,2176]{1,0:T(8,128)(2,1)S(1)}, u32[]{:S(2)}, u32[]{:S(2)}) collective-permute-start(bf16[16,2176]{1,0:T(8,128)(2,1)S(1)} %add_convert_fusion.a_ref), channel_id=1, source_target_pairs={{0,4},{2,6},{4,0},{6,2},{8,12},{10,14},{12,8},{14,10},{1,5},{3,7},... | collective-permute-start | bytes 208904 | tf_op jit(solution)/shard_map/ppermute | solution.py:489
  47.6 0.6 %dynamic-slice_bitcast_fusion = f32[12]{0:T(128)} fusion(f32[1,128]{1,0:T(1,128)S(1)} %slice.3, s32[]{:T(128)S(6)} %select_n.16), kind=kLoop, calls=%fused_computation.2 | loop fusion | bytes 100 | tf_op jit(solution)/shard_map/dynamic_slice | solution.py:570
  48.2 1.4 %collective-permute-done.18.b_ref = bf16[16,2176]{1,0:T(8,128)(2,1)S(1)} collective-permute-done((bf16[16,2176]{1,0:T(8,128)(2,1)S(1)}, bf16[16,2176]{1,0:T(8,128)(2,1)S(1)}, u32[]{:S(2)}, u32[]{:S(2)}) %collective-permute-start.18) | collective-permute-done | bytes 69664 | tf_op jit(solution)/shard_map/ppermute | solution.py:489
  49.5 2.1 %collective-permute-done.19.c_ref = bf16[16,2176]{1,0:T(8,128)(2,1)S(1)} collective-permute-done((bf16[16,2176]{1,0:T(8,128)(2,1)S(1)}, bf16[16,2176]{1,0:T(8,128)(2,1)S(1)}, u32[]{:S(2)}, u32[]{:S(2)}) %collective-permute-start.19) | collective-permute-done | bytes 69664 | tf_op jit(solution)/shard_map/ppermute | solution.py:489
  51.6 0.0 collective-permute-done.20.d_ref
  51.6 0.7 %add_four.1 = (f32[16,2048]{1,0:T(8,128)}, f32[16,128]{1,0:T(8,128)}) custom-call(bf16[16,2176]{1,0:T(8,128)(2,1)S(1)} %add_convert_fusion.a_ref, bf16[16,2176]{1,0:T(8,128)(2,1)S(1)} %collective-permute-done.18.b_ref, bf16[16,2176]{1,0:T(8,128)(2,1)S(1)} %collective-permute-done.19.c_ref, bf16[16,2176]{1,0:T(8,128)(2,1)S(1)} %collective-permute-done.20.d_ref), custom_call_target="tpu_custom_call" | custom-call | flops 770000000 | bytes 2450000 | tf_op jit(solution)/shard_map/add_four/pallas_call | solution.py:470
  (17 shorter events, 0.1 us)
Async XLA Ops:
  4.4 2.2 %copy-start.3 = (bf16[16,128]{1,0:T(8,128)(2,1)S(1)}, bf16[16,128]{1,0:T(8,128)(2,1)}, u32[]{:S(2)}) copy-start(bf16[16,128]{1,0:T(8,128)(2,1)} %refs_11_.1) | copy-start | bytes 12292
  4.5 2.2 %collective-permute-start = (f32[288,128]{1,0:T(8,128)S(1)}, f32[288,128]{1,0:T(8,128)S(1)}, u32[]{:S(2)}, u32[]{:S(2)}) collective-permute-start(f32[288,128]{1,0:T(8,128)S(1)} %get-tuple-element.31), channel_id=1, source_target_pairs={{0,1},{1,0},{2,3},{3,2},{4,5},{5,4},{6,7},{7,6},{8,9},{9,8},{10,11... | collective-permute-start | bytes 442376 | tf_op jit(solution)/shard_map/ppermute | solution.py:485
  6.5 6.2 %collective-permute-start.8 = (f32[432,128]{1,0:T(8,128)S(1)}, f32[432,128]{1,0:T(8,128)S(1)}, u32[]{:S(2)}, u32[]{:S(2)}) collective-permute-start(f32[432,128]{1,0:T(8,128)S(1)} %get-tuple-element.36), channel_id=1, source_target_pairs={{0,1},{1,0},{2,3},{3,2},{4,5},{5,4},{6,7},{7,6},{8,9},{9,8},{10,11... | collective-permute-start | bytes 663560 | tf_op jit(solution)/shard_map/ppermute | solution.py:485
  6.6 6.1 %copy-start.2 = (s32[24,9]{0,1:T(8,128)S(1)}, s32[24,9]{0,1:T(8,128)}, u32[]{:S(2)}) copy-start(s32[24,9]{0,1:T(8,128)} %param.12) | copy-start | bytes 2596
  6.7 6.1 %copy-start.4 = (s32[16]{0:T(128)S(1)}, s32[16]{0:T(128)}, u32[]{:S(2)}) copy-start(s32[16]{0:T(128)} %table_ref.1) | copy-start | bytes 196
  7.0 9.7 %collective-permute-start.1 = (bf16[1,288,128]{2,1,0:T(8,128)(2,1)S(1)}, bf16[1,288,128]{2,1,0:T(8,128)(2,1)S(1)}, u32[]{:S(2)}, u32[]{:S(2)}) collective-permute-start(bf16[1,288,128]{2,1,0:T(8,128)(2,1)S(1)} %bitcast.15), channel_id=1, source_target_pairs={{0,12},{2,14},{4,8},{6,10},{8,4},{10,6},{12,0},{14,2},{1,13},{3,15... | collective-permute-start | bytes 221192 | tf_op jit(solution)/shard_map/ppermute | solution.py:489
  12.1 6.4 %collective-permute-start.2 = (bf16[1,288,128]{2,1,0:T(8,128)(2,1)S(1)}, bf16[1,288,128]{2,1,0:T(8,128)(2,1)S(1)}, u32[]{:S(2)}, u32[]{:S(2)}) collective-permute-start(bf16[1,288,128]{2,1,0:T(8,128)(2,1)S(1)} %bitcast.16), channel_id=1, source_target_pairs={{0,8},{2,10},{4,12},{6,14},{8,0},{10,2},{12,4},{14,6},{1,9},{3,11}... | collective-permute-start | bytes 221192 | tf_op jit(solution)/shard_map/ppermute | solution.py:489
  12.1 6.4 %collective-permute-start.3 = (bf16[1,288,128]{2,1,0:T(8,128)(2,1)S(1)}, bf16[1,288,128]{2,1,0:T(8,128)(2,1)S(1)}, u32[]{:S(2)}, u32[]{:S(2)}) collective-permute-start(bf16[1,288,128]{2,1,0:T(8,128)(2,1)S(1)} %bitcast.17), channel_id=1, source_target_pairs={{0,4},{2,6},{4,0},{6,2},{8,12},{10,14},{12,8},{14,10},{1,5},{3,7},... | collective-permute-start | bytes 221192 | tf_op jit(solution)/shard_map/ppermute | solution.py:489
  13.7 6.2 %collective-permute-start.10 = (bf16[448,128]{1,0:T(8,128)(2,1)S(1)}, bf16[448,128]{1,0:T(8,128)(2,1)S(1)}, u32[]{:S(2)}, u32[]{:S(2)}) collective-permute-start(bf16[448,128]{1,0:T(8,128)(2,1)S(1)} %get-tuple-element.39.refs_9_), channel_id=1, source_target_pairs={{0,2},{2,0},{4,6},{6,4},{8,10},{10,8},{12,14},{14,12},{1,3},{3,1},... | collective-permute-start | bytes 344072 | tf_op jit(solution)/shard_map/ppermute | solution.py:489
  15.4 1.2 %collective-permute-start.9 = (f32[8,256]{1,0:T(8,128)S(1)}, f32[8,256]{1,0:T(8,128)S(1)}, u32[]{:S(2)}, u32[]{:S(2)}) collective-permute-start(f32[8,256]{1,0:T(8,128)S(1)} %get-tuple-element.38.r_mine_ref), channel_id=1, source_target_pairs={{0,1},{1,0},{2,3},{3,2},{4,5},{5,4},{6,7},{7,6},{8,9},{9,8},{10,11... | collective-permute-start | bytes 24584 | tf_op jit(solution)/shard_map/ppermute | solution.py:485
  16.5 2.5 %collective-permute-start.4 = (bf16[1,288,128]{2,1,0:T(8,128)(2,1)S(1)}, bf16[1,288,128]{2,1,0:T(8,128)(2,1)S(1)}, u32[]{:S(2)}, u32[]{:S(2)}) collective-permute-start(bf16[1,288,128]{2,1,0:T(8,128)(2,1)S(1)} %bitcast.18), channel_id=1, source_target_pairs={{0,1},{1,0},{2,3},{3,2},{4,5},{5,4},{6,7},{7,6},{8,9},{9,8},{10,11... | collective-permute-start | bytes 221192 | tf_op jit(solution)/shard_map/ppermute | solution.py:485
  16.7 2.3 %collective-permute-start.5 = (bf16[1,288,128]{2,1,0:T(8,128)(2,1)S(1)}, bf16[1,288,128]{2,1,0:T(8,128)(2,1)S(1)}, u32[]{:S(2)}, u32[]{:S(2)}) collective-permute-start(bf16[1,288,128]{2,1,0:T(8,128)(2,1)S(1)} %collective-permute-done.1.refs_1_), channel_id=1, source_target_pairs={{0,1},{1,0},{2,3},{3,2},{4,5},{5,4},{6,7},{7,6},{8,9},{9,8},{10,11... | collective-permute-start | bytes 221192 | tf_op jit(solution)/shard_map/ppermute | solution.py:485
  18.5 1.3 %collective-permute-start.6 = (bf16[1,288,128]{2,1,0:T(8,128)(2,1)S(1)}, bf16[1,288,128]{2,1,0:T(8,128)(2,1)S(1)}, u32[]{:S(2)}, u32[]{:S(2)}) collective-permute-start(bf16[1,288,128]{2,1,0:T(8,128)(2,1)S(1)} %collective-permute-done.2.refs_2_), channel_id=1, source_target_pairs={{0,1},{1,0},{2,3},{3,2},{4,5},{5,4},{6,7},{7,6},{8,9},{9,8},{10,11... | collective-permute-start | bytes 221192 | tf_op jit(solution)/shard_map/ppermute | solution.py:485
  18.5 1.4 %collective-permute-start.7 = (bf16[1,288,128]{2,1,0:T(8,128)(2,1)S(1)}, bf16[1,288,128]{2,1,0:T(8,128)(2,1)S(1)}, u32[]{:S(2)}, u32[]{:S(2)}) collective-permute-start(bf16[1,288,128]{2,1,0:T(8,128)(2,1)S(1)} %collective-permute-done.3.refs_3_), channel_id=1, source_target_pairs={{0,1},{1,0},{2,3},{3,2},{4,5},{5,4},{6,7},{7,6},{8,9},{9,8},{10,11... | collective-permute-start | bytes 221192 | tf_op jit(solution)/shard_map/ppermute | solution.py:485
  21.8 3.7 %collective-permute-start.11 = (f32[8,128]{1,0:T(8,128)S(1)}, f32[8,128]{1,0:T(8,128)S(1)}, u32[]{:S(2)}, u32[]{:S(2)}) collective-permute-start(f32[8,128]{1,0:T(8,128)S(1)} %get-tuple-element.42.refs_14_), channel_id=1, source_target_pairs={{0,2},{2,0},{4,6},{6,4},{8,10},{10,8},{12,14},{14,12},{1,3},{3,1},... | collective-permute-start | bytes 12296 | tf_op jit(solution)/shard_map/ppermute | solution.py:489
  25.5 11.9 %copy-start = (bf16[24,32,2048]{2,1,0:T(8,128)(2,1)S(1)}, bf16[24,32,2048]{2,1,0:T(8,128)(2,1)}, u32[]{:S(2)}) copy-start(bf16[24,32,2048]{2,1,0:T(8,128)(2,1)} %param.7) | copy-start | bytes 9437188
  25.5 11.9 %copy-start.1 = (bf16[2,256,2048]{2,1,0:T(8,128)(2,1)S(1)}, bf16[2,256,2048]{2,1,0:T(8,128)(2,1)}, u32[]{:S(2)}) copy-start(bf16[2,256,2048]{2,1,0:T(8,128)(2,1)} %param.8) | copy-start | bytes 6291460
  27.9 8.2 %collective-permute-start.12 = (bf16[2,16,256]{2,1,0:T(8,128)(2,1)S(1)}, bf16[2,16,256]{2,1,0:T(8,128)(2,1)S(1)}, u32[]{:S(2)}, u32[]{:S(2)}) collective-permute-start(bf16[2,16,256]{2,1,0:T(8,128)(2,1)S(1)} %get-tuple-element.47), channel_id=1, source_target_pairs={{0,12},{2,14},{4,8},{6,10},{8,4},{10,6},{12,0},{14,2},{1,13},{3,15... | collective-permute-start | bytes 49160 | tf_op jit(solution)/shard_map/ppermute | solution.py:489
  30.6 5.5 %collective-permute-start.13 = (bf16[2,16,256]{2,1,0:T(8,128)(2,1)S(1)}, bf16[2,16,256]{2,1,0:T(8,128)(2,1)S(1)}, u32[]{:S(2)}, u32[]{:S(2)}) collective-permute-start(bf16[2,16,256]{2,1,0:T(8,128)(2,1)S(1)} %get-tuple-element.48), channel_id=1, source_target_pairs={{0,8},{2,10},{4,12},{6,14},{8,0},{10,2},{12,4},{14,6},{1,9},{3,11}... | collective-permute-start | bytes 49160 | tf_op jit(solution)/shard_map/ppermute | solution.py:489
  30.6 5.5 %collective-permute-start.14 = (bf16[2,16,256]{2,1,0:T(8,128)(2,1)S(1)}, bf16[2,16,256]{2,1,0:T(8,128)(2,1)S(1)}, u32[]{:S(2)}, u32[]{:S(2)}) collective-permute-start(bf16[2,16,256]{2,1,0:T(8,128)(2,1)S(1)} %get-tuple-element.49), channel_id=1, source_target_pairs={{0,4},{2,6},{4,0},{6,2},{8,12},{10,14},{12,8},{14,10},{1,5},{3,7},... | collective-permute-start | bytes 49160 | tf_op jit(solution)/shard_map/ppermute | solution.py:489
  32.4 3.7 %collective-permute-start.15 = (bf16[16,384]{1,0:T(8,128)(2,1)S(1)}, bf16[16,384]{1,0:T(8,128)(2,1)S(1)}, u32[]{:S(2)}, u32[]{:S(2)}) collective-permute-start(bf16[16,384]{1,0:T(8,128)(2,1)S(1)} %get-tuple-element.51), channel_id=1, source_target_pairs={{0,2},{2,0},{4,6},{6,4},{8,10},{10,8},{12,14},{14,12},{1,3},{3,1},... | collective-permute-start | bytes 36872 | tf_op jit(solution)/shard_map/ppermute | solution.py:489
  36.1 1.3 %collective-permute-start.16 = (f32[16,1024]{1,0:T(8,128)S(1)}, f32[16,1024]{1,0:T(8,128)S(1)}, u32[]{:S(2)}, u32[]{:S(2)}) collective-permute-start(f32[16,1024]{1,0:T(8,128)S(1)} %collect.1.mine_ref), channel_id=1, source_target_pairs={{0,1},{1,0},{2,3},{3,2},{4,5},{5,4},{6,7},{7,6},{8,9},{9,8},{10,11... | collective-permute-start | bytes 196616 | tf_op jit(solution)/shard_map/ppermute | solution.py:485
  38.8 4.3 %collective-permute-start.17 = (bf16[16,2176]{1,0:T(8,128)(2,1)S(1)}, bf16[16,2176]{1,0:T(8,128)(2,1)S(1)}, u32[]{:S(2)}, u32[]{:S(2)}) collective-permute-start(bf16[16,2176]{1,0:T(8,128)(2,1)S(1)} %grad_all.1), channel_id=1, source_target_pairs={{0,2},{2,0},{4,6},{6,4},{8,10},{10,8},{12,14},{14,12},{1,3},{3,1},... | collective-permute-start | bytes 208904 | tf_op jit(solution)/shard_map/ppermute | solution.py:489
  43.1 6.4 %collective-permute-start.18 = (bf16[16,2176]{1,0:T(8,128)(2,1)S(1)}, bf16[16,2176]{1,0:T(8,128)(2,1)S(1)}, u32[]{:S(2)}, u32[]{:S(2)}) collective-permute-start(bf16[16,2176]{1,0:T(8,128)(2,1)S(1)} %add_convert_fusion.a_ref), channel_id=1, source_target_pairs={{0,12},{2,14},{4,8},{6,10},{8,4},{10,6},{12,0},{14,2},{1,13},{3,15... | collective-permute-start | bytes 208904 | tf_op jit(solution)/shard_map/ppermute | solution.py:489
  45.7 5.9 %collective-permute-start.19 = (bf16[16,2176]{1,0:T(8,128)(2,1)S(1)}, bf16[16,2176]{1,0:T(8,128)(2,1)S(1)}, u32[]{:S(2)}, u32[]{:S(2)}) collective-permute-start(bf16[16,2176]{1,0:T(8,128)(2,1)S(1)} %add_convert_fusion.a_ref), channel_id=1, source_target_pairs={{0,8},{2,10},{4,12},{6,14},{8,0},{10,2},{12,4},{14,6},{1,9},{3,11}... | collective-permute-start | bytes 208904 | tf_op jit(solution)/shard_map/ppermute | solution.py:489
  45.8 5.9 %collective-permute-start.20 = (bf16[16,2176]{1,0:T(8,128)(2,1)S(1)}, bf16[16,2176]{1,0:T(8,128)(2,1)S(1)}, u32[]{:S(2)}, u32[]{:S(2)}) collective-permute-start(bf16[16,2176]{1,0:T(8,128)(2,1)S(1)} %add_convert_fusion.a_ref), channel_id=1, source_target_pairs={{0,4},{2,6},{4,0},{6,2},{8,12},{10,14},{12,8},{14,10},{1,5},{3,7},... | collective-permute-start | bytes 208904 | tf_op jit(solution)/shard_map/ppermute | solution.py:489

commit v4 on v3

--- a/solution.py
+++ b/solution.py
@@ -37,40 +37,47 @@
 TN = ((0,), (0,))
 
 
-def put_projection(out_ref, projected, rank):
-    tokens = projected.shape[0]
-    out_ref[:tokens, :] = projected[:, :LANES]
+def put_projection(send_ref, keep_ref, projected, rank):
+    tokens = projected.shape[0] // 2
     low = jnp.transpose(projected[:, LANES:])[:rank, :]
-    for t in range(tokens // LANES):
-        out_ref[tokens + t * rank : tokens + (t + 1) * rank, :] = low[:, t * LANES : (t + 1) * LANES]
+    for i, ref in enumerate((send_ref, keep_ref)):
+        ref[:tokens, :] = projected[i * tokens : (i + 1) * tokens, :LANES]
+        for t in range(tokens // LANES):
+            at = i * tokens + t * LANES
+            ref[tokens + t * rank : tokens + (t + 1) * rank, :] = low[:, at : at + LANES]
 
 
 def project_passages_kernel(
     info_ref, p_hbm, q_hbm, proj_hbm, down_hbm, send_ref, keep_ref, q_ref, weight_ref, p_ref, down_ref, sems
 ):
     core = info_ref[2]
-    half = p_hbm.shape[0] // 2
     weights = [
         pltpu.make_async_copy(down_hbm, down_ref, sems.at[0]),
         pltpu.make_async_copy(proj_hbm, weight_ref.at[:, :LANES], sems.at[1]),
     ]
     loads = []
-    for i, owner in enumerate((1 - core, core)):
-        rows = pl.ds(pl.multiple_of(owner * half, LANES), half)
-        loads.append(pltpu.make_async_copy(p_hbm.at[rows, :], p_ref.at[i], sems.at[2 + i]))
-    queries = pltpu.make_async_copy(q_hbm, q_ref, sems.at[4])
-    for copy in weights + loads:
+    for source, to in ((p_hbm, p_ref), (q_hbm, q_ref)):
+        half = source.shape[0] // 2
+        for i, owner in enumerate((1 - core, core)):
+            rows = pl.ds(pl.multiple_of(owner * half, LANES), half)
+            copy = pltpu.make_async_copy(
+                source.at[rows, :], to.at[i * half : (i + 1) * half, :], sems.at[2 + len(loads)]
+            )
+            loads.append(copy)
+    for copy in weights + loads[:2]:
         copy.start()
     weights[0].wait()
     rank, width = down_ref.shape
     low = jnp.concatenate([down_ref[...].astype(f32), jnp.zeros((LANES - rank, width), f32)], axis=0)
     weight_ref[:, LANES:] = jnp.transpose(low).astype(bf16)
     weights[1].wait()
-    queries.start()
-    for i, out in enumerate((send_ref, keep_ref)):
-        loads[i].wait()
-        put_projection(out, dot(p_ref[i], weight_ref[...], NN), rank)
-    queries.wait()
+    for copy in loads[2:]:
+        copy.start()
+    for copy in loads[:2]:
+        copy.wait()
+    put_projection(send_ref, keep_ref, dot(p_ref[...], weight_ref[...], NN), rank)
+    for copy in loads[2:]:
+        copy.wait()
 
 
 def project_passages(info, passage_rows, query_rows, projection, down):
@@ -90,9 +97,9 @@
             pltpu.VMEM((width, 2 * LANES), bf16),
         ),
         scratch_shapes=[
-            pltpu.VMEM((2, half, width), bf16),
+            pltpu.VMEM((2 * half, width), bf16),
             pltpu.VMEM((rank, width), bf16),
-            pltpu.SemaphoreType.DMA((5,)),
+            pltpu.SemaphoreType.DMA((6,)),
         ],
         compiler_params=pltpu.CompilerParams(vmem_limit_bytes=8 * 2**20),
         cost_estimate=cost(3.7),
@@ -100,25 +107,22 @@
     )(info, *operands)
 
 
-def project_queries_kernel(rank, info_ref, q_ref, weight_ref, send_ref, keep_ref):
-    half = q_ref.shape[0] // 2
-    for owner, out in ((1 - info_ref[2], send_ref), (info_ref[2], keep_ref)):
-        rows = pl.ds(pl.multiple_of(owner * half, LANES), half)
-        put_projection(out, dot(q_ref[rows, :], weight_ref[...], NN), rank)
-
-
-def project_queries(info, query_rows, weight, rank):
+def project_queries_kernel(rank, q_ref, weight_ref, send_ref, keep_ref):
+    put_projection(send_ref, keep_ref, dot(q_ref[...], weight_ref[...], NN), rank)
+
+
+def project_queries(query_rows, weight, rank):
     half = query_rows.shape[0] // 2
     shape = jax.ShapeDtypeStruct((half + half // LANES * rank, LANES), f32)
     return pl.pallas_call(
         functools.partial(project_queries_kernel, rank),
-        in_specs=[SMEM] + [VMEM] * 2,
+        in_specs=[VMEM] * 2,
         out_specs=[VMEM] * 2,
         out_shape=(shape, shape),
         compiler_params=pltpu.CompilerParams(vmem_limit_bytes=4 * 2**20),
         cost_estimate=cost(1.5),
         name="project_queries",
-    )(info, query_rows, weight)
+    )(query_rows, weight)
 
 
 def pad_lanes(x):
@@ -267,10 +271,9 @@
 def backward_kernel(cfg, *refs):
     qlen, qtok, plen, store, where, n_packs = cfg
     packs = refs[:n_packs]
-    info_ref, mine_ref, other_ref, up_ref, stats_ref, total_ref, sums_ref, recv_ref, expo_ref, vqt_ref = refs[
-        n_packs : n_packs + 10
-    ]
-    refs = refs[n_packs + 10 :]
+    info_ref, mine_ref, other_ref, up_ref, stats_ref, total_ref, sums_ref, recv_ref = refs[n_packs : n_packs + 8]
+    expo_ref, unit_ref, vqt_ref = refs[n_packs + 8 : n_packs + 11]
+    refs = refs[n_packs + 11 :]
     n_parts = n_packs // 2 if store else 1
     part_refs, (dmine_ref, dother_ref, gup_ref, loss_ref) = refs[:n_parts], refs[n_parts : n_parts + 4]
     scale_ref, dvqt_ref, grad_ref, dv_ref, dvb_ref = refs[n_parts + 4 :]
@@ -300,7 +303,7 @@
             rows = slice(pos * plen, (pos + 1) * plen)
             grad_ref[rows, :] = (expo_ref[pos].astype(f32) * scale_ref[pos : pos + 1, :]).astype(bf16)
             dv_ref[rows, :] = dot(grad_ref[rows, :], vq, NN)
-            dvqt = dot(packs[pos][0, :plen, :], grad_ref[rows, :], TN)
+            dvqt = unit_ref[pos] * scale_ref[pos : pos + 1, :]
             dvqt_ref[...] = dvqt if pos == 0 else dvqt_ref[...] + dvqt
         for pos, pack in enumerate(packs):
             rows = slice(pos * plen, (pos + 1) * plen)
@@ -370,7 +373,28 @@
     )(*packs, info, mine, other)
 
 
-def score_backward(packs, steps, info, mine, other, up, stats, total, sums, recv, expo, vqt, qlen, qtok, plen):
+def unit_kernel(plen, *refs):
+    packs, (expo_ref, unit_ref) = refs[:-2], refs[-2:]
+    for pos, pack in enumerate(packs):
+        unit_ref[pos] = dot(pack[0, :plen, :], expo_ref[pos], TN)
+
+
+def unit_of(packs, expo):
+    npos, plen, ntok = expo.shape
+    if npos != len(packs):
+        return jnp.zeros((1, 8, LANES), f32)
+    return pl.pallas_call(
+        functools.partial(unit_kernel, plen),
+        in_specs=[VMEM] * (npos + 1),
+        out_specs=VMEM,
+        out_shape=jax.ShapeDtypeStruct((npos, LANES, ntok), f32),
+        compiler_params=pltpu.CompilerParams(vmem_limit_bytes=4 * 2**20),
+        cost_estimate=cost(1.2),
+        name="unit",
+    )(*packs, expo)
+
+
+def score_backward(packs, steps, info, mine, other, up, stats, total, sums, recv, expo, unit, vqt, qlen, qtok, plen):
     npos, rank = 2 * len(steps), up.shape[0]
     store = len(packs) == npos
     cfg = (qlen, qtok, plen, store, places(steps), len(packs))
@@ -380,7 +404,7 @@
     parts = (part,) * len(steps) if store else (whole,)
     return pl.pallas_call(
         functools.partial(backward_kernel, cfg),
-        in_specs=[VMEM] * len(packs) + [SMEM] + [VMEM] * 9,
+        in_specs=[VMEM] * len(packs) + [SMEM] + [VMEM] * 10,
         out_specs=[VMEM] * (len(parts) + 4),
         out_shape=(
             *parts,
@@ -399,34 +423,35 @@
         compiler_params=pltpu.CompilerParams(vmem_limit_bytes=(20 if store else 40) * 2**20),
         cost_estimate=cost(2.5),
         name="score_backward",
-    )(*packs, info, mine, other, up, stats, total, sums, recv, expo, vqt)
+    )(*packs, info, mine, other, up, stats, total, sums, recv, expo, unit, vqt)
 
 
 def collect_kernel(n, *refs):
-    parts, (mine_ref, recv_ref, r_ref, up_ref, out_ref) = refs[:n], refs[n:]
+    parts, (mine_ref, recv_ref, r_ref, r_p_ref, up_ref, out_ref) = refs[:n], refs[n:]
     _, _, plen = parts[0].shape
     qtok = mine_ref.shape[1]
     for i in range(2):
         out_ref[:, i * plen : (i + 1) * plen] = sum(part[i].astype(f32) for part in parts)
     out_ref[:, 2 * plen : 2 * plen + qtok] = (mine_ref[...] + recv_ref[...].astype(f32)) * r_ref[:1, :]
-    out_ref[:, 2 * plen + qtok :] = up_ref[...]
-
-
-def collect(parts, mine, recv, r, up):
+    out_ref[:, 2 * plen + qtok : 2 * plen + qtok + LANES] = up_ref[...]
+    out_ref[:, 2 * plen + qtok + LANES :] = jnp.broadcast_to(r_p_ref[:1, :], (out_ref.shape[0], plen))
+
+
+def collect(parts, mine, recv, r, r_p, up):
     rank, qtok = mine.shape
     plen = parts[0].shape[2]
     return pl.pallas_call(
         functools.partial(collect_kernel, len(parts)),
-        in_specs=[VMEM] * (len(parts) + 4),
+        in_specs=[VMEM] * (len(parts) + 5),
         out_specs=VMEM,
-        out_shape=jax.ShapeDtypeStruct((rank, 2 * plen + qtok + LANES), f32),
+        out_shape=jax.ShapeDtypeStruct((rank, 3 * plen + qtok + LANES), f32),
         compiler_params=pltpu.CompilerParams(vmem_limit_bytes=4 * 2**20),
         cost_estimate=cost(0.3),
         name="collect",
-    )(*parts, mine, recv, r, up)
-
-
-def grad_kernel(plen, qtok, info_ref, p_ref, q_ref, mine_ref, other_ref, r_mine_ref, r_other_ref, out_ref):
+    )(*parts, mine, recv, r, r_p, up)
+
+
+def grad_kernel(plen, qtok, info_ref, p_ref, q_ref, mine_ref, other_ref, out_ref):
     core = info_ref[2]
     width = p_ref.shape[1]
     queries = slice(2 * plen, 2 * plen + qtok)
@@ -434,31 +459,32 @@
     q_dlow = [jnp.where(core == i, q_mine, q_other) for i in range(2)]
     p_dlow = []
     for i in range(2):
-        r = jnp.where(core == i, r_mine_ref[:1, :plen], r_other_ref[:1, :plen])
+        r = jnp.where(core == i, mine_ref[:, -plen:], other_ref[:, -plen:])
         rows = slice(i * plen, (i + 1) * plen)
         p_dlow.append(((mine_ref[:, rows] + other_ref[:, rows]) * r).astype(bf16))
     total = dot(jnp.concatenate(q_dlow, axis=1), q_ref[...], NN)
     total += dot(jnp.concatenate(p_dlow, axis=1), p_ref[...], NN)
     out_ref[:, :width] = total.astype(bf16)
-    out_ref[:, width:] = (mine_ref[:, 2 * plen + qtok :] + other_ref[:, 2 * plen + qtok :]).astype(bf16)
-
-
-def grad_all(info, passage_rows, query_rows, mine, other, r_mine, r_other, plen, qtok):
+    ups = slice(2 * plen + qtok, 2 * plen + qtok + LANES)
+    out_ref[:, width:] = (mine_ref[:, ups] + other_ref[:, ups]).astype(bf16)
+
+
+def grad_all(info, passage_rows, query_rows, mine, other, plen, qtok):
     rank, width = mine.shape[0], passage_rows.shape[1]
     return pl.pallas_call(
         functools.partial(grad_kernel, plen, qtok),
-        in_specs=[SMEM] + [VMEM] * 6,
+        in_specs=[SMEM] + [VMEM] * 4,
         out_specs=VMEM,
         out_shape=jax.ShapeDtypeStruct((rank, width + LANES), bf16),
         compiler_params=pltpu.CompilerParams(vmem_limit_bytes=4 * 2**20),
         cost_estimate=cost(1.3),
         name="grad_all",
-    )(info, passage_rows, query_rows, mine, other, r_mine, r_other)
+    )(info, passage_rows, query_rows, mine, other)
 
 
 def add_kernel(a_ref, b_ref, c_ref, d_ref, down_ref, up_ref):
-    total = (a_ref[...].astype(f32) + d_ref[...].astype(f32)) + (
-        b_ref[...].astype(f32) + c_ref[...].astype(f32)
+    total = (a_ref[...].astype(f32) + b_ref[...].astype(f32)) + (
+        c_ref[...].astype(f32) + d_ref[...].astype(f32)
     )
     width = down_ref.shape[1]
     down_ref[...] = total[:, :width]
@@ -492,8 +518,8 @@
 def gather_packs(pack, nshard, groups):
     if nshard == 8:
         pack = pack[None]
-        near = [pack] + [across(pack, nshard, k) for k in (6, 4, 2)]
-        return near + [swap(piece) for piece in near], (0, 3, 2, 1)
+        near = [pack] + [across(pack, nshard, k) for k in (2, 4, 6)]
+        return near + [swap(piece) for piece in near], (0, 1, 2, 3)
     near = lax.all_gather(pack, "shard", axis_index_groups=groups)
     return [near, swap(near)], tuple(range(nshard // 2))
 
@@ -502,7 +528,7 @@
     if len(parts) == 1:
         parts = lax.all_to_all(parts[0], "shard", split_axis=0, concat_axis=0, tiled=True, axis_index_groups=groups)
         return [jnp.sum(parts.astype(f32), axis=0)]
-    return [parts[0]] + [across(part, nshard, 2 * step) for part, step in zip(parts[1:], steps[1:], strict=True)]
+    return [parts[0]] + [across(part, nshard, 2 * step) for part, step in reversed([*zip(parts, steps, strict=True)][1:])]
 
 
 def sum_over_shards(x, nshard, width):
@@ -510,7 +536,7 @@
         x = lax.psum(x.astype(f32), "shard")
         return x[:, :width], x[:, width:]
     x = (x.astype(f32) + across(x, nshard, 1).astype(f32)).astype(bf16)
-    return add_four([x] + [across(x, nshard, k) for k in (6, 4, 2)], width)
+    return add_four([x] + [across(x, nshard, k) for k in (2, 4, 6)], width)
 
 
 def per_device(
@@ -537,14 +563,13 @@
     send_p, keep_p, query_vmem, weight = project_passages(
         info, passage_rows, query_rows, projection_matrix, jnp.transpose(adapter_down_weight)
     )
-    send_q, keep_q = project_queries(info, query_vmem, weight, adapter_up_weight.shape[0])
+    send_q, keep_q = project_queries(query_vmem, weight, adapter_up_weight.shape[0])
     ppack, r_p = pack_passage(keep_p, swap(send_p), adapter_up_weight)
     mine, r_q = pack_queries(
         info, passage_row_table, jnp.transpose(passage_pair_index), keep_q, swap(send_q), adapter_up_weight
     )
     other = across(mine, nshard, 1)
     packs, steps = gather_packs(ppack, nshard, groups)
-    mine, r_other = lax.optimization_barrier((mine, swap(r_p)))
 
     stats, total, sums, expo, vqt = score_forward(packs, steps, info, mine, other, qlen, qtok, plen)
     *parts, dlow_mine, dlow_other, gup, loss = score_backward(
@@ -559,14 +584,15 @@
         sums,
         across(sums, nshard, 1),
         expo,
+        unit_of(packs, expo),
         vqt,
         qlen,
         qtok,
         plen,
     )
     parts = exchange_parts(parts, steps, nshard, groups)
-    collected = collect(parts, dlow_mine, across(dlow_other, nshard, 1), r_q, gup)
-    grads = grad_all(info, passage_rows, query_rows, collected, swap(collected), r_p, r_other, plen, qtok)
+    collected = collect(parts, dlow_mine, across(dlow_other, nshard, 1), r_q, r_p, gup)
+    grads = grad_all(info, passage_rows, query_rows, collected, swap(collected), plen, qtok)
     query_loss = lax.dynamic_slice_in_dim(loss[0], info[0] * half, half, 0)
     down_sum, up_sum = sum_over_shards(grads, nshard, width)
     return (query_loss, jnp.transpose(down_sum), up_sum)

time: 52.5 us -> 51.8 us (0.987)
  waiting for transfers between devices: 15.4 us -> 14.8 us
    ppermute x8 -> x7, waiting for transfers between devices: 3.33 us -> 2.18 us  [swap(): return lax.ppermute(x, 'sub', [(0, 1), (1, 0)])]
    pallas_call x0 -> x1, Pallas kernels: none -> 0.61 us  [unit_of(): pl.pallas_call(functools.partial(unit_kernel, plen), in_specs=[VMEM] * (n...]
    ppermute x13, waiting for transfers between devices: 12.1 us -> 12.6 us  [across(): return lax.ppermute(x, 'shard', [(i, i ^ step) for i in range(nshard)])]
    pallas_call x1, Pallas kernels: 1.56 us -> 1.02 us  [project_queries(): pl.pallas_call(functools.partial(project_queries_kernel, rank), in_specs=...]
    ppermute x8 -> x7, starting transfers between devices: 1.72 us -> 1.71 us  [swap(): return lax.ppermute(x, 'sub', [(0, 1), (1, 0)])]
  transfers between devices with their start and end apart: 21 -> 20, of which waited for: 10 -> 9; matrix products, arithmetic and copies ran while one was open for 1% -> 1% of each run, Pallas kernels for 5% -> 6%
where the time goes in v4:
time: 51.8 us; the launch traced here: 51.7 us
  starting transfers between devices  22.6 us (44%)
  waiting for transfers between devices  14.8 us (29%)
  Pallas kernels  12.9 us (25%)
  between operations  0.73 us (1%)
  local copies, waits for them, and re-layouts  0.6 us (1%)
    ppermute x13, starting transfers between devices, across(): return lax.ppermute(x, 'shard', [(i, i ^ step) for i in range(nshard)])  20.8 us
    ppermute x13, waiting for transfers between devices, across(): return lax.ppermute(x, 'shard', [(i, i ^ step) for i in range(nshard)])  12.6 us
    pallas_call x1, Pallas kernels, project_passages(): pl.pallas_call(project_passages_kernel, in_specs=[SMEM] + [HBM] * 4, out_...  3.71 us
    pallas_call x1, Pallas kernels, score_backward(): pl.pallas_call(functools.partial(backward_kernel, cfg), in_specs=[VMEM] *...  2.33 us
    ppermute x7, waiting for transfers between devices, swap(): return lax.ppermute(x, 'sub', [(0, 1), (1, 0)])  2.18 us
    pallas_call x1, Pallas kernels, score_forward(): pl.pallas_call(functools.partial(forward_kernel, cfg), in_specs=[VMEM] *...  1.88 us
    ppermute x7, starting transfers between devices, swap(): return lax.ppermute(x, 'sub', [(0, 1), (1, 0)])  1.71 us
    pallas_call x1, Pallas kernels, grad_all(): pl.pallas_call(functools.partial(grad_kernel, plen, qtok), in_specs=[SMEM...  1.32 us
  transfers between devices with their start and end apart: 20, of which 9 were waited for; matrix products, arithmetic and copies ran while one was open for 1% of the time, Pallas kernels for 6%

profile of v4, /device:TPU:0, one launch (start us, length us, event | category | flops | bytes accessed | tf_op | source)
XLA Modules:
  0.0 51.7 jit_solution(12150094471933932406)
XLA Ops:
  0.6 0.1 pad_add_fusion.info_ref.refs_8_
  0.7 3.7 %project_passages.1 = (f32[288,128]{1,0:T(8,128)S(1)}, f32[288,128]{1,0:T(8,128)S(1)}, bf16[768,2048]{1,0:T(8,128)(2,1)S(1)}, bf16[2048,256]{1,0:T(8,128)(2,1)S(1)}) custom-call(s32[3]{0:T(128)S(1)} %pad_add_fusion.info_ref.refs_8_, bf16[512,2048]{1,0:T(8,128)(2,1)} %bitcast.13, bf16[768,2048]{1,0:T(8,128)(2,1)} %bitcast.11, bf16[2048,128]{1,0:T(8,128)(2,1)} %proj_hbm.1, ...), custom_call_target="tpu_custom_call" | custom-call | flops 4070000128 | bytes 12950000 | tf_op jit(solution)/shard_map/project_passages/pallas_call | solution.py:89
  4.4 0.0 copy-start.3
  4.5 0.5 %collective-permute-start = (f32[288,128]{1,0:T(8,128)S(1)}, f32[288,128]{1,0:T(8,128)S(1)}, u32[]{:S(2)}, u32[]{:S(2)}) collective-permute-start(f32[288,128]{1,0:T(8,128)S(1)} %get-tuple-element.29), channel_id=1, source_target_pairs={{0,1},{1,0},{2,3},{3,2},{4,5},{5,4},{6,7},{7,6},{8,9},{9,8},{10,11... | collective-permute-start | bytes 442376 | tf_op jit(solution)/shard_map/ppermute | solution.py:511
  5.0 1.0 %project_queries.1 = (f32[432,128]{1,0:T(8,128)S(1)}, f32[432,128]{1,0:T(8,128)S(1)}) custom-call(bf16[768,2048]{1,0:T(8,128)(2,1)S(1)} %get-tuple-element.31.q_ref, bf16[2048,256]{1,0:T(8,128)(2,1)S(1)} %get-tuple-element.32.weight_ref), custom_call_target="tpu_custom_call" | custom-call | flops 1650000000 | bytes 5250000 | tf_op jit(solution)/shard_map/project_queries/pallas_call | solution.py:117
  6.0 0.1 collective-permute-start.8
  6.1 0.0 collective-permute-done.recv_ref
  6.1 0.3 pack_passage.1
  6.5 5.1 %collective-permute-start.3 = (bf16[1,288,128]{2,1,0:T(8,128)(2,1)S(1)}, bf16[1,288,128]{2,1,0:T(8,128)(2,1)S(1)}, u32[]{:S(2)}, u32[]{:S(2)}) collective-permute-start(bf16[1,288,128]{2,1,0:T(8,128)(2,1)S(1)} %bitcast.15), channel_id=1, source_target_pairs={{0,12},{2,14},{4,8},{6,10},{8,4},{10,6},{12,0},{14,2},{1,13},{3,15... | collective-permute-start | bytes 221192 | tf_op jit(solution)/shard_map/ppermute | solution.py:515
  11.5 0.6 %collective-permute-start.1 = (bf16[1,288,128]{2,1,0:T(8,128)(2,1)S(1)}, bf16[1,288,128]{2,1,0:T(8,128)(2,1)S(1)}, u32[]{:S(2)}, u32[]{:S(2)}) collective-permute-start(bf16[1,288,128]{2,1,0:T(8,128)(2,1)S(1)} %bitcast.17), channel_id=1, source_target_pairs={{0,4},{2,6},{4,0},{6,2},{8,12},{10,14},{12,8},{14,10},{1,5},{3,7},... | collective-permute-start | bytes 221192 | tf_op jit(solution)/shard_map/ppermute | solution.py:515
  12.2 1.0 %pack_queries.1 = (bf16[448,128]{1,0:T(8,128)(2,1)S(1)}, f32[8,384]{1,0:T(8,128)S(1)}) custom-call(s32[3]{0:T(128)S(1)} %pad_add_fusion.info_ref.refs_8_, s32[16]{0:T(128)S(1)} %copy-done.4, s32[9,24]{1,0:T(8,128)S(1)} %bitcast.22, f32[432,128]{1,0:T(8,128)S(1)} %get-tuple-element.33.keep_ref, f32[432,128]{1,0:T(8,128)S(1)} %collective-permute-done.8.recv_ref, ...), custom_call_target="tpu_custom_call" | custom-call | flops 990000000 | bytes 3150000 | tf_op jit(solution)/shard_map/pack_queries/pallas_call | solution.py:192
  13.2 1.7 %collective-permute-start.9 = (bf16[448,128]{1,0:T(8,128)(2,1)S(1)}, bf16[448,128]{1,0:T(8,128)(2,1)S(1)}, u32[]{:S(2)}, u32[]{:S(2)}) collective-permute-start(bf16[448,128]{1,0:T(8,128)(2,1)S(1)} %get-tuple-element.35.refs_9_), channel_id=1, source_target_pairs={{0,2},{2,0},{4,6},{6,4},{8,10},{10,8},{12,14},{14,12},{1,3},{3,1},... | collective-permute-start | bytes 344072 | tf_op jit(solution)/shard_map/ppermute | solution.py:515
  14.8 0.0 collective-permute-start.4
  14.8 0.0 collective-permute-done.3.refs_3_
  14.8 0.5 collective-permute-start.7
  15.3 2.6 %collective-permute-done.2.refs_2_ = bf16[1,288,128]{2,1,0:T(8,128)(2,1)S(1)} collective-permute-done((bf16[1,288,128]{2,1,0:T(8,128)(2,1)S(1)}, bf16[1,288,128]{2,1,0:T(8,128)(2,1)S(1)}, u32[]{:S(2)}, u32[]{:S(2)}) %collective-permute-start.2) | collective-permute-done | bytes 73760 | tf_op jit(solution)/shard_map/ppermute | solution.py:515
  18.0 0.0 collective-permute-done.1.refs_1_
  18.0 0.5 collective-permute-start.5
  18.5 0.0 collective-permute-done.4.refs_4_
  18.5 0.0 collective-permute-done.7.refs_7_
  18.5 0.7 %collective-permute-done.6.refs_6_ = bf16[1,288,128]{2,1,0:T(8,128)(2,1)S(1)} collective-permute-done((bf16[1,288,128]{2,1,0:T(8,128)(2,1)S(1)}, bf16[1,288,128]{2,1,0:T(8,128)(2,1)S(1)}, u32[]{:S(2)}, u32[]{:S(2)}) %collective-permute-start.6) | collective-permute-done | bytes 73760 | tf_op jit(solution)/shard_map/ppermute | solution.py:511
  19.2 0.2 collective-permute-done.5.refs_5_
  19.4 0.0 collective-permute-done.9.refs_10_
  19.4 1.9 %score_forward.1 = (f32[3,8,128]{2,1,0:T(8,128)S(1)}, f32[8,768]{1,0:T(8,128)S(1)}, f32[8,128]{1,0:T(8,128)S(1)}, bf16[8,256,768]{2,1,0:T(8,128)(2,1)S(1)}, bf16[128,768]{1,0:T(8,128)(2,1)S(1)}) custom-call(bf16[1,288,128]{2,1,0:T(8,128)(2,1)S(1)} %bitcast.19, bf16[1,288,128]{2,1,0:T(8,128)(2,1)S(1)} %collective-permute-done.1.refs_1_, ...), custom_call_target="tpu_custom_call" | custom-call | flops 2090000000 | bytes 6650000 | tf_op jit(solution)/shard_map/score_forward/pallas_call | solution.py:359
  21.3 1.6 %collective-permute-start.10 = (f32[8,128]{1,0:T(8,128)S(1)}, f32[8,128]{1,0:T(8,128)S(1)}, u32[]{:S(2)}, u32[]{:S(2)}) collective-permute-start(f32[8,128]{1,0:T(8,128)S(1)} %get-tuple-element.38.refs_14_), channel_id=1, source_target_pairs={{0,2},{2,0},{4,6},{6,4},{8,10},{10,8},{12,14},{14,12},{1,3},{3,1},... | collective-permute-start | bytes 12296 | tf_op jit(solution)/shard_map/ppermute | solution.py:515
  22.8 0.6 %unit.1.refs_17_ = f32[8,128,768]{2,1,0:T(8,128)S(1)} custom-call(bf16[1,288,128]{2,1,0:T(8,128)(2,1)S(1)} %bitcast.20, bf16[1,288,128]{2,1,0:T(8,128)(2,1)S(1)} %collective-permute-done.1.refs_1_, bf16[1,288,128]{2,1,0:T(8,128)(2,1)S(1)} %collective-permute-done.2.refs_2_, bf16[1,288,128]{2,1,0:T(8,128)(2,1)S(1)} %collective-permute-done.3.refs_3_, ...), custom_call_target="tpu_custom_call" | custom-call | flops 1320000000 | bytes 4200000 | tf_op jit(solution)/shard_map/unit/pallas_call | solution.py:386
  23.5 1.5 %collective-permute-done.10.refs_15_ = f32[8,128]{1,0:T(8,128)S(1)} collective-permute-done((f32[8,128]{1,0:T(8,128)S(1)}, f32[8,128]{1,0:T(8,128)S(1)}, u32[]{:S(2)}, u32[]{:S(2)}) %collective-permute-start.10) | collective-permute-done | bytes 4128 | tf_op jit(solution)/shard_map/ppermute | solution.py:515
  25.0 2.3 %score_backward.1 = (bf16[2,16,256]{2,1,0:T(8,128)(2,1)S(1)}, bf16[2,16,256]{2,1,0:T(8,128)(2,1)S(1)}, bf16[2,16,256]{2,1,0:T(8,128)(2,1)S(1)}, bf16[2,16,256]{2...) custom-call(bf16[1,288,128]{2,1,0:T(8,128)(2,1)S(1)} %bitcast.21, ...), custom_call_target="tpu_custom_call" | custom-call | flops 2750000128 | bytes 8750000 | tf_op jit(solution)/shard_map/score_backward/pallas_call | solution.py:405
  27.3 2.6 %collective-permute-start.11 = (bf16[2,16,256]{2,1,0:T(8,128)(2,1)S(1)}, bf16[2,16,256]{2,1,0:T(8,128)(2,1)S(1)}, u32[]{:S(2)}, u32[]{:S(2)}) collective-permute-start(bf16[2,16,256]{2,1,0:T(8,128)(2,1)S(1)} %get-tuple-element.43), channel_id=1, source_target_pairs={{0,12},{2,14},{4,8},{6,10},{8,4},{10,6},{12,0},{14,2},{1,13},{3,15... | collective-permute-start | bytes 49160 | tf_op jit(solution)/shard_map/ppermute | solution.py:515
  29.9 0.0 collective-permute-start.12
  29.9 1.8 %collective-permute-start.13 = (bf16[2,16,256]{2,1,0:T(8,128)(2,1)S(1)}, bf16[2,16,256]{2,1,0:T(8,128)(2,1)S(1)}, u32[]{:S(2)}, u32[]{:S(2)}) collective-permute-start(bf16[2,16,256]{2,1,0:T(8,128)(2,1)S(1)} %get-tuple-element.45), channel_id=1, source_target_pairs={{0,4},{2,6},{4,0},{6,2},{8,12},{10,14},{12,8},{14,10},{1,5},{3,7},... | collective-permute-start | bytes 49160 | tf_op jit(solution)/shard_map/ppermute | solution.py:515
  31.7 1.5 %collective-permute-start.14 = (bf16[16,384]{1,0:T(8,128)(2,1)S(1)}, bf16[16,384]{1,0:T(8,128)(2,1)S(1)}, u32[]{:S(2)}, u32[]{:S(2)}) collective-permute-start(bf16[16,384]{1,0:T(8,128)(2,1)S(1)} %get-tuple-element.47), channel_id=1, source_target_pairs={{0,2},{2,0},{4,6},{6,4},{8,10},{10,8},{12,14},{14,12},{1,3},{3,1},... | collective-permute-start | bytes 36872 | tf_op jit(solution)/shard_map/ppermute | solution.py:515
  33.2 2.2 %collective-permute-done.14.refs_5_ = bf16[16,384]{1,0:T(8,128)(2,1)S(1)} collective-permute-done((bf16[16,384]{1,0:T(8,128)(2,1)S(1)}, bf16[16,384]{1,0:T(8,128)(2,1)S(1)}, u32[]{:S(2)}, u32[]{:S(2)}) %collective-permute-start.14) | collective-permute-done | bytes 12320 | tf_op jit(solution)/shard_map/ppermute | solution.py:515
  35.4 0.0 collective-permute-done.11.refs_1_
  35.4 0.0 collective-permute-done.12.refs_2_
  35.4 0.0 collective-permute-done.13.refs_3_
  35.5 0.1 collective-permute-start.15
  35.6 1.3 %collective-permute-done.15.other_ref = f32[16,1280]{1,0:T(8,128)S(1)} collective-permute-done((f32[16,1280]{1,0:T(8,128)S(1)}, f32[16,1280]{1,0:T(8,128)S(1)}, u32[]{:S(2)}, u32[]{:S(2)}) %collective-permute-start.15) | collective-permute-done | bytes 81952 | tf_op jit(solution)/shard_map/ppermute | solution.py:511
  36.8 1.3 %grad_all.1 = bf16[16,2176]{1,0:T(8,128)(2,1)S(1)} custom-call(s32[3]{0:T(128)S(1)} %pad_add_fusion.info_ref.refs_8_, bf16[512,2048]{1,0:T(8,128)(2,1)S(1)} %bitcast.14, bf16[768,2048]{1,0:T(8,128)(2,1)S(1)} %bitcast.12, f32[16,1280]{1,0:T(8,128)S(1)} %collect.1.mine_ref, f32[16,1280]{1,0:T(8,128)S(1)} %collective-permute-done.15.other_ref), custom_call_target="tpu_custom_call" | custom-call | flops 1430000000 | bytes 4550000 | tf_op jit(solution)/shard_map/grad_all/pallas_call | solution.py:474
  38.1 1.5 %collective-permute-start.16 = (bf16[16,2176]{1,0:T(8,128)(2,1)S(1)}, bf16[16,2176]{1,0:T(8,128)(2,1)S(1)}, u32[]{:S(2)}, u32[]{:S(2)}) collective-permute-start(bf16[16,2176]{1,0:T(8,128)(2,1)S(1)} %grad_all.1), channel_id=1, source_target_pairs={{0,2},{2,0},{4,6},{6,4},{8,10},{10,8},{12,14},{14,12},{1,3},{3,1},... | collective-permute-start | bytes 208904 | tf_op jit(solution)/shard_map/ppermute | solution.py:515
  39.7 2.8 %collective-permute-done.16 = bf16[16,2176]{1,0:T(8,128)(2,1)S(1)} collective-permute-done((bf16[16,2176]{1,0:T(8,128)(2,1)S(1)}, bf16[16,2176]{1,0:T(8,128)(2,1)S(1)}, u32[]{:S(2)}, u32[]{:S(2)}) %collective-permute-start.16) | collective-permute-done | bytes 69664 | tf_op jit(solution)/shard_map/ppermute | solution.py:515
  42.5 2.6 %collective-permute-start.19 = (bf16[16,2176]{1,0:T(8,128)(2,1)S(1)}, bf16[16,2176]{1,0:T(8,128)(2,1)S(1)}, u32[]{:S(2)}, u32[]{:S(2)}) collective-permute-start(bf16[16,2176]{1,0:T(8,128)(2,1)S(1)} %add_convert_fusion.a_ref), channel_id=1, source_target_pairs={{0,12},{2,14},{4,8},{6,10},{8,4},{10,6},{12,0},{14,2},{1,13},{3,15... | collective-permute-start | bytes 208904 | tf_op jit(solution)/shard_map/ppermute | solution.py:515
  45.1 1.8 %collective-permute-start.17 = (bf16[16,2176]{1,0:T(8,128)(2,1)S(1)}, bf16[16,2176]{1,0:T(8,128)(2,1)S(1)}, u32[]{:S(2)}, u32[]{:S(2)}) collective-permute-start(bf16[16,2176]{1,0:T(8,128)(2,1)S(1)} %add_convert_fusion.a_ref), channel_id=1, source_target_pairs={{0,4},{2,6},{4,0},{6,2},{8,12},{10,14},{12,8},{14,10},{1,5},{3,7},... | collective-permute-start | bytes 208904 | tf_op jit(solution)/shard_map/ppermute | solution.py:515
  46.9 0.6 %dynamic-slice_bitcast_fusion = f32[12]{0:T(128)} fusion(f32[1,128]{1,0:T(1,128)S(1)} %slice.3, s32[]{:T(128)S(6)} %select_n.16), kind=kLoop, calls=%fused_computation.2 | loop fusion | bytes 100 | tf_op jit(solution)/shard_map/dynamic_slice | solution.py:596
  47.5 1.4 %collective-permute-done.19.d_ref = bf16[16,2176]{1,0:T(8,128)(2,1)S(1)} collective-permute-done((bf16[16,2176]{1,0:T(8,128)(2,1)S(1)}, bf16[16,2176]{1,0:T(8,128)(2,1)S(1)}, u32[]{:S(2)}, u32[]{:S(2)}) %collective-permute-start.19) | collective-permute-done | bytes 69664 | tf_op jit(solution)/shard_map/ppermute | solution.py:515
  48.9 2.0 %collective-permute-done.18.c_ref = bf16[16,2176]{1,0:T(8,128)(2,1)S(1)} collective-permute-done((bf16[16,2176]{1,0:T(8,128)(2,1)S(1)}, bf16[16,2176]{1,0:T(8,128)(2,1)S(1)}, u32[]{:S(2)}, u32[]{:S(2)}) %collective-permute-start.18) | collective-permute-done | bytes 69664 | tf_op jit(solution)/shard_map/ppermute | solution.py:515
  51.0 0.0 collective-permute-done.17.b_ref
  51.0 0.7 %add_four.1 = (f32[16,2048]{1,0:T(8,128)}, f32[16,128]{1,0:T(8,128)}) custom-call(bf16[16,2176]{1,0:T(8,128)(2,1)S(1)} %add_convert_fusion.a_ref, bf16[16,2176]{1,0:T(8,128)(2,1)S(1)} %collective-permute-done.17.b_ref, bf16[16,2176]{1,0:T(8,128)(2,1)S(1)} %collective-permute-done.18.c_ref, bf16[16,2176]{1,0:T(8,128)(2,1)S(1)} %collective-permute-done.19.d_ref), custom_call_target="tpu_custom_call" | custom-call | flops 770000000 | bytes 2450000 | tf_op jit(solution)/shard_map/add_four/pallas_call | solution.py:496
  (16 shorter events, 0.1 us)
Async XLA Ops:
  4.4 1.7 %copy-start.3 = (bf16[16,128]{1,0:T(8,128)(2,1)S(1)}, bf16[16,128]{1,0:T(8,128)(2,1)}, u32[]{:S(2)}) copy-start(bf16[16,128]{1,0:T(8,128)(2,1)} %refs_11_.1) | copy-start | bytes 12292
  4.5 1.6 %collective-permute-start = (f32[288,128]{1,0:T(8,128)S(1)}, f32[288,128]{1,0:T(8,128)S(1)}, u32[]{:S(2)}, u32[]{:S(2)}) collective-permute-start(f32[288,128]{1,0:T(8,128)S(1)} %get-tuple-element.29), channel_id=1, source_target_pairs={{0,1},{1,0},{2,3},{3,2},{4,5},{5,4},{6,7},{7,6},{8,9},{9,8},{10,11... | collective-permute-start | bytes 442376 | tf_op jit(solution)/shard_map/ppermute | solution.py:511
  6.0 6.2 %collective-permute-start.8 = (f32[432,128]{1,0:T(8,128)S(1)}, f32[432,128]{1,0:T(8,128)S(1)}, u32[]{:S(2)}, u32[]{:S(2)}) collective-permute-start(f32[432,128]{1,0:T(8,128)S(1)} %get-tuple-element.34), channel_id=1, source_target_pairs={{0,1},{1,0},{2,3},{3,2},{4,5},{5,4},{6,7},{7,6},{8,9},{9,8},{10,11... | collective-permute-start | bytes 663560 | tf_op jit(solution)/shard_map/ppermute | solution.py:511
  6.1 6.1 %copy-start.2 = (s32[24,9]{0,1:T(8,128)S(1)}, s32[24,9]{0,1:T(8,128)}, u32[]{:S(2)}) copy-start(s32[24,9]{0,1:T(8,128)} %param.12) | copy-start | bytes 2596
  6.1 6.1 %copy-start.4 = (s32[16]{0:T(128)S(1)}, s32[16]{0:T(128)}, u32[]{:S(2)}) copy-start(s32[16]{0:T(128)} %table_ref.1) | copy-start | bytes 196
  6.5 8.4 %collective-permute-start.3 = (bf16[1,288,128]{2,1,0:T(8,128)(2,1)S(1)}, bf16[1,288,128]{2,1,0:T(8,128)(2,1)S(1)}, u32[]{:S(2)}, u32[]{:S(2)}) collective-permute-start(bf16[1,288,128]{2,1,0:T(8,128)(2,1)S(1)} %bitcast.15), channel_id=1, source_target_pairs={{0,12},{2,14},{4,8},{6,10},{8,4},{10,6},{12,0},{14,2},{1,13},{3,15... | collective-permute-start | bytes 221192 | tf_op jit(solution)/shard_map/ppermute | solution.py:515
  11.5 6.4 %collective-permute-start.2 = (bf16[1,288,128]{2,1,0:T(8,128)(2,1)S(1)}, bf16[1,288,128]{2,1,0:T(8,128)(2,1)S(1)}, u32[]{:S(2)}, u32[]{:S(2)}) collective-permute-start(bf16[1,288,128]{2,1,0:T(8,128)(2,1)S(1)} %bitcast.16), channel_id=1, source_target_pairs={{0,8},{2,10},{4,12},{6,14},{8,0},{10,2},{12,4},{14,6},{1,9},{3,11}... | collective-permute-start | bytes 221192 | tf_op jit(solution)/shard_map/ppermute | solution.py:515
  11.5 6.4 %collective-permute-start.1 = (bf16[1,288,128]{2,1,0:T(8,128)(2,1)S(1)}, bf16[1,288,128]{2,1,0:T(8,128)(2,1)S(1)}, u32[]{:S(2)}, u32[]{:S(2)}) collective-permute-start(bf16[1,288,128]{2,1,0:T(8,128)(2,1)S(1)} %bitcast.17), channel_id=1, source_target_pairs={{0,4},{2,6},{4,0},{6,2},{8,12},{10,14},{12,8},{14,10},{1,5},{3,7},... | collective-permute-start | bytes 221192 | tf_op jit(solution)/shard_map/ppermute | solution.py:515
  13.2 6.2 %collective-permute-start.9 = (bf16[448,128]{1,0:T(8,128)(2,1)S(1)}, bf16[448,128]{1,0:T(8,128)(2,1)S(1)}, u32[]{:S(2)}, u32[]{:S(2)}) collective-permute-start(bf16[448,128]{1,0:T(8,128)(2,1)S(1)} %get-tuple-element.35.refs_9_), channel_id=1, source_target_pairs={{0,2},{2,0},{4,6},{6,4},{8,10},{10,8},{12,14},{14,12},{1,3},{3,1},... | collective-permute-start | bytes 344072 | tf_op jit(solution)/shard_map/ppermute | solution.py:515
  14.8 3.7 %collective-permute-start.4 = (bf16[1,288,128]{2,1,0:T(8,128)(2,1)S(1)}, bf16[1,288,128]{2,1,0:T(8,128)(2,1)S(1)}, u32[]{:S(2)}, u32[]{:S(2)}) collective-permute-start(bf16[1,288,128]{2,1,0:T(8,128)(2,1)S(1)} %bitcast.18), channel_id=1, source_target_pairs={{0,1},{1,0},{2,3},{3,2},{4,5},{5,4},{6,7},{7,6},{8,9},{9,8},{10,11... | collective-permute-start | bytes 221192 | tf_op jit(solution)/shard_map/ppermute | solution.py:511
  14.8 3.7 %collective-permute-start.7 = (bf16[1,288,128]{2,1,0:T(8,128)(2,1)S(1)}, bf16[1,288,128]{2,1,0:T(8,128)(2,1)S(1)}, u32[]{:S(2)}, u32[]{:S(2)}) collective-permute-start(bf16[1,288,128]{2,1,0:T(8,128)(2,1)S(1)} %collective-permute-done.3.refs_3_), channel_id=1, source_target_pairs={{0,1},{1,0},{2,3},{3,2},{4,5},{5,4},{6,7},{7,6},{8,9},{9,8},{10,11... | collective-permute-start | bytes 221192 | tf_op jit(solution)/shard_map/ppermute | solution.py:511
  18.0 1.3 %collective-permute-start.6 = (bf16[1,288,128]{2,1,0:T(8,128)(2,1)S(1)}, bf16[1,288,128]{2,1,0:T(8,128)(2,1)S(1)}, u32[]{:S(2)}, u32[]{:S(2)}) collective-permute-start(bf16[1,288,128]{2,1,0:T(8,128)(2,1)S(1)} %collective-permute-done.2.refs_2_), channel_id=1, source_target_pairs={{0,1},{1,0},{2,3},{3,2},{4,5},{5,4},{6,7},{7,6},{8,9},{9,8},{10,11... | collective-permute-start | bytes 221192 | tf_op jit(solution)/shard_map/ppermute | solution.py:511
  18.0 1.4 %collective-permute-start.5 = (bf16[1,288,128]{2,1,0:T(8,128)(2,1)S(1)}, bf16[1,288,128]{2,1,0:T(8,128)(2,1)S(1)}, u32[]{:S(2)}, u32[]{:S(2)}) collective-permute-start(bf16[1,288,128]{2,1,0:T(8,128)(2,1)S(1)} %collective-permute-done.1.refs_1_), channel_id=1, source_target_pairs={{0,1},{1,0},{2,3},{3,2},{4,5},{5,4},{6,7},{7,6},{8,9},{9,8},{10,11... | collective-permute-start | bytes 221192 | tf_op jit(solution)/shard_map/ppermute | solution.py:511
  21.3 3.7 %collective-permute-start.10 = (f32[8,128]{1,0:T(8,128)S(1)}, f32[8,128]{1,0:T(8,128)S(1)}, u32[]{:S(2)}, u32[]{:S(2)}) collective-permute-start(f32[8,128]{1,0:T(8,128)S(1)} %get-tuple-element.38.refs_14_), channel_id=1, source_target_pairs={{0,2},{2,0},{4,6},{6,4},{8,10},{10,8},{12,14},{14,12},{1,3},{3,1},... | collective-permute-start | bytes 12296 | tf_op jit(solution)/shard_map/ppermute | solution.py:515
  25.0 11.9 %copy-start = (bf16[24,32,2048]{2,1,0:T(8,128)(2,1)S(1)}, bf16[24,32,2048]{2,1,0:T(8,128)(2,1)}, u32[]{:S(2)}) copy-start(bf16[24,32,2048]{2,1,0:T(8,128)(2,1)} %param.7) | copy-start | bytes 9437188
  25.0 11.9 %copy-start.1 = (bf16[2,256,2048]{2,1,0:T(8,128)(2,1)S(1)}, bf16[2,256,2048]{2,1,0:T(8,128)(2,1)}, u32[]{:S(2)}) copy-start(bf16[2,256,2048]{2,1,0:T(8,128)(2,1)} %param.8) | copy-start | bytes 6291460
  27.3 8.2 %collective-permute-start.11 = (bf16[2,16,256]{2,1,0:T(8,128)(2,1)S(1)}, bf16[2,16,256]{2,1,0:T(8,128)(2,1)S(1)}, u32[]{:S(2)}, u32[]{:S(2)}) collective-permute-start(bf16[2,16,256]{2,1,0:T(8,128)(2,1)S(1)} %get-tuple-element.43), channel_id=1, source_target_pairs={{0,12},{2,14},{4,8},{6,10},{8,4},{10,6},{12,0},{14,2},{1,13},{3,15... | collective-permute-start | bytes 49160 | tf_op jit(solution)/shard_map/ppermute | solution.py:515
  29.9 5.5 %collective-permute-start.12 = (bf16[2,16,256]{2,1,0:T(8,128)(2,1)S(1)}, bf16[2,16,256]{2,1,0:T(8,128)(2,1)S(1)}, u32[]{:S(2)}, u32[]{:S(2)}) collective-permute-start(bf16[2,16,256]{2,1,0:T(8,128)(2,1)S(1)} %get-tuple-element.44), channel_id=1, source_target_pairs={{0,8},{2,10},{4,12},{6,14},{8,0},{10,2},{12,4},{14,6},{1,9},{3,11}... | collective-permute-start | bytes 49160 | tf_op jit(solution)/shard_map/ppermute | solution.py:515
  29.9 5.5 %collective-permute-start.13 = (bf16[2,16,256]{2,1,0:T(8,128)(2,1)S(1)}, bf16[2,16,256]{2,1,0:T(8,128)(2,1)S(1)}, u32[]{:S(2)}, u32[]{:S(2)}) collective-permute-start(bf16[2,16,256]{2,1,0:T(8,128)(2,1)S(1)} %get-tuple-element.45), channel_id=1, source_target_pairs={{0,4},{2,6},{4,0},{6,2},{8,12},{10,14},{12,8},{14,10},{1,5},{3,7},... | collective-permute-start | bytes 49160 | tf_op jit(solution)/shard_map/ppermute | solution.py:515
  31.7 3.7 %collective-permute-start.14 = (bf16[16,384]{1,0:T(8,128)(2,1)S(1)}, bf16[16,384]{1,0:T(8,128)(2,1)S(1)}, u32[]{:S(2)}, u32[]{:S(2)}) collective-permute-start(bf16[16,384]{1,0:T(8,128)(2,1)S(1)} %get-tuple-element.47), channel_id=1, source_target_pairs={{0,2},{2,0},{4,6},{6,4},{8,10},{10,8},{12,14},{14,12},{1,3},{3,1},... | collective-permute-start | bytes 36872 | tf_op jit(solution)/shard_map/ppermute | solution.py:515
  35.5 1.3 %collective-permute-start.15 = (f32[16,1280]{1,0:T(8,128)S(1)}, f32[16,1280]{1,0:T(8,128)S(1)}, u32[]{:S(2)}, u32[]{:S(2)}) collective-permute-start(f32[16,1280]{1,0:T(8,128)S(1)} %collect.1.mine_ref), channel_id=1, source_target_pairs={{0,1},{1,0},{2,3},{3,2},{4,5},{5,4},{6,7},{7,6},{8,9},{9,8},{10,11... | collective-permute-start | bytes 245768 | tf_op jit(solution)/shard_map/ppermute | solution.py:511
  38.1 4.3 %collective-permute-start.16 = (bf16[16,2176]{1,0:T(8,128)(2,1)S(1)}, bf16[16,2176]{1,0:T(8,128)(2,1)S(1)}, u32[]{:S(2)}, u32[]{:S(2)}) collective-permute-start(bf16[16,2176]{1,0:T(8,128)(2,1)S(1)} %grad_all.1), channel_id=1, source_target_pairs={{0,2},{2,0},{4,6},{6,4},{8,10},{10,8},{12,14},{14,12},{1,3},{3,1},... | collective-permute-start | bytes 208904 | tf_op jit(solution)/shard_map/ppermute | solution.py:515
  42.5 6.4 %collective-permute-start.19 = (bf16[16,2176]{1,0:T(8,128)(2,1)S(1)}, bf16[16,2176]{1,0:T(8,128)(2,1)S(1)}, u32[]{:S(2)}, u32[]{:S(2)}) collective-permute-start(bf16[16,2176]{1,0:T(8,128)(2,1)S(1)} %add_convert_fusion.a_ref), channel_id=1, source_target_pairs={{0,12},{2,14},{4,8},{6,10},{8,4},{10,6},{12,0},{14,2},{1,13},{3,15... | collective-permute-start | bytes 208904 | tf_op jit(solution)/shard_map/ppermute | solution.py:515
  45.1 5.9 %collective-permute-start.18 = (bf16[16,2176]{1,0:T(8,128)(2,1)S(1)}, bf16[16,2176]{1,0:T(8,128)(2,1)S(1)}, u32[]{:S(2)}, u32[]{:S(2)}) collective-permute-start(bf16[16,2176]{1,0:T(8,128)(2,1)S(1)} %add_convert_fusion.a_ref), channel_id=1, source_target_pairs={{0,8},{2,10},{4,12},{6,14},{8,0},{10,2},{12,4},{14,6},{1,9},{3,11}... | collective-permute-start | bytes 208904 | tf_op jit(solution)/shard_map/ppermute | solution.py:515
  45.1 5.9 %collective-permute-start.17 = (bf16[16,2176]{1,0:T(8,128)(2,1)S(1)}, bf16[16,2176]{1,0:T(8,128)(2,1)S(1)}, u32[]{:S(2)}, u32[]{:S(2)}) collective-permute-start(bf16[16,2176]{1,0:T(8,128)(2,1)S(1)} %add_convert_fusion.a_ref), channel_id=1, source_target_pairs={{0,4},{2,6},{4,0},{6,2},{8,12},{10,14},{12,8},{14,10},{1,5},{3,7},... | collective-permute-start | bytes 208904 | tf_op jit(solution)/shard_map/ppermute | solution.py:515

commit v5 on v4

--- a/solution.py
+++ b/solution.py
@@ -241,7 +241,7 @@
     qlen, qtok, plen, store, where, n_packs = cfg
     packs = refs[:n_packs]
     info_ref, mine_ref, other_ref = refs[n_packs : n_packs + 3]
-    stats_ref, total_ref, sums_ref, expo_ref, vqt_ref = refs[n_packs + 3 :]
+    stats_ref, total_ref, sums_ref, weights_ref, vqt_ref = refs[n_packs + 3 :]
     lo = info_ref[0]
     first_half, second_half = both_queries(lo, mine_ref, other_ref, slice(0, qtok))
     vqt_ref[:, :qtok] = jnp.transpose(first_half.astype(f32)).astype(bf16)
@@ -251,9 +251,10 @@
 
     def forward(pack, p, pos):
         expo = expo_of(pack[p, :plen, :], vqt_ref[...])
-        total_ref[pl.ds(pos, 1), :] = jnp.sum(expo, axis=0, keepdims=True)
+        total = jnp.sum(expo, axis=0, keepdims=True)
+        total_ref[pl.ds(pos, 1), :] = total
         if store:
-            expo_ref[pos] = expo.astype(bf16)
+            weights_ref[pos] = (expo * (1.0 / total)).astype(bf16)
         hi, core = where(info_ref, pos)
         here = (rows == ((hi * 2 + lo) * 2 + core).astype(f32)).astype(f32)
         stats_ref[1, pl.ds(pos, 1), :] = jnp.sum(here, axis=0, keepdims=True)
@@ -272,7 +273,7 @@
     qlen, qtok, plen, store, where, n_packs = cfg
     packs = refs[:n_packs]
     info_ref, mine_ref, other_ref, up_ref, stats_ref, total_ref, sums_ref, recv_ref = refs[n_packs : n_packs + 8]
-    expo_ref, unit_ref, vqt_ref = refs[n_packs + 8 : n_packs + 11]
+    weights_ref, unit_ref, vqt_ref = refs[n_packs + 8 : n_packs + 11]
     refs = refs[n_packs + 11 :]
     n_parts = n_packs // 2 if store else 1
     part_refs, (dmine_ref, dother_ref, gup_ref, loss_ref) = refs[:n_parts], refs[n_parts : n_parts + 4]
@@ -288,7 +289,7 @@
     loss_ref[...] = jnp.broadcast_to(jnp.log(summed) - (sums_ref[1:2, :] + recv_ref[1:2, :]), loss_ref.shape)
     dscore = (mult * jnp.exp(logits) / summed - first) * (1.0 / loss_temp)
     same = same_query((LANES, 2 * qtok), 1, qlen)
-    scale_ref[...] = sum(dot(part, same, NN) for part in parts_of(dscore, 2)) / (total_ref[...] * qlen)
+    scale_ref[...] = sum(dot(part, same, NN) for part in parts_of(dscore, 3))
 
     def scaled_low(pack, p):
         blocks = range(plen, plen + plen // LANES * rank, rank)
@@ -296,56 +297,60 @@
 
     def project_out(vp, dv):
         vpf = vp.astype(f32)
-        return (dv - vpf * jnp.sum(vpf * dv, axis=1, keepdims=True)).astype(bf16)
+        return parts_of(dv - vpf * jnp.sum(vpf * dv, axis=1, keepdims=True), 2)
 
     if store:
         for pos in range(n_packs):
             rows = slice(pos * plen, (pos + 1) * plen)
-            grad_ref[rows, :] = (expo_ref[pos].astype(f32) * scale_ref[pos : pos + 1, :]).astype(bf16)
+            grad_ref[rows, :] = (weights_ref[pos].astype(f32) * (scale_ref[pos : pos + 1, :] * (1.0 / qlen))).astype(bf16)
             dv_ref[rows, :] = dot(grad_ref[rows, :], vq, NN)
-            dvqt = unit_ref[pos] * scale_ref[pos : pos + 1, :]
+            dvqt = unit_ref[pos].astype(f32) * scale_ref[pos : pos + 1, :]
             dvqt_ref[...] = dvqt if pos == 0 else dvqt_ref[...] + dvqt
         for pos, pack in enumerate(packs):
             rows = slice(pos * plen, (pos + 1) * plen)
             dv = project_out(pack[0, :plen, :], dv_ref[rows, :])
-            dvb_ref[rows, :] = dv
-            part_refs[pos % n_parts][where(info_ref, pos)[1]] = dot(up, dv, NT).astype(bf16)
+            dvb_ref[0, rows, :], dvb_ref[1, rows, :] = dv
+            part_refs[pos % n_parts][where(info_ref, pos)[1]] = (dot(up, dv[0], NT) + dot(up, dv[1], NT))
         lows = jnp.concatenate([scaled_low(pack, 0) for pack in packs], axis=1)
-        gup = dot(lows, dvb_ref[...], NN)
+        gup = dot(lows, dvb_ref[0], NN) + dot(lows, dvb_ref[1], NN)
     else:
         dvqt_ref[...] = jnp.zeros_like(dvqt_ref)
         gup_ref[...] = jnp.zeros_like(gup_ref)
 
         def backward(pack, p, pos):
             vp = pack[p, :plen, :]
-            grad = (expo_of(vp, vqt_ref[...]) * scale_ref[pl.ds(pos, 1), :]).astype(bf16)
-            dvqt_ref[...] += dot(vp, grad, TN)
+            scale = scale_ref[pl.ds(pos, 1), :]
+            weights = (expo_of(vp, vqt_ref[...]) * (1.0 / total_ref[pl.ds(pos, 1), :])).astype(bf16)
+            unit = (dot(vp, weights, TN) * (1.0 / qlen)).astype(bf16)
+            dvqt_ref[...] += unit.astype(f32) * scale
+            grad = (weights.astype(f32) * (scale * (1.0 / qlen))).astype(bf16)
             dv = project_out(vp, dot(grad, vq, NN))
             hi, core = where(info_ref, pos)
-            part_refs[0][hi, core] = dot(up, dv, NT).astype(bf16)
-            gup_ref[...] += dot(scaled_low(pack, p), dv, NN)
+            part_refs[0][hi, core] = (dot(up, dv[0], NT) + dot(up, dv[1], NT))
+            low = scaled_low(pack, p)
+            gup_ref[...] += dot(low, dv[0], NN) + dot(low, dv[1], NN)
 
         over_packs(packs, backward)
         gup = gup_ref[...]
 
     vqt = vqt_ref[...].astype(f32)
     dvqt = dvqt_ref[...]
-    dvqt = (dvqt - vqt * jnp.sum(vqt * dvqt, axis=0, keepdims=True)).astype(bf16)
-    dlow = dot(up, dvqt, NN)
+    dvqt = parts_of(dvqt - vqt * jnp.sum(vqt * dvqt, axis=0, keepdims=True), 2)
+    dlow = dot(up, dvqt[0], NN) + dot(up, dvqt[1], NN)
     dmine_ref[...] = jnp.where(lo == 0, dlow[:, :qtok], dlow[:, qtok:])
-    dother_ref[...] = jnp.where(lo == 0, dlow[:, qtok:], dlow[:, :qtok]).astype(bf16)
+    dother_ref[...] = jnp.where(lo == 0, dlow[:, qtok:], dlow[:, :qtok])
     lows = [
         both_queries(lo, mine_ref, other_ref, slice(at, at + rank))
         for at in range(qtok, qtok + qtok // LANES * rank, rank)
     ]
     lows = jnp.concatenate([low[0] for low in lows] + [low[1] for low in lows], axis=1)
-    gup_ref[...] = gup + dot(lows, dvqt, NT)
+    gup_ref[...] = gup + dot(lows, dvqt[0], NT) + dot(lows, dvqt[1], NT)
 
 
 def places(steps):
     def where(info_ref, pos):
         n = len(steps)
-        if n <= 8:
+        if n == 4:
             return jnp.bitwise_xor(info_ref[1], steps[pos % n]), info_ref[2] if pos < n else 1 - info_ref[2]
         return lax.rem(pos, n), jnp.where(pos < n, info_ref[2], 1 - info_ref[2])
 
@@ -373,33 +378,33 @@
     )(*packs, info, mine, other)
 
 
-def unit_kernel(plen, *refs):
-    packs, (expo_ref, unit_ref) = refs[:-2], refs[-2:]
+def unit_kernel(qlen, plen, *refs):
+    packs, (weights_ref, unit_ref) = refs[:-2], refs[-2:]
     for pos, pack in enumerate(packs):
-        unit_ref[pos] = dot(pack[0, :plen, :], expo_ref[pos], TN)
-
-
-def unit_of(packs, expo):
-    npos, plen, ntok = expo.shape
+        unit_ref[pos] = (dot(pack[0, :plen, :], weights_ref[pos], TN) * (1.0 / qlen)).astype(bf16)
+
+
+def unit_of(packs, weights, qlen):
+    npos, plen, ntok = weights.shape
     if npos != len(packs):
-        return jnp.zeros((1, 8, LANES), f32)
-    return pl.pallas_call(
-        functools.partial(unit_kernel, plen),
+        return jnp.zeros((1, 16, LANES), bf16)
+    return pl.pallas_call(
+        functools.partial(unit_kernel, qlen, plen),
         in_specs=[VMEM] * (npos + 1),
         out_specs=VMEM,
-        out_shape=jax.ShapeDtypeStruct((npos, LANES, ntok), f32),
+        out_shape=jax.ShapeDtypeStruct((npos, LANES, ntok), bf16),
         compiler_params=pltpu.CompilerParams(vmem_limit_bytes=4 * 2**20),
         cost_estimate=cost(1.2),
         name="unit",
-    )(*packs, expo)
-
-
-def score_backward(packs, steps, info, mine, other, up, stats, total, sums, recv, expo, unit, vqt, qlen, qtok, plen):
+    )(*packs, weights)
+
+
+def score_backward(packs, steps, info, mine, other, up, stats, total, sums, recv, weights, unit, vqt, qlen, qtok, plen):
     npos, rank = 2 * len(steps), up.shape[0]
     store = len(packs) == npos
     cfg = (qlen, qtok, plen, store, places(steps), len(packs))
-    part = jax.ShapeDtypeStruct((2, rank, plen), bf16)
-    whole = jax.ShapeDtypeStruct((len(steps), 2, rank, plen), bf16)
+    part = jax.ShapeDtypeStruct((2, rank, plen), f32)
+    whole = jax.ShapeDtypeStruct((len(steps), 2, rank, plen), f32)
     kept = npos * plen if store else 16
     parts = (part,) * len(steps) if store else (whole,)
     return pl.pallas_call(
@@ -409,7 +414,7 @@
         out_shape=(
             *parts,
             jax.ShapeDtypeStruct((rank, qtok), f32),
-            jax.ShapeDtypeStruct((rank, qtok), bf16),
+            jax.ShapeDtypeStruct((rank, qtok), f32),
             jax.ShapeDtypeStruct((rank, LANES), f32),
             jax.ShapeDtypeStruct((8, LANES), f32),
         ),
@@ -418,12 +423,12 @@
             pltpu.VMEM((LANES, 2 * qtok), f32),
             pltpu.VMEM((kept, 2 * qtok), bf16),
             pltpu.VMEM((kept, LANES), f32),
-            pltpu.VMEM((kept, LANES), bf16),
+            pltpu.VMEM((2, kept, LANES), bf16),
         ],
         compiler_params=pltpu.CompilerParams(vmem_limit_bytes=(20 if store else 40) * 2**20),
         cost_estimate=cost(2.5),
         name="score_backward",
-    )(*packs, info, mine, other, up, stats, total, sums, recv, expo, unit, vqt)
+    )(*packs, info, mine, other, up, stats, total, sums, recv, weights, unit, vqt)
 
 
 def collect_kernel(n, *refs):
@@ -464,9 +469,9 @@
         p_dlow.append(((mine_ref[:, rows] + other_ref[:, rows]) * r).astype(bf16))
     total = dot(jnp.concatenate(q_dlow, axis=1), q_ref[...], NN)
     total += dot(jnp.concatenate(p_dlow, axis=1), p_ref[...], NN)
-    out_ref[:, :width] = total.astype(bf16)
+    out_ref[:, :width] = total
     ups = slice(2 * plen + qtok, 2 * plen + qtok + LANES)
-    out_ref[:, width:] = (mine_ref[:, ups] + other_ref[:, ups]).astype(bf16)
+    out_ref[:, width:] = (mine_ref[:, ups] + other_ref[:, ups])
 
 
 def grad_all(info, passage_rows, query_rows, mine, other, plen, qtok):
@@ -475,36 +480,11 @@
         functools.partial(grad_kernel, plen, qtok),
         in_specs=[SMEM] + [VMEM] * 4,
         out_specs=VMEM,
-        out_shape=jax.ShapeDtypeStruct((rank, width + LANES), bf16),
+        out_shape=jax.ShapeDtypeStruct((rank, width + LANES), f32),
         compiler_params=pltpu.CompilerParams(vmem_limit_bytes=4 * 2**20),
         cost_estimate=cost(1.3),
         name="grad_all",
     )(info, passage_rows, query_rows, mine, other)
-
-
-def add_kernel(a_ref, b_ref, c_ref, d_ref, down_ref, up_ref):
-    total = (a_ref[...].astype(f32) + b_ref[...].astype(f32)) + (
-        c_ref[...].astype(f32) + d_ref[...].astype(f32)
-    )
-    width = down_ref.shape[1]
-    down_ref[...] = total[:, :width]
-    up_ref[...] = total[:, width:]
-
-
-def add_four(parts, width):
-    rank = parts[0].shape[0]
-    return pl.pallas_call(
-        add_kernel,
-        in_specs=[VMEM] * 4,
-        out_specs=[VMEM] * 2,
-        out_shape=(
-            jax.ShapeDtypeStruct((rank, width), f32),
-            jax.ShapeDtypeStruct((rank, LANES), f32),
-        ),
-        compiler_params=pltpu.CompilerParams(vmem_limit_bytes=4 * 2**20),
-        cost_estimate=cost(0.7),
-        name="add_four",
-    )(*parts)
 
 
 def swap(x):
@@ -531,12 +511,37 @@
     return [parts[0]] + [across(part, nshard, 2 * step) for part, step in reversed([*zip(parts, steps, strict=True)][1:])]
 
 
+def power_of_two(exponent):
+    power = jnp.ones_like(exponent)
+    for sign in (1, -1):
+        digits = jnp.maximum(sign * exponent, 0.0).astype(jnp.int32)
+        for k in range(7):
+            power = power * jnp.where((digits >> k) % 2 == 1, 2.0 ** (sign * 2**k), 1.0)
+    return power
+
+
+def coded(x):
+    largest = jnp.max(jnp.abs(x), axis=1, keepdims=True)
+    exponent = jnp.ceil(jnp.log2(jnp.clip(largest, 1e-20, 1e30))) - 14.0
+    held = jnp.broadcast_to(exponent, (x.shape[0], LANES))
+    scaled = jnp.concatenate([x * power_of_two(-exponent), held], axis=1)
+    return scaled.astype(jnp.float16)
+
+
+def decoded(x):
+    x = x.astype(f32)
+    return x[:, :-LANES] * power_of_two(x[:, -LANES : 1 - LANES])
+
+
 def sum_over_shards(x, nshard, width):
     if nshard != 8:
-        x = lax.psum(x.astype(f32), "shard")
+        x = lax.psum(x, "shard")
         return x[:, :width], x[:, width:]
-    x = (x.astype(f32) + across(x, nshard, 1).astype(f32)).astype(bf16)
-    return add_four([x] + [across(x, nshard, k) for k in (2, 4, 6)], width)
+    x = coded(x)
+    x = coded(decoded(x) + decoded(across(x, nshard, 1)))
+    a, b, c = (decoded(across(x, nshard, k)) for k in (6, 4, 2))
+    x = (decoded(x) + c) + (a + b)
+    return x[:, :width], x[:, width:]
 
 
 def per_device(
@@ -571,7 +576,7 @@
     other = across(mine, nshard, 1)
     packs, steps = gather_packs(ppack, nshard, groups)
 
-    stats, total, sums, expo, vqt = score_forward(packs, steps, info, mine, other, qlen, qtok, plen)
+    stats, total, sums, weights, vqt = score_forward(packs, steps, info, mine, other, qlen, qtok, plen)
     *parts, dlow_mine, dlow_other, gup, loss = score_backward(
         packs,
         steps,
@@ -583,8 +588,8 @@
         total,
         sums,
         across(sums, nshard, 1),
-        expo,
-        unit_of(packs, expo),
+        weights,
+        unit_of(packs, weights, qlen),
         vqt,
         qlen,
         qtok,
@@ -593,8 +598,9 @@
     parts = exchange_parts(parts, steps, nshard, groups)
     collected = collect(parts, dlow_mine, across(dlow_other, nshard, 1), r_q, r_p, gup)
     grads = grad_all(info, passage_rows, query_rows, collected, swap(collected), plen, qtok)
+    loss, _ = lax.optimization_barrier((loss, grads))
+    down_sum, up_sum = sum_over_shards(grads, nshard, width)
     query_loss = lax.dynamic_slice_in_dim(loss[0], info[0] * half, half, 0)
-    down_sum, up_sum = sum_over_shards(grads, nshard, width)
     return (query_loss, jnp.transpose(down_sum), up_sum)
 
 

time: 51.8 us -> 56.5 us (1.091)
  local copies, waits for them, and re-layouts: 0.6 us -> 3.61 us
  other arithmetic: 0.1 us -> 1.93 us
    unnamed x10, local copies, waits for them, and re-layouts: 0.02 us -> 1.61 us
    mul x0 -> x8, other arithmetic: none -> 1.15 us  [power_of_two(): power * jnp.where((digits >> k) % 2 == 1, 2.0 ** (sign * 2 ** k), 1.0)]
    pallas_call x2 -> x1, Pallas kernels: 1.31 us -> 0.62 us  [unit_of(): pl.pallas_call(functools.partial(unit_kernel, qlen, plen), in_specs=[VMEM...]
    transpose x0 -> x1, local copies, waits for them, and re-layouts: none -> 0.66 us  [per_device(): return (query_loss, jnp.transpose(down_sum), up_sum)]
    slice x0 -> x1, local copies, waits for them, and re-layouts: none -> 0.6 us  [sum_over_shards(): return (x[:, :width], x[:, width:])]
  transfers between devices with their start and end apart: 20 -> 20, of which waited for: 9 -> 9; matrix products, arithmetic and copies ran while one was open for 1% -> 2% of each run, Pallas kernels for 6% -> 5%
where the time goes in v5:
time: 56.5 us; the launch traced here: 56.3 us
  starting transfers between devices  22.6 us (40%)
  waiting for transfers between devices  14.4 us (25%)
  Pallas kernels  13 us (23%)
  local copies, waits for them, and re-layouts  3.61 us (6%)
  other arithmetic  1.93 us (3%)
  between operations  0.81 us (1%)
    ppermute x13, starting transfers between devices, across(): return lax.ppermute(x, 'shard', [(i, i ^ step) for i in range(nshard)])  20.9 us
    ppermute x13, waiting for transfers between devices, across(): return lax.ppermute(x, 'shard', [(i, i ^ step) for i in range(nshard)])  12.2 us
    pallas_call x1, Pallas kernels, project_passages(): pl.pallas_call(project_passages_kernel, in_specs=[SMEM] + [HBM] * 4, out_...  3.71 us
    pallas_call x1, Pallas kernels, score_backward(): pl.pallas_call(functools.partial(backward_kernel, cfg), in_specs=[VMEM] *...  2.53 us
    pallas_call x1, Pallas kernels, score_forward(): pl.pallas_call(functools.partial(forward_kernel, cfg), in_specs=[VMEM] *...  2.44 us
    ppermute x7, waiting for transfers between devices, swap(): return lax.ppermute(x, 'sub', [(0, 1), (1, 0)])  2.17 us
    ppermute x7, starting transfers between devices, swap(): return lax.ppermute(x, 'sub', [(0, 1), (1, 0)])  1.71 us
    unnamed x10, local copies, waits for them, and re-layouts  1.61 us
  transfers between devices with their start and end apart: 20, of which 9 were waited for; matrix products, arithmetic and copies ran while one was open for 2% of the time, Pallas kernels for 5%

profile of v5, /device:TPU:0, one launch (start us, length us, event | category | flops | bytes accessed | tf_op | source)
XLA Modules:
  0.0 56.3 jit_solution(1946629633010472937)
XLA Ops:
  0.6 0.1 pad_add_fusion.info_ref.refs_8_
  0.7 3.7 %project_passages.1 = (f32[288,128]{1,0:T(8,128)S(1)}, f32[288,128]{1,0:T(8,128)S(1)}, bf16[768,2048]{1,0:T(8,128)(2,1)S(1)}, bf16[2048,256]{1,0:T(8,128)(2,1)S(1)}) custom-call(s32[3]{0:T(128)S(1)} %pad_add_fusion.info_ref.refs_8_, bf16[512,2048]{1,0:T(8,128)(2,1)} %bitcast.14, bf16[768,2048]{1,0:T(8,128)(2,1)} %bitcast.12, bf16[2048,128]{1,0:T(8,128)(2,1)} %proj_hbm.1, ...), custom_call_target="tpu_custom_call" | custom-call | flops 4070000128 | bytes 12950000 | tf_op jit(solution)/shard_map/project_passages/pallas_call | solution.py:89
  4.5 0.5 collective-permute-start
  5.0 1.0 %project_queries.1 = (f32[432,128]{1,0:T(8,128)S(1)}, f32[432,128]{1,0:T(8,128)S(1)}) custom-call(bf16[768,2048]{1,0:T(8,128)(2,1)S(1)} %get-tuple-element.30.q_ref, bf16[2048,256]{1,0:T(8,128)(2,1)S(1)} %get-tuple-element.31.weight_ref), custom_call_target="tpu_custom_call" | custom-call | flops 1650000000 | bytes 5250000 | tf_op jit(solution)/shard_map/project_queries/pallas_call | solution.py:117
  6.0 0.1 collective-permute-start.8
  6.1 0.3 pack_passage.1
  6.5 5.1 %collective-permute-start.3 = (bf16[1,288,128]{2,1,0:T(8,128)(2,1)S(1)}, bf16[1,288,128]{2,1,0:T(8,128)(2,1)S(1)}, u32[]{:S(2)}, u32[]{:S(2)}) collective-permute-start(bf16[1,288,128]{2,1,0:T(8,128)(2,1)S(1)} %bitcast.16), channel_id=1, source_target_pairs={{0,12},{2,14},{4,8},{6,10},{8,4},{10,6},{12,0},{14,2},{1,13},{3,15... | collective-permute-start | bytes 221192 | tf_op jit(solution)/shard_map/ppermute | solution.py:495
  11.5 0.6 %collective-permute-start.1 = (bf16[1,288,128]{2,1,0:T(8,128)(2,1)S(1)}, bf16[1,288,128]{2,1,0:T(8,128)(2,1)S(1)}, u32[]{:S(2)}, u32[]{:S(2)}) collective-permute-start(bf16[1,288,128]{2,1,0:T(8,128)(2,1)S(1)} %bitcast.18), channel_id=1, source_target_pairs={{0,4},{2,6},{4,0},{6,2},{8,12},{10,14},{12,8},{14,10},{1,5},{3,7},... | collective-permute-start | bytes 221192 | tf_op jit(solution)/shard_map/ppermute | solution.py:495
  12.2 1.0 %pack_queries.1 = (bf16[448,128]{1,0:T(8,128)(2,1)S(1)}, f32[8,384]{1,0:T(8,128)S(1)}) custom-call(s32[3]{0:T(128)S(1)} %pad_add_fusion.info_ref.refs_8_, s32[16]{0:T(128)S(1)} %copy-done.4, s32[9,24]{1,0:T(8,128)S(1)} %bitcast.23, f32[432,128]{1,0:T(8,128)S(1)} %get-tuple-element.32.keep_ref, f32[432,128]{1,0:T(8,128)S(1)} %collective-permute-done.8.recv_ref, ...), custom_call_target="tpu_custom_call" | custom-call | flops 990000000 | bytes 3150000 | tf_op jit(solution)/shard_map/pack_queries/pallas_call | solution.py:192
  13.1 1.7 %collective-permute-start.9 = (bf16[448,128]{1,0:T(8,128)(2,1)S(1)}, bf16[448,128]{1,0:T(8,128)(2,1)S(1)}, u32[]{:S(2)}, u32[]{:S(2)}) collective-permute-start(bf16[448,128]{1,0:T(8,128)(2,1)S(1)} %get-tuple-element.34.refs_9_), channel_id=1, source_target_pairs={{0,2},{2,0},{4,6},{6,4},{8,10},{10,8},{12,14},{14,12},{1,3},{3,1},... | collective-permute-start | bytes 344072 | tf_op jit(solution)/shard_map/ppermute | solution.py:495
  14.8 0.5 collective-permute-start.7
  15.3 2.6 %collective-permute-done.2.refs_2_ = bf16[1,288,128]{2,1,0:T(8,128)(2,1)S(1)} collective-permute-done((bf16[1,288,128]{2,1,0:T(8,128)(2,1)S(1)}, bf16[1,288,128]{2,1,0:T(8,128)(2,1)S(1)}, u32[]{:S(2)}, u32[]{:S(2)}) %collective-permute-start.2) | collective-permute-done | bytes 73760 | tf_op jit(solution)/shard_map/ppermute | solution.py:495
  18.0 0.5 collective-permute-start.5
  18.5 0.7 %collective-permute-done.6.refs_6_ = bf16[1,288,128]{2,1,0:T(8,128)(2,1)S(1)} collective-permute-done((bf16[1,288,128]{2,1,0:T(8,128)(2,1)S(1)}, bf16[1,288,128]{2,1,0:T(8,128)(2,1)S(1)}, u32[]{:S(2)}, u32[]{:S(2)}) %collective-permute-start.6) | collective-permute-done | bytes 73760 | tf_op jit(solution)/shard_map/ppermute | solution.py:491
  19.2 0.2 collective-permute-done.5.refs_5_
  19.4 2.4 %score_forward.1 = (f32[3,8,128]{2,1,0:T(8,128)S(1)}, f32[8,768]{1,0:T(8,128)S(1)}, f32[8,128]{1,0:T(8,128)S(1)}, bf16[8,256,768]{2,1,0:T(8,128)(2,1)S(1)}, bf16[128,768]{1,0:T(8,128)(2,1)S(1)}) custom-call(bf16[1,288,128]{2,1,0:T(8,128)(2,1)S(1)} %bitcast.20, bf16[1,288,128]{2,1,0:T(8,128)(2,1)S(1)} %collective-permute-done.1.refs_1_, ...), custom_call_target="tpu_custom_call" | custom-call | flops 2090000000 | bytes 6650000 | tf_op jit(solution)/shard_map/score_forward/pallas_call | solution.py:364
  21.8 1.6 %collective-permute-start.10 = (f32[8,128]{1,0:T(8,128)S(1)}, f32[8,128]{1,0:T(8,128)S(1)}, u32[]{:S(2)}, u32[]{:S(2)}) collective-permute-start(f32[8,128]{1,0:T(8,128)S(1)} %get-tuple-element.37.refs_14_), channel_id=1, source_target_pairs={{0,2},{2,0},{4,6},{6,4},{8,10},{10,8},{12,14},{14,12},{1,3},{3,1},... | collective-permute-start | bytes 12296 | tf_op jit(solution)/shard_map/ppermute | solution.py:495
  23.4 0.6 %unit.1.refs_17_ = bf16[8,128,768]{2,1,0:T(8,128)(2,1)S(1)} custom-call(bf16[1,288,128]{2,1,0:T(8,128)(2,1)S(1)} %bitcast.21, bf16[1,288,128]{2,1,0:T(8,128)(2,1)S(1)} %collective-permute-done.1.refs_1_, bf16[1,288,128]{2,1,0:T(8,128)(2,1)S(1)} %collective-permute-done.2.refs_2_, bf16[1,288,128]{2,1,0:T(8,128)(2,1)S(1)} %collective-permute-done.3.refs_3_, ...), custom_call_target="tpu_custom_call" | custom-call | flops 1320000000 | bytes 4200000 | tf_op jit(solution)/shard_map/unit/pallas_call | solution.py:391
  24.0 1.5 %collective-permute-done.10.refs_15_ = f32[8,128]{1,0:T(8,128)S(1)} collective-permute-done((f32[8,128]{1,0:T(8,128)S(1)}, f32[8,128]{1,0:T(8,128)S(1)}, u32[]{:S(2)}, u32[]{:S(2)}) %collective-permute-start.10) | collective-permute-done | bytes 4128 | tf_op jit(solution)/shard_map/ppermute | solution.py:495
  25.5 2.5 %score_backward.1 = (f32[2,16,256]{2,1,0:T(8,128)S(1)}, f32[2,16,256]{2,1,0:T(8,128)S(1)}, f32[2,16,256]{2,1,0:T(8,128)S(1)}, f32[2,16,256]{2,1,0:T(8,128)S(1)},...) custom-call(bf16[1,288,128]{2,1,0:T(8,128)(2,1)S(1)} %bitcast.22, ...), custom_call_target="tpu_custom_call" | custom-call | flops 2750000128 | bytes 8750000 | tf_op jit(solution)/shard_map/score_backward/pallas_call | solution.py:410
  28.0 2.6 %collective-permute-start.11 = (f32[2,16,256]{2,1,0:T(8,128)S(1)}, f32[2,16,256]{2,1,0:T(8,128)S(1)}, u32[]{:S(2)}, u32[]{:S(2)}) collective-permute-start(f32[2,16,256]{2,1,0:T(8,128)S(1)} %get-tuple-element.42), channel_id=1, source_target_pairs={{0,12},{2,14},{4,8},{6,10},{8,4},{10,6},{12,0},{14,2},{1,13},{3,15... | collective-permute-start | bytes 98312 | tf_op jit(solution)/shard_map/ppermute | solution.py:495
  30.6 1.8 %collective-permute-start.13 = (f32[2,16,256]{2,1,0:T(8,128)S(1)}, f32[2,16,256]{2,1,0:T(8,128)S(1)}, u32[]{:S(2)}, u32[]{:S(2)}) collective-permute-start(f32[2,16,256]{2,1,0:T(8,128)S(1)} %get-tuple-element.44), channel_id=1, source_target_pairs={{0,4},{2,6},{4,0},{6,2},{8,12},{10,14},{12,8},{14,10},{1,5},{3,7},... | collective-permute-start | bytes 98312 | tf_op jit(solution)/shard_map/ppermute | solution.py:495
  32.5 1.5 %collective-permute-start.14 = (f32[16,384]{1,0:T(8,128)S(1)}, f32[16,384]{1,0:T(8,128)S(1)}, u32[]{:S(2)}, u32[]{:S(2)}) collective-permute-start(f32[16,384]{1,0:T(8,128)S(1)} %get-tuple-element.46), channel_id=1, source_target_pairs={{0,2},{2,0},{4,6},{6,4},{8,10},{10,8},{12,14},{14,12},{1,3},{3,1},... | collective-permute-start | bytes 73736 | tf_op jit(solution)/shard_map/ppermute | solution.py:495
  34.0 2.3 %collective-permute-done.14.refs_5_ = f32[16,384]{1,0:T(8,128)S(1)} collective-permute-done((f32[16,384]{1,0:T(8,128)S(1)}, f32[16,384]{1,0:T(8,128)S(1)}, u32[]{:S(2)}, u32[]{:S(2)}) %collective-permute-start.14) | collective-permute-done | bytes 24608 | tf_op jit(solution)/shard_map/ppermute | solution.py:495
  36.4 1.3 %collective-permute-done.15.other_ref = f32[16,1280]{1,0:T(8,128)S(1)} collective-permute-done((f32[16,1280]{1,0:T(8,128)S(1)}, f32[16,1280]{1,0:T(8,128)S(1)}, u32[]{:S(2)}, u32[]{:S(2)}) %collective-permute-start.15) | collective-permute-done | bytes 81952 | tf_op jit(solution)/shard_map/ppermute | solution.py:491
  37.7 1.6 %copy-done.1 = bf16[2,256,2048]{2,1,0:T(8,128)(2,1)S(1)} copy-done((bf16[2,256,2048]{2,1,0:T(8,128)(2,1)S(1)}, bf16[2,256,2048]{2,1,0:T(8,128)(2,1)}, u32[]{:S(2)}) %copy-start.1) | copy-done | bytes 2097176
  39.3 1.3 %grad_all.1 = f32[16,2176]{1,0:T(8,128)S(1)} custom-call(s32[3]{0:T(128)S(1)} %pad_add_fusion.info_ref.refs_8_, bf16[512,2048]{1,0:T(8,128)(2,1)S(1)} %bitcast.15, bf16[768,2048]{1,0:T(8,128)(2,1)S(1)} %bitcast.13, f32[16,1280]{1,0:T(8,128)S(1)} %collect.1.mine_ref, f32[16,1280]{1,0:T(8,128)S(1)} %collective-permute-done.15.other_ref), custom_call_target="tpu_custom_call" | custom-call | flops 1430000000 | bytes 4550000 | tf_op jit(solution)/shard_map/grad_all/pallas_call | solution.py:479
  40.6 0.1 abs_reduce_fusion.1
  40.8 0.1 multiply_convert_fusion.1
  40.9 0.1 broadcast_in_dim.317
  41.0 0.2 multiply_reduce_fusion.5
  41.2 1.6 %collective-permute-start.16 = (f16[16,2304]{1,0:T(8,128)(2,1)S(1)}, f16[16,2304]{1,0:T(8,128)(2,1)S(1)}, u32[]{:S(2)}, u32[]{:S(2)}) collective-permute-start(f16[16,2304]{1,0:T(8,128)(2,1)S(1)} %get-tuple-element.54), channel_id=1, source_target_pairs={{0,2},{2,0},{4,6},{6,4},{8,10},{10,8},{12,14},{14,12},{1,3},{3,1},... | collective-permute-start | bytes 221192 | tf_op jit(solution)/shard_map/ppermute | solution.py:495
  42.7 0.6 %dynamic-slice_bitcast_fusion = f32[12]{0:T(128)} fusion(f32[1,128]{1,0:T(1,128)S(1)} %slice.45, s32[]{:T(128)S(6)} %select_n.1083), kind=kLoop, calls=%fused_computation.660 | loop fusion | bytes 100 | tf_op jit(solution)/shard_map/dynamic_slice | solution.py:603
  43.3 2.3 %collective-permute-done.16 = f16[16,2304]{1,0:T(8,128)(2,1)S(1)} collective-permute-done((f16[16,2304]{1,0:T(8,128)(2,1)S(1)}, f16[16,2304]{1,0:T(8,128)(2,1)S(1)}, u32[]{:S(2)}, u32[]{:S(2)}) %collective-permute-start.16) | collective-permute-done | bytes 73760 | tf_op jit(solution)/shard_map/ppermute | solution.py:495
  45.6 0.2 multiply_reduce_fusion.4
  45.8 0.2 abs_reduce_fusion
  46.0 0.1 multiply_convert_fusion
  46.2 2.6 %collective-permute-start.18 = (f16[16,2304]{1,0:T(8,128)(2,1)S(1)}, f16[16,2304]{1,0:T(8,128)(2,1)S(1)}, u32[]{:S(2)}, u32[]{:S(2)}) collective-permute-start(f16[16,2304]{1,0:T(8,128)(2,1)S(1)} %get-tuple-element.52), channel_id=1, source_target_pairs={{0,12},{2,14},{4,8},{6,10},{8,4},{10,6},{12,0},{14,2},{1,13},{3,15... | collective-permute-start | bytes 221192 | tf_op jit(solution)/shard_map/ppermute | solution.py:495
  48.8 1.8 %collective-permute-start.19 = (f16[16,2304]{1,0:T(8,128)(2,1)S(1)}, f16[16,2304]{1,0:T(8,128)(2,1)S(1)}, u32[]{:S(2)}, u32[]{:S(2)}) collective-permute-start(f16[16,2304]{1,0:T(8,128)(2,1)S(1)} %get-tuple-element.52), channel_id=1, source_target_pairs={{0,8},{2,10},{4,12},{6,14},{8,0},{10,2},{12,4},{14,6},{1,9},{3,11}... | collective-permute-start | bytes 221192 | tf_op jit(solution)/shard_map/ppermute | solution.py:495
  50.7 0.2 multiply_reduce_fusion.3
  50.9 2.0 %collective-permute-done.18 = f16[16,2304]{1,0:T(8,128)(2,1)S(1)} collective-permute-done((f16[16,2304]{1,0:T(8,128)(2,1)S(1)}, f16[16,2304]{1,0:T(8,128)(2,1)S(1)}, u32[]{:S(2)}, u32[]{:S(2)}) %collective-permute-start.18) | collective-permute-done | bytes 73760 | tf_op jit(solution)/shard_map/ppermute | solution.py:495
  52.8 0.2 multiply_reduce_fusion.1
  53.0 1.5 %collective-permute-done.17 = f16[16,2304]{1,0:T(8,128)(2,1)S(1)} collective-permute-done((f16[16,2304]{1,0:T(8,128)(2,1)S(1)}, f16[16,2304]{1,0:T(8,128)(2,1)S(1)}, u32[]{:S(2)}, u32[]{:S(2)}) %collective-permute-start.17) | collective-permute-done | bytes 73760 | tf_op jit(solution)/shard_map/ppermute | solution.py:495
  54.5 0.2 multiply_reduce_fusion.2
  54.7 0.2 multiply_reduce_fusion
  54.9 0.1 fusion.1
  55.0 0.6 %slice.73 = f32[16,128]{1,0:T(8,128)} slice(f32[16,2176]{1,0:T(8,128)S(1)} %fusion.1), slice={[0:16], [2048:2176]} | slice | bytes 16384 | tf_op jit(solution)/shard_map/slice | solution.py:544
  55.6 0.7 %slice_bitcast_fusion = f32[2048,16]{0,1:T(8,128)} fusion(f32[16,2176]{1,0:T(8,128)S(1)} %fusion.1), kind=kLoop, calls=%fused_computation.14 | loop fusion | bytes 262144 | tf_op jit(solution)/shard_map/transpose | solution.py:604
  (37 shorter events, 0.4 us)
Async XLA Ops:
  4.4 1.7 %copy-start.3 = (bf16[16,128]{1,0:T(8,128)(2,1)S(1)}, bf16[16,128]{1,0:T(8,128)(2,1)}, u32[]{:S(2)}) copy-start(bf16[16,128]{1,0:T(8,128)(2,1)} %refs_11_.1) | copy-start | bytes 12292
  4.5 1.6 %collective-permute-start = (f32[288,128]{1,0:T(8,128)S(1)}, f32[288,128]{1,0:T(8,128)S(1)}, u32[]{:S(2)}, u32[]{:S(2)}) collective-permute-start(f32[288,128]{1,0:T(8,128)S(1)} %get-tuple-element.28), channel_id=1, source_target_pairs={{0,1},{1,0},{2,3},{3,2},{4,5},{5,4},{6,7},{7,6},{8,9},{9,8},{10,11... | collective-permute-start | bytes 442376 | tf_op jit(solution)/shard_map/ppermute | solution.py:491
  6.0 6.2 %collective-permute-start.8 = (f32[432,128]{1,0:T(8,128)S(1)}, f32[432,128]{1,0:T(8,128)S(1)}, u32[]{:S(2)}, u32[]{:S(2)}) collective-permute-start(f32[432,128]{1,0:T(8,128)S(1)} %get-tuple-element.33), channel_id=1, source_target_pairs={{0,1},{1,0},{2,3},{3,2},{4,5},{5,4},{6,7},{7,6},{8,9},{9,8},{10,11... | collective-permute-start | bytes 663560 | tf_op jit(solution)/shard_map/ppermute | solution.py:491
  6.1 6.1 %copy-start.2 = (s32[24,9]{0,1:T(8,128)S(1)}, s32[24,9]{0,1:T(8,128)}, u32[]{:S(2)}) copy-start(s32[24,9]{0,1:T(8,128)} %param.12) | copy-start | bytes 2596
  6.1 6.1 %copy-start.4 = (s32[16]{0:T(128)S(1)}, s32[16]{0:T(128)}, u32[]{:S(2)}) copy-start(s32[16]{0:T(128)} %table_ref.1) | copy-start | bytes 196
  6.5 8.4 %collective-permute-start.3 = (bf16[1,288,128]{2,1,0:T(8,128)(2,1)S(1)}, bf16[1,288,128]{2,1,0:T(8,128)(2,1)S(1)}, u32[]{:S(2)}, u32[]{:S(2)}) collective-permute-start(bf16[1,288,128]{2,1,0:T(8,128)(2,1)S(1)} %bitcast.16), channel_id=1, source_target_pairs={{0,12},{2,14},{4,8},{6,10},{8,4},{10,6},{12,0},{14,2},{1,13},{3,15... | collective-permute-start | bytes 221192 | tf_op jit(solution)/shard_map/ppermute | solution.py:495
  11.5 6.4 %collective-permute-start.2 = (bf16[1,288,128]{2,1,0:T(8,128)(2,1)S(1)}, bf16[1,288,128]{2,1,0:T(8,128)(2,1)S(1)}, u32[]{:S(2)}, u32[]{:S(2)}) collective-permute-start(bf16[1,288,128]{2,1,0:T(8,128)(2,1)S(1)} %bitcast.17), channel_id=1, source_target_pairs={{0,8},{2,10},{4,12},{6,14},{8,0},{10,2},{12,4},{14,6},{1,9},{3,11}... | collective-permute-start | bytes 221192 | tf_op jit(solution)/shard_map/ppermute | solution.py:495
  11.5 6.4 %collective-permute-start.1 = (bf16[1,288,128]{2,1,0:T(8,128)(2,1)S(1)}, bf16[1,288,128]{2,1,0:T(8,128)(2,1)S(1)}, u32[]{:S(2)}, u32[]{:S(2)}) collective-permute-start(bf16[1,288,128]{2,1,0:T(8,128)(2,1)S(1)} %bitcast.18), channel_id=1, source_target_pairs={{0,4},{2,6},{4,0},{6,2},{8,12},{10,14},{12,8},{14,10},{1,5},{3,7},... | collective-permute-start | bytes 221192 | tf_op jit(solution)/shard_map/ppermute | solution.py:495
  13.1 6.2 %collective-permute-start.9 = (bf16[448,128]{1,0:T(8,128)(2,1)S(1)}, bf16[448,128]{1,0:T(8,128)(2,1)S(1)}, u32[]{:S(2)}, u32[]{:S(2)}) collective-permute-start(bf16[448,128]{1,0:T(8,128)(2,1)S(1)} %get-tuple-element.34.refs_9_), channel_id=1, source_target_pairs={{0,2},{2,0},{4,6},{6,4},{8,10},{10,8},{12,14},{14,12},{1,3},{3,1},... | collective-permute-start | bytes 344072 | tf_op jit(solution)/shard_map/ppermute | solution.py:495
  14.8 3.7 %collective-permute-start.4 = (bf16[1,288,128]{2,1,0:T(8,128)(2,1)S(1)}, bf16[1,288,128]{2,1,0:T(8,128)(2,1)S(1)}, u32[]{:S(2)}, u32[]{:S(2)}) collective-permute-start(bf16[1,288,128]{2,1,0:T(8,128)(2,1)S(1)} %bitcast.19), channel_id=1, source_target_pairs={{0,1},{1,0},{2,3},{3,2},{4,5},{5,4},{6,7},{7,6},{8,9},{9,8},{10,11... | collective-permute-start | bytes 221192 | tf_op jit(solution)/shard_map/ppermute | solution.py:491
  14.8 3.7 %collective-permute-start.7 = (bf16[1,288,128]{2,1,0:T(8,128)(2,1)S(1)}, bf16[1,288,128]{2,1,0:T(8,128)(2,1)S(1)}, u32[]{:S(2)}, u32[]{:S(2)}) collective-permute-start(bf16[1,288,128]{2,1,0:T(8,128)(2,1)S(1)} %collective-permute-done.3.refs_3_), channel_id=1, source_target_pairs={{0,1},{1,0},{2,3},{3,2},{4,5},{5,4},{6,7},{7,6},{8,9},{9,8},{10,11... | collective-permute-start | bytes 221192 | tf_op jit(solution)/shard_map/ppermute | solution.py:491
  18.0 1.3 %collective-permute-start.6 = (bf16[1,288,128]{2,1,0:T(8,128)(2,1)S(1)}, bf16[1,288,128]{2,1,0:T(8,128)(2,1)S(1)}, u32[]{:S(2)}, u32[]{:S(2)}) collective-permute-start(bf16[1,288,128]{2,1,0:T(8,128)(2,1)S(1)} %collective-permute-done.2.refs_2_), channel_id=1, source_target_pairs={{0,1},{1,0},{2,3},{3,2},{4,5},{5,4},{6,7},{7,6},{8,9},{9,8},{10,11... | collective-permute-start | bytes 221192 | tf_op jit(solution)/shard_map/ppermute | solution.py:491
  18.0 1.4 %collective-permute-start.5 = (bf16[1,288,128]{2,1,0:T(8,128)(2,1)S(1)}, bf16[1,288,128]{2,1,0:T(8,128)(2,1)S(1)}, u32[]{:S(2)}, u32[]{:S(2)}) collective-permute-start(bf16[1,288,128]{2,1,0:T(8,128)(2,1)S(1)} %collective-permute-done.1.refs_1_), channel_id=1, source_target_pairs={{0,1},{1,0},{2,3},{3,2},{4,5},{5,4},{6,7},{7,6},{8,9},{9,8},{10,11... | collective-permute-start | bytes 221192 | tf_op jit(solution)/shard_map/ppermute | solution.py:491
  21.8 3.7 %collective-permute-start.10 = (f32[8,128]{1,0:T(8,128)S(1)}, f32[8,128]{1,0:T(8,128)S(1)}, u32[]{:S(2)}, u32[]{:S(2)}) collective-permute-start(f32[8,128]{1,0:T(8,128)S(1)} %get-tuple-element.37.refs_14_), channel_id=1, source_target_pairs={{0,2},{2,0},{4,6},{6,4},{8,10},{10,8},{12,14},{14,12},{1,3},{3,1},... | collective-permute-start | bytes 12296 | tf_op jit(solution)/shard_map/ppermute | solution.py:495
  25.5 12.2 %copy-start = (bf16[24,32,2048]{2,1,0:T(8,128)(2,1)S(1)}, bf16[24,32,2048]{2,1,0:T(8,128)(2,1)}, u32[]{:S(2)}) copy-start(bf16[24,32,2048]{2,1,0:T(8,128)(2,1)} %param.7) | copy-start | bytes 9437188
  28.0 8.3 %collective-permute-start.11 = (f32[2,16,256]{2,1,0:T(8,128)S(1)}, f32[2,16,256]{2,1,0:T(8,128)S(1)}, u32[]{:S(2)}, u32[]{:S(2)}) collective-permute-start(f32[2,16,256]{2,1,0:T(8,128)S(1)} %get-tuple-element.42), channel_id=1, source_target_pairs={{0,12},{2,14},{4,8},{6,10},{8,4},{10,6},{12,0},{14,2},{1,13},{3,15... | collective-permute-start | bytes 98312 | tf_op jit(solution)/shard_map/ppermute | solution.py:495
  30.6 5.7 %collective-permute-start.12 = (f32[2,16,256]{2,1,0:T(8,128)S(1)}, f32[2,16,256]{2,1,0:T(8,128)S(1)}, u32[]{:S(2)}, u32[]{:S(2)}) collective-permute-start(f32[2,16,256]{2,1,0:T(8,128)S(1)} %get-tuple-element.43), channel_id=1, source_target_pairs={{0,8},{2,10},{4,12},{6,14},{8,0},{10,2},{12,4},{14,6},{1,9},{3,11}... | collective-permute-start | bytes 98312 | tf_op jit(solution)/shard_map/ppermute | solution.py:495
  30.6 5.7 %collective-permute-start.13 = (f32[2,16,256]{2,1,0:T(8,128)S(1)}, f32[2,16,256]{2,1,0:T(8,128)S(1)}, u32[]{:S(2)}, u32[]{:S(2)}) collective-permute-start(f32[2,16,256]{2,1,0:T(8,128)S(1)} %get-tuple-element.44), channel_id=1, source_target_pairs={{0,4},{2,6},{4,0},{6,2},{8,12},{10,14},{12,8},{14,10},{1,5},{3,7},... | collective-permute-start | bytes 98312 | tf_op jit(solution)/shard_map/ppermute | solution.py:495
  32.5 3.8 %collective-permute-start.14 = (f32[16,384]{1,0:T(8,128)S(1)}, f32[16,384]{1,0:T(8,128)S(1)}, u32[]{:S(2)}, u32[]{:S(2)}) collective-permute-start(f32[16,384]{1,0:T(8,128)S(1)} %get-tuple-element.46), channel_id=1, source_target_pairs={{0,2},{2,0},{4,6},{6,4},{8,10},{10,8},{12,14},{14,12},{1,3},{3,1},... | collective-permute-start | bytes 73736 | tf_op jit(solution)/shard_map/ppermute | solution.py:495
  36.3 1.3 %collective-permute-start.15 = (f32[16,1280]{1,0:T(8,128)S(1)}, f32[16,1280]{1,0:T(8,128)S(1)}, u32[]{:S(2)}, u32[]{:S(2)}) collective-permute-start(f32[16,1280]{1,0:T(8,128)S(1)} %collect.1.mine_ref), channel_id=1, source_target_pairs={{0,1},{1,0},{2,3},{3,2},{4,5},{5,4},{6,7},{7,6},{8,9},{9,8},{10,11... | collective-permute-start | bytes 245768 | tf_op jit(solution)/shard_map/ppermute | solution.py:491
  37.7 1.6 %copy-start.1 = (bf16[2,256,2048]{2,1,0:T(8,128)(2,1)S(1)}, bf16[2,256,2048]{2,1,0:T(8,128)(2,1)}, u32[]{:S(2)}) copy-start(bf16[2,256,2048]{2,1,0:T(8,128)(2,1)} %param.8) | copy-start | bytes 6291460
  41.2 4.4 %collective-permute-start.16 = (f16[16,2304]{1,0:T(8,128)(2,1)S(1)}, f16[16,2304]{1,0:T(8,128)(2,1)S(1)}, u32[]{:S(2)}, u32[]{:S(2)}) collective-permute-start(f16[16,2304]{1,0:T(8,128)(2,1)S(1)} %get-tuple-element.54), channel_id=1, source_target_pairs={{0,2},{2,0},{4,6},{6,4},{8,10},{10,8},{12,14},{14,12},{1,3},{3,1},... | collective-permute-start | bytes 221192 | tf_op jit(solution)/shard_map/ppermute | solution.py:495
  46.2 6.6 %collective-permute-start.18 = (f16[16,2304]{1,0:T(8,128)(2,1)S(1)}, f16[16,2304]{1,0:T(8,128)(2,1)S(1)}, u32[]{:S(2)}, u32[]{:S(2)}) collective-permute-start(f16[16,2304]{1,0:T(8,128)(2,1)S(1)} %get-tuple-element.52), channel_id=1, source_target_pairs={{0,12},{2,14},{4,8},{6,10},{8,4},{10,6},{12,0},{14,2},{1,13},{3,15... | collective-permute-start | bytes 221192 | tf_op jit(solution)/shard_map/ppermute | solution.py:495
  48.8 5.7 %collective-permute-start.17 = (f16[16,2304]{1,0:T(8,128)(2,1)S(1)}, f16[16,2304]{1,0:T(8,128)(2,1)S(1)}, u32[]{:S(2)}, u32[]{:S(2)}) collective-permute-start(f16[16,2304]{1,0:T(8,128)(2,1)S(1)} %get-tuple-element.52), channel_id=1, source_target_pairs={{0,4},{2,6},{4,0},{6,2},{8,12},{10,14},{12,8},{14,10},{1,5},{3,7},... | collective-permute-start | bytes 221192 | tf_op jit(solution)/shard_map/ppermute | solution.py:495
  48.8 5.9 %collective-permute-start.19 = (f16[16,2304]{1,0:T(8,128)(2,1)S(1)}, f16[16,2304]{1,0:T(8,128)(2,1)S(1)}, u32[]{:S(2)}, u32[]{:S(2)}) collective-permute-start(f16[16,2304]{1,0:T(8,128)(2,1)S(1)} %get-tuple-element.52), channel_id=1, source_target_pairs={{0,8},{2,10},{4,12},{6,14},{8,0},{10,2},{12,4},{14,6},{1,9},{3,11}... | collective-permute-start | bytes 221192 | tf_op jit(solution)/shard_map/ppermute | solution.py:495

commit v6 on v5

--- a/solution.py
+++ b/solution.py
@@ -528,9 +528,8 @@
     return scaled.astype(jnp.float16)
 
 
-def decoded(x):
-    x = x.astype(f32)
-    return x[:, :-LANES] * power_of_two(x[:, -LANES : 1 - LANES])
+def decoded(x, columns=slice(0, -LANES)):
+    return x[:, columns].astype(f32) * power_of_two(x[:, -LANES : 1 - LANES].astype(f32))
 
 
 def sum_over_shards(x, nshard, width):
@@ -539,9 +538,13 @@
         return x[:, :width], x[:, width:]
     x = coded(x)
     x = coded(decoded(x) + decoded(across(x, nshard, 1)))
-    a, b, c = (decoded(across(x, nshard, k)) for k in (6, 4, 2))
-    x = (decoded(x) + c) + (a + b)
-    return x[:, :width], x[:, width:]
+    arrays = [x] + [across(x, nshard, k) for k in (6, 4, 2)]
+
+    def total(columns):
+        x, a, b, c = (decoded(array, columns) for array in arrays)
+        return (x + c) + (a + b)
+
+    return total(slice(0, width)), total(slice(width, -LANES))
 
 
 def per_device(

time: 56.5 us -> 57.5 us (1.018)
  other arithmetic: 1.93 us -> 3.27 us
  local copies, waits for them, and re-layouts: 3.61 us -> 4.66 us
  starting transfers between devices: 22.6 us -> 21.7 us
    shift_right_arithmetic x0 -> x28, local copies, waits for them, and re-layouts: none -> 2.31 us  [power_of_two(): digits >> k]
    ppermute x13, starting transfers between devices: 20.9 us -> 20 us  [across(): return lax.ppermute(x, 'shard', [(i, i ^ step) for i in range(nshard)])]
    transpose x0 -> x1, other arithmetic: none -> 0.76 us  [per_device(): return (query_loss, jnp.transpose(down_sum), up_sum)]
    transpose x1 -> x0, local copies, waits for them, and re-layouts: 0.66 us -> none  [per_device(): return (query_loss, jnp.transpose(down_sum), up_sum)]
    slice x1 -> x0, local copies, waits for them, and re-layouts: 0.6 us -> none  [sum_over_shards(): return (x[:, :width], x[:, width:])]
    add x1, other arithmetic: 0.1 us -> 0.68 us  [total(): return x + c + (a + b)]
  transfers between devices with their start and end apart: 20 -> 20, of which waited for: 9 -> 9; matrix products, arithmetic and copies ran while one was open for 2% -> 4% of each run, Pallas kernels for 5% -> 5%
where the time goes in v6:
time: 57.5 us; the launch traced here: 57.4 us
  starting transfers between devices  21.7 us (38%)
  waiting for transfers between devices  14 us (24%)
  Pallas kernels  13 us (23%)
  local copies, waits for them, and re-layouts  4.66 us (8%)
  other arithmetic  3.27 us (6%)
  between operations  0.81 us (1%)
    ppermute x13, starting transfers between devices, across(): return lax.ppermute(x, 'shard', [(i, i ^ step) for i in range(nshard)])  20 us
    ppermute x13, waiting for transfers between devices, across(): return lax.ppermute(x, 'shard', [(i, i ^ step) for i in range(nshard)])  11.8 us
    pallas_call x1, Pallas kernels, project_passages(): pl.pallas_call(project_passages_kernel, in_specs=[SMEM] + [HBM] * 4, out_...  3.71 us
    pallas_call x1, Pallas kernels, score_backward(): pl.pallas_call(functools.partial(backward_kernel, cfg), in_specs=[VMEM] *...  2.53 us
    pallas_call x1, Pallas kernels, score_forward(): pl.pallas_call(functools.partial(forward_kernel, cfg), in_specs=[VMEM] *...  2.43 us
    shift_right_arithmetic x28, local copies, waits for them, and re-layouts, power_of_two(): digits >> k  2.31 us
    ppermute x7, waiting for transfers between devices, swap(): return lax.ppermute(x, 'sub', [(0, 1), (1, 0)])  2.17 us
    ppermute x7, starting transfers between devices, swap(): return lax.ppermute(x, 'sub', [(0, 1), (1, 0)])  1.71 us
  transfers between devices with their start and end apart: 20, of which 9 were waited for; matrix products, arithmetic and copies ran while one was open for 4% of the time, Pallas kernels for 5%

profile of v6, /device:TPU:0, one launch (start us, length us, event | category | flops | bytes accessed | tf_op | source)
XLA Modules:
  0.0 57.4 jit_solution(11757376214878777582)
XLA Ops:
  0.7 3.7 %project_passages.1 = (f32[288,128]{1,0:T(8,128)S(1)}, f32[288,128]{1,0:T(8,128)S(1)}, bf16[768,2048]{1,0:T(8,128)(2,1)S(1)}, bf16[2048,256]{1,0:T(8,128)(2,1)S(1)}) custom-call(s32[3]{0:T(128)S(1)} %pad_add_fusion.info_ref.refs_8_, bf16[512,2048]{1,0:T(8,128)(2,1)} %bitcast.70, bf16[768,2048]{1,0:T(8,128)(2,1)} %bitcast.68, bf16[2048,128]{1,0:T(8,128)(2,1)} %proj_hbm.1, ...), custom_call_target="tpu_custom_call" | custom-call | flops 4070000128 | bytes 12950000 | tf_op jit(solution)/shard_map/project_passages/pallas_call | solution.py:89
  4.5 0.5 collective-permute-start
  5.0 1.0 %project_queries.1 = (f32[432,128]{1,0:T(8,128)S(1)}, f32[432,128]{1,0:T(8,128)S(1)}) custom-call(bf16[768,2048]{1,0:T(8,128)(2,1)S(1)} %get-tuple-element.30.q_ref, bf16[2048,256]{1,0:T(8,128)(2,1)S(1)} %get-tuple-element.31.weight_ref), custom_call_target="tpu_custom_call" | custom-call | flops 1650000000 | bytes 5250000 | tf_op jit(solution)/shard_map/project_queries/pallas_call | solution.py:117
  6.0 0.1 collective-permute-start.8
  6.1 0.3 pack_passage.1
  6.5 5.1 %collective-permute-start.3 = (bf16[1,288,128]{2,1,0:T(8,128)(2,1)S(1)}, bf16[1,288,128]{2,1,0:T(8,128)(2,1)S(1)}, u32[]{:S(2)}, u32[]{:S(2)}) collective-permute-start(bf16[1,288,128]{2,1,0:T(8,128)(2,1)S(1)} %bitcast.72), channel_id=1, source_target_pairs={{0,12},{2,14},{4,8},{6,10},{8,4},{10,6},{12,0},{14,2},{1,13},{3,15... | collective-permute-start | bytes 221192 | tf_op jit(solution)/shard_map/ppermute | solution.py:495
  11.5 0.6 %collective-permute-start.1 = (bf16[1,288,128]{2,1,0:T(8,128)(2,1)S(1)}, bf16[1,288,128]{2,1,0:T(8,128)(2,1)S(1)}, u32[]{:S(2)}, u32[]{:S(2)}) collective-permute-start(bf16[1,288,128]{2,1,0:T(8,128)(2,1)S(1)} %bitcast.74), channel_id=1, source_target_pairs={{0,4},{2,6},{4,0},{6,2},{8,12},{10,14},{12,8},{14,10},{1,5},{3,7},... | collective-permute-start | bytes 221192 | tf_op jit(solution)/shard_map/ppermute | solution.py:495
  12.2 1.0 %pack_queries.1 = (bf16[448,128]{1,0:T(8,128)(2,1)S(1)}, f32[8,384]{1,0:T(8,128)S(1)}) custom-call(s32[3]{0:T(128)S(1)} %pad_add_fusion.info_ref.refs_8_, s32[16]{0:T(128)S(1)} %copy-done.4, s32[9,24]{1,0:T(8,128)S(1)} %bitcast.79, f32[432,128]{1,0:T(8,128)S(1)} %get-tuple-element.32.keep_ref, f32[432,128]{1,0:T(8,128)S(1)} %collective-permute-done.8.recv_ref, ...), custom_call_target="tpu_custom_call" | custom-call | flops 990000000 | bytes 3150000 | tf_op jit(solution)/shard_map/pack_queries/pallas_call | solution.py:192
  13.1 1.7 %collective-permute-start.9 = (bf16[448,128]{1,0:T(8,128)(2,1)S(1)}, bf16[448,128]{1,0:T(8,128)(2,1)S(1)}, u32[]{:S(2)}, u32[]{:S(2)}) collective-permute-start(bf16[448,128]{1,0:T(8,128)(2,1)S(1)} %get-tuple-element.34.refs_9_), channel_id=1, source_target_pairs={{0,2},{2,0},{4,6},{6,4},{8,10},{10,8},{12,14},{14,12},{1,3},{3,1},... | collective-permute-start | bytes 344072 | tf_op jit(solution)/shard_map/ppermute | solution.py:495
  14.8 0.5 collective-permute-start.7
  15.3 2.6 %collective-permute-done.2.refs_2_ = bf16[1,288,128]{2,1,0:T(8,128)(2,1)S(1)} collective-permute-done((bf16[1,288,128]{2,1,0:T(8,128)(2,1)S(1)}, bf16[1,288,128]{2,1,0:T(8,128)(2,1)S(1)}, u32[]{:S(2)}, u32[]{:S(2)}) %collective-permute-start.2) | collective-permute-done | bytes 73760 | tf_op jit(solution)/shard_map/ppermute | solution.py:495
  18.0 0.5 collective-permute-start.5
  18.5 0.7 %collective-permute-done.6.refs_6_ = bf16[1,288,128]{2,1,0:T(8,128)(2,1)S(1)} collective-permute-done((bf16[1,288,128]{2,1,0:T(8,128)(2,1)S(1)}, bf16[1,288,128]{2,1,0:T(8,128)(2,1)S(1)}, u32[]{:S(2)}, u32[]{:S(2)}) %collective-permute-start.6) | collective-permute-done | bytes 73760 | tf_op jit(solution)/shard_map/ppermute | solution.py:491
  19.2 0.2 collective-permute-done.5.refs_5_
  19.4 2.4 %score_forward.1 = (f32[3,8,128]{2,1,0:T(8,128)S(1)}, f32[8,768]{1,0:T(8,128)S(1)}, f32[8,128]{1,0:T(8,128)S(1)}, bf16[8,256,768]{2,1,0:T(8,128)(2,1)S(1)}, bf16[128,768]{1,0:T(8,128)(2,1)S(1)}) custom-call(bf16[1,288,128]{2,1,0:T(8,128)(2,1)S(1)} %bitcast.76, bf16[1,288,128]{2,1,0:T(8,128)(2,1)S(1)} %collective-permute-done.1.refs_1_, ...), custom_call_target="tpu_custom_call" | custom-call | flops 2090000000 | bytes 6650000 | tf_op jit(solution)/shard_map/score_forward/pallas_call | solution.py:364
  21.8 1.6 %collective-permute-start.10 = (f32[8,128]{1,0:T(8,128)S(1)}, f32[8,128]{1,0:T(8,128)S(1)}, u32[]{:S(2)}, u32[]{:S(2)}) collective-permute-start(f32[8,128]{1,0:T(8,128)S(1)} %get-tuple-element.37.refs_14_), channel_id=1, source_target_pairs={{0,2},{2,0},{4,6},{6,4},{8,10},{10,8},{12,14},{14,12},{1,3},{3,1},... | collective-permute-start | bytes 12296 | tf_op jit(solution)/shard_map/ppermute | solution.py:495
  23.4 0.6 %unit.1.refs_17_ = bf16[8,128,768]{2,1,0:T(8,128)(2,1)S(1)} custom-call(bf16[1,288,128]{2,1,0:T(8,128)(2,1)S(1)} %bitcast.77, bf16[1,288,128]{2,1,0:T(8,128)(2,1)S(1)} %collective-permute-done.1.refs_1_, bf16[1,288,128]{2,1,0:T(8,128)(2,1)S(1)} %collective-permute-done.2.refs_2_, bf16[1,288,128]{2,1,0:T(8,128)(2,1)S(1)} %collective-permute-done.3.refs_3_, ...), custom_call_target="tpu_custom_call" | custom-call | flops 1320000000 | bytes 4200000 | tf_op jit(solution)/shard_map/unit/pallas_call | solution.py:391
  24.0 1.5 %collective-permute-done.10.refs_15_ = f32[8,128]{1,0:T(8,128)S(1)} collective-permute-done((f32[8,128]{1,0:T(8,128)S(1)}, f32[8,128]{1,0:T(8,128)S(1)}, u32[]{:S(2)}, u32[]{:S(2)}) %collective-permute-start.10) | collective-permute-done | bytes 4128 | tf_op jit(solution)/shard_map/ppermute | solution.py:495
  25.5 2.5 %score_backward.1 = (f32[2,16,256]{2,1,0:T(8,128)S(1)}, f32[2,16,256]{2,1,0:T(8,128)S(1)}, f32[2,16,256]{2,1,0:T(8,128)S(1)}, f32[2,16,256]{2,1,0:T(8,128)S(1)},...) custom-call(bf16[1,288,128]{2,1,0:T(8,128)(2,1)S(1)} %bitcast.78, ...), custom_call_target="tpu_custom_call" | custom-call | flops 2750000128 | bytes 8750000 | tf_op jit(solution)/shard_map/score_backward/pallas_call | solution.py:410
  28.0 2.6 %collective-permute-start.11 = (f32[2,16,256]{2,1,0:T(8,128)S(1)}, f32[2,16,256]{2,1,0:T(8,128)S(1)}, u32[]{:S(2)}, u32[]{:S(2)}) collective-permute-start(f32[2,16,256]{2,1,0:T(8,128)S(1)} %get-tuple-element.42), channel_id=1, source_target_pairs={{0,12},{2,14},{4,8},{6,10},{8,4},{10,6},{12,0},{14,2},{1,13},{3,15... | collective-permute-start | bytes 98312 | tf_op jit(solution)/shard_map/ppermute | solution.py:495
  30.7 1.8 %collective-permute-start.13 = (f32[2,16,256]{2,1,0:T(8,128)S(1)}, f32[2,16,256]{2,1,0:T(8,128)S(1)}, u32[]{:S(2)}, u32[]{:S(2)}) collective-permute-start(f32[2,16,256]{2,1,0:T(8,128)S(1)} %get-tuple-element.44), channel_id=1, source_target_pairs={{0,4},{2,6},{4,0},{6,2},{8,12},{10,14},{12,8},{14,10},{1,5},{3,7},... | collective-permute-start | bytes 98312 | tf_op jit(solution)/shard_map/ppermute | solution.py:495
  32.5 1.5 %collective-permute-start.14 = (f32[16,384]{1,0:T(8,128)S(1)}, f32[16,384]{1,0:T(8,128)S(1)}, u32[]{:S(2)}, u32[]{:S(2)}) collective-permute-start(f32[16,384]{1,0:T(8,128)S(1)} %get-tuple-element.46), channel_id=1, source_target_pairs={{0,2},{2,0},{4,6},{6,4},{8,10},{10,8},{12,14},{14,12},{1,3},{3,1},... | collective-permute-start | bytes 73736 | tf_op jit(solution)/shard_map/ppermute | solution.py:495
  34.0 2.3 %collective-permute-done.14.refs_5_ = f32[16,384]{1,0:T(8,128)S(1)} collective-permute-done((f32[16,384]{1,0:T(8,128)S(1)}, f32[16,384]{1,0:T(8,128)S(1)}, u32[]{:S(2)}, u32[]{:S(2)}) %collective-permute-start.14) | collective-permute-done | bytes 24608 | tf_op jit(solution)/shard_map/ppermute | solution.py:495
  36.4 1.3 %collective-permute-done.15.other_ref = f32[16,1280]{1,0:T(8,128)S(1)} collective-permute-done((f32[16,1280]{1,0:T(8,128)S(1)}, f32[16,1280]{1,0:T(8,128)S(1)}, u32[]{:S(2)}, u32[]{:S(2)}) %collective-permute-start.15) | collective-permute-done | bytes 81952 | tf_op jit(solution)/shard_map/ppermute | solution.py:491
  37.7 1.6 %copy-done.1 = bf16[2,256,2048]{2,1,0:T(8,128)(2,1)S(1)} copy-done((bf16[2,256,2048]{2,1,0:T(8,128)(2,1)S(1)}, bf16[2,256,2048]{2,1,0:T(8,128)(2,1)}, u32[]{:S(2)}) %copy-start.1) | copy-done | bytes 2097176
  39.3 1.3 %grad_all.1 = f32[16,2176]{1,0:T(8,128)S(1)} custom-call(s32[3]{0:T(128)S(1)} %pad_add_fusion.info_ref.refs_8_, bf16[512,2048]{1,0:T(8,128)(2,1)S(1)} %bitcast.71, bf16[768,2048]{1,0:T(8,128)(2,1)S(1)} %bitcast.69, f32[16,1280]{1,0:T(8,128)S(1)} %collect.1.mine_ref, f32[16,1280]{1,0:T(8,128)S(1)} %collective-permute-done.15.other_ref), custom_call_target="tpu_custom_call" | custom-call | flops 1430000000 | bytes 4550000 | tf_op jit(solution)/shard_map/grad_all/pallas_call | solution.py:479
  40.6 0.1 abs_reduce_fusion.1
  40.8 0.1 copy.97
  40.9 0.1 copy.94
  41.0 0.1 copy.127
  41.4 0.1 copy.109
  42.2 1.6 %collective-permute-start.16 = (f16[16,2304]{1,0:T(8,128)(2,1)S(1)}, f16[16,2304]{1,0:T(8,128)(2,1)S(1)}, u32[]{:S(2)}, u32[]{:S(2)}) collective-permute-start(f16[16,2304]{1,0:T(8,128)(2,1)S(1)} %pad_maximum_fusion), channel_id=1, source_target_pairs={{0,2},{2,0},{4,6},{6,4},{8,10},{10,8},{12,14},{14,12},{1,3},{3,1},... | collective-permute-start | bytes 221192 | tf_op jit(solution)/shard_map/ppermute | solution.py:495
  43.7 0.2 multiply_reduce_fusion.5
  43.9 0.6 %dynamic-slice_bitcast_fusion = f32[12]{0:T(128)} fusion(f32[1,128]{1,0:T(1,128)S(1)} %slice.59, s32[]{:T(128)S(6)} %select_n.1251), kind=kLoop, calls=%fused_computation.712 | loop fusion | bytes 100 | tf_op jit(solution)/shard_map/dynamic_slice | solution.py:606
  44.5 2.1 %collective-permute-done.16 = f16[16,2304]{1,0:T(8,128)(2,1)S(1)} collective-permute-done((f16[16,2304]{1,0:T(8,128)(2,1)S(1)}, f16[16,2304]{1,0:T(8,128)(2,1)S(1)}, u32[]{:S(2)}, u32[]{:S(2)}) %collective-permute-start.16) | collective-permute-done | bytes 73760 | tf_op jit(solution)/shard_map/ppermute | solution.py:495
  46.6 0.2 multiply_reduce_fusion.4
  46.8 0.2 abs_reduce_fusion
  47.1 0.1 multiply_convert_fusion
  47.3 1.2 %collective-permute-start.19 = (f16[16,2304]{1,0:T(8,128)(2,1)S(1)}, f16[16,2304]{1,0:T(8,128)(2,1)S(1)}, u32[]{:S(2)}, u32[]{:S(2)}) collective-permute-start(f16[16,2304]{1,0:T(8,128)(2,1)S(1)} %pad_maximum_fusion.1), channel_id=1, source_target_pairs={{0,8},{2,10},{4,12},{6,14},{8,0},{10,2},{12,4},{14,6},{1,9},{3,11}... | collective-permute-start | bytes 221192 | tf_op jit(solution)/shard_map/ppermute | solution.py:495
  48.5 1.5 %collective-permute-start.18 = (f16[16,2304]{1,0:T(8,128)(2,1)S(1)}, f16[16,2304]{1,0:T(8,128)(2,1)S(1)}, u32[]{:S(2)}, u32[]{:S(2)}) collective-permute-start(f16[16,2304]{1,0:T(8,128)(2,1)S(1)} %pad_maximum_fusion.1), channel_id=1, source_target_pairs={{0,12},{2,14},{4,8},{6,10},{8,4},{10,6},{12,0},{14,2},{1,13},{3,15... | collective-permute-start | bytes 221192 | tf_op jit(solution)/shard_map/ppermute | solution.py:495
  50.0 0.8 %collective-permute-start.17 = (f16[16,2304]{1,0:T(8,128)(2,1)S(1)}, f16[16,2304]{1,0:T(8,128)(2,1)S(1)}, u32[]{:S(2)}, u32[]{:S(2)}) collective-permute-start(f16[16,2304]{1,0:T(8,128)(2,1)S(1)} %pad_maximum_fusion.1), channel_id=1, source_target_pairs={{0,4},{2,6},{4,0},{6,2},{8,12},{10,14},{12,8},{14,10},{1,5},{3,7},... | collective-permute-start | bytes 221192 | tf_op jit(solution)/shard_map/ppermute | solution.py:495
  52.0 0.2 multiply_reduce_fusion.3
  52.2 3.2 %collective-permute-done.19 = f16[16,2304]{1,0:T(8,128)(2,1)S(1)} collective-permute-done((f16[16,2304]{1,0:T(8,128)(2,1)S(1)}, f16[16,2304]{1,0:T(8,128)(2,1)S(1)}, u32[]{:S(2)}, u32[]{:S(2)}) %collective-permute-start.19) | collective-permute-done | bytes 73760 | tf_op jit(solution)/shard_map/ppermute | solution.py:495
  55.3 0.2 multiply_reduce_fusion
  55.5 0.2 multiply_reduce_fusion.1
  55.7 0.2 multiply_reduce_fusion.2
  55.9 0.7 %add_add_fusion = f32[16,128]{1,0:T(8,128)} fusion(f16[16,2304]{1,0:T(8,128)(2,1)S(1)} %collective-permute-done.19, f16[16,2304]{1,0:T(8,128)(2,1)S(1)} %collective-permute-done.18, f16[16,2304]{1,0:T(8,128)(2,1)S(1)} %collective-permute-done.17, f16[16,2176]{1,0:T(8,128)(2,1)S(1)} %multiply_convert_fusion, f32[16]{0:T(128)S(1)} %multiply_reduce_fusion, ...), kind=kLoop, calls=%fused_computation.504 | loop fusion | flops 22528 | bytes 24832 | tf_op jit(solution)/shard_map/add | solution.py:545
  56.6 0.8 %add_bitcast_fusion = f32[2048,16]{0,1:T(8,128)} fusion(f16[16,2304]{1,0:T(8,128)(2,1)S(1)} %collective-permute-done.19, f16[16,2304]{1,0:T(8,128)(2,1)S(1)} %collective-permute-done.18, f16[16,2304]{1,0:T(8,128)(2,1)S(1)} %collective-permute-done.17, f16[16,2176]{1,0:T(8,128)(2,1)S(1)} %multiply_convert_fusion, f32[16]{0:T(128)S(1)} %multiply_reduce_fusion, ...), kind=kLoop, calls=%fused_computation.5 | loop fusion | flops 360448 | bytes 393472 | tf_op jit(solution)/shard_map/transpose | solution.py:607
  (64 shorter events, 2.7 us)
Async XLA Ops:
  4.4 1.7 %copy-start.3 = (bf16[16,128]{1,0:T(8,128)(2,1)S(1)}, bf16[16,128]{1,0:T(8,128)(2,1)}, u32[]{:S(2)}) copy-start(bf16[16,128]{1,0:T(8,128)(2,1)} %refs_11_.1) | copy-start | bytes 12292
  4.5 1.6 %collective-permute-start = (f32[288,128]{1,0:T(8,128)S(1)}, f32[288,128]{1,0:T(8,128)S(1)}, u32[]{:S(2)}, u32[]{:S(2)}) collective-permute-start(f32[288,128]{1,0:T(8,128)S(1)} %get-tuple-element.28), channel_id=1, source_target_pairs={{0,1},{1,0},{2,3},{3,2},{4,5},{5,4},{6,7},{7,6},{8,9},{9,8},{10,11... | collective-permute-start | bytes 442376 | tf_op jit(solution)/shard_map/ppermute | solution.py:491
  6.0 6.2 %collective-permute-start.8 = (f32[432,128]{1,0:T(8,128)S(1)}, f32[432,128]{1,0:T(8,128)S(1)}, u32[]{:S(2)}, u32[]{:S(2)}) collective-permute-start(f32[432,128]{1,0:T(8,128)S(1)} %get-tuple-element.33), channel_id=1, source_target_pairs={{0,1},{1,0},{2,3},{3,2},{4,5},{5,4},{6,7},{7,6},{8,9},{9,8},{10,11... | collective-permute-start | bytes 663560 | tf_op jit(solution)/shard_map/ppermute | solution.py:491
  6.1 6.1 %copy-start.2 = (s32[24,9]{0,1:T(8,128)S(1)}, s32[24,9]{0,1:T(8,128)}, u32[]{:S(2)}) copy-start(s32[24,9]{0,1:T(8,128)} %param.12) | copy-start | bytes 2596
  6.1 6.1 %copy-start.4 = (s32[16]{0:T(128)S(1)}, s32[16]{0:T(128)}, u32[]{:S(2)}) copy-start(s32[16]{0:T(128)} %table_ref.1) | copy-start | bytes 196
  6.5 8.4 %collective-permute-start.3 = (bf16[1,288,128]{2,1,0:T(8,128)(2,1)S(1)}, bf16[1,288,128]{2,1,0:T(8,128)(2,1)S(1)}, u32[]{:S(2)}, u32[]{:S(2)}) collective-permute-start(bf16[1,288,128]{2,1,0:T(8,128)(2,1)S(1)} %bitcast.72), channel_id=1, source_target_pairs={{0,12},{2,14},{4,8},{6,10},{8,4},{10,6},{12,0},{14,2},{1,13},{3,15... | collective-permute-start | bytes 221192 | tf_op jit(solution)/shard_map/ppermute | solution.py:495
  11.5 6.4 %collective-permute-start.2 = (bf16[1,288,128]{2,1,0:T(8,128)(2,1)S(1)}, bf16[1,288,128]{2,1,0:T(8,128)(2,1)S(1)}, u32[]{:S(2)}, u32[]{:S(2)}) collective-permute-start(bf16[1,288,128]{2,1,0:T(8,128)(2,1)S(1)} %bitcast.73), channel_id=1, source_target_pairs={{0,8},{2,10},{4,12},{6,14},{8,0},{10,2},{12,4},{14,6},{1,9},{3,11}... | collective-permute-start | bytes 221192 | tf_op jit(solution)/shard_map/ppermute | solution.py:495
  11.5 6.4 %collective-permute-start.1 = (bf16[1,288,128]{2,1,0:T(8,128)(2,1)S(1)}, bf16[1,288,128]{2,1,0:T(8,128)(2,1)S(1)}, u32[]{:S(2)}, u32[]{:S(2)}) collective-permute-start(bf16[1,288,128]{2,1,0:T(8,128)(2,1)S(1)} %bitcast.74), channel_id=1, source_target_pairs={{0,4},{2,6},{4,0},{6,2},{8,12},{10,14},{12,8},{14,10},{1,5},{3,7},... | collective-permute-start | bytes 221192 | tf_op jit(solution)/shard_map/ppermute | solution.py:495
  13.1 6.2 %collective-permute-start.9 = (bf16[448,128]{1,0:T(8,128)(2,1)S(1)}, bf16[448,128]{1,0:T(8,128)(2,1)S(1)}, u32[]{:S(2)}, u32[]{:S(2)}) collective-permute-start(bf16[448,128]{1,0:T(8,128)(2,1)S(1)} %get-tuple-element.34.refs_9_), channel_id=1, source_target_pairs={{0,2},{2,0},{4,6},{6,4},{8,10},{10,8},{12,14},{14,12},{1,3},{3,1},... | collective-permute-start | bytes 344072 | tf_op jit(solution)/shard_map/ppermute | solution.py:495
  14.8 3.7 %collective-permute-start.4 = (bf16[1,288,128]{2,1,0:T(8,128)(2,1)S(1)}, bf16[1,288,128]{2,1,0:T(8,128)(2,1)S(1)}, u32[]{:S(2)}, u32[]{:S(2)}) collective-permute-start(bf16[1,288,128]{2,1,0:T(8,128)(2,1)S(1)} %bitcast.75), channel_id=1, source_target_pairs={{0,1},{1,0},{2,3},{3,2},{4,5},{5,4},{6,7},{7,6},{8,9},{9,8},{10,11... | collective-permute-start | bytes 221192 | tf_op jit(solution)/shard_map/ppermute | solution.py:491
  14.8 3.7 %collective-permute-start.7 = (bf16[1,288,128]{2,1,0:T(8,128)(2,1)S(1)}, bf16[1,288,128]{2,1,0:T(8,128)(2,1)S(1)}, u32[]{:S(2)}, u32[]{:S(2)}) collective-permute-start(bf16[1,288,128]{2,1,0:T(8,128)(2,1)S(1)} %collective-permute-done.3.refs_3_), channel_id=1, source_target_pairs={{0,1},{1,0},{2,3},{3,2},{4,5},{5,4},{6,7},{7,6},{8,9},{9,8},{10,11... | collective-permute-start | bytes 221192 | tf_op jit(solution)/shard_map/ppermute | solution.py:491
  18.0 1.3 %collective-permute-start.6 = (bf16[1,288,128]{2,1,0:T(8,128)(2,1)S(1)}, bf16[1,288,128]{2,1,0:T(8,128)(2,1)S(1)}, u32[]{:S(2)}, u32[]{:S(2)}) collective-permute-start(bf16[1,288,128]{2,1,0:T(8,128)(2,1)S(1)} %collective-permute-done.2.refs_2_), channel_id=1, source_target_pairs={{0,1},{1,0},{2,3},{3,2},{4,5},{5,4},{6,7},{7,6},{8,9},{9,8},{10,11... | collective-permute-start | bytes 221192 | tf_op jit(solution)/shard_map/ppermute | solution.py:491
  18.0 1.4 %collective-permute-start.5 = (bf16[1,288,128]{2,1,0:T(8,128)(2,1)S(1)}, bf16[1,288,128]{2,1,0:T(8,128)(2,1)S(1)}, u32[]{:S(2)}, u32[]{:S(2)}) collective-permute-start(bf16[1,288,128]{2,1,0:T(8,128)(2,1)S(1)} %collective-permute-done.1.refs_1_), channel_id=1, source_target_pairs={{0,1},{1,0},{2,3},{3,2},{4,5},{5,4},{6,7},{7,6},{8,9},{9,8},{10,11... | collective-permute-start | bytes 221192 | tf_op jit(solution)/shard_map/ppermute | solution.py:491
  21.8 3.7 %collective-permute-start.10 = (f32[8,128]{1,0:T(8,128)S(1)}, f32[8,128]{1,0:T(8,128)S(1)}, u32[]{:S(2)}, u32[]{:S(2)}) collective-permute-start(f32[8,128]{1,0:T(8,128)S(1)} %get-tuple-element.37.refs_14_), channel_id=1, source_target_pairs={{0,2},{2,0},{4,6},{6,4},{8,10},{10,8},{12,14},{14,12},{1,3},{3,1},... | collective-permute-start | bytes 12296 | tf_op jit(solution)/shard_map/ppermute | solution.py:495
  25.5 12.2 %copy-start = (bf16[24,32,2048]{2,1,0:T(8,128)(2,1)S(1)}, bf16[24,32,2048]{2,1,0:T(8,128)(2,1)}, u32[]{:S(2)}) copy-start(bf16[24,32,2048]{2,1,0:T(8,128)(2,1)} %param.7) | copy-start | bytes 9437188
  28.0 8.3 %collective-permute-start.11 = (f32[2,16,256]{2,1,0:T(8,128)S(1)}, f32[2,16,256]{2,1,0:T(8,128)S(1)}, u32[]{:S(2)}, u32[]{:S(2)}) collective-permute-start(f32[2,16,256]{2,1,0:T(8,128)S(1)} %get-tuple-element.42), channel_id=1, source_target_pairs={{0,12},{2,14},{4,8},{6,10},{8,4},{10,6},{12,0},{14,2},{1,13},{3,15... | collective-permute-start | bytes 98312 | tf_op jit(solution)/shard_map/ppermute | solution.py:495
  30.7 5.7 %collective-permute-start.12 = (f32[2,16,256]{2,1,0:T(8,128)S(1)}, f32[2,16,256]{2,1,0:T(8,128)S(1)}, u32[]{:S(2)}, u32[]{:S(2)}) collective-permute-start(f32[2,16,256]{2,1,0:T(8,128)S(1)} %get-tuple-element.43), channel_id=1, source_target_pairs={{0,8},{2,10},{4,12},{6,14},{8,0},{10,2},{12,4},{14,6},{1,9},{3,11}... | collective-permute-start | bytes 98312 | tf_op jit(solution)/shard_map/ppermute | solution.py:495
  30.7 5.7 %collective-permute-start.13 = (f32[2,16,256]{2,1,0:T(8,128)S(1)}, f32[2,16,256]{2,1,0:T(8,128)S(1)}, u32[]{:S(2)}, u32[]{:S(2)}) collective-permute-start(f32[2,16,256]{2,1,0:T(8,128)S(1)} %get-tuple-element.44), channel_id=1, source_target_pairs={{0,4},{2,6},{4,0},{6,2},{8,12},{10,14},{12,8},{14,10},{1,5},{3,7},... | collective-permute-start | bytes 98312 | tf_op jit(solution)/shard_map/ppermute | solution.py:495
  32.5 3.8 %collective-permute-start.14 = (f32[16,384]{1,0:T(8,128)S(1)}, f32[16,384]{1,0:T(8,128)S(1)}, u32[]{:S(2)}, u32[]{:S(2)}) collective-permute-start(f32[16,384]{1,0:T(8,128)S(1)} %get-tuple-element.46), channel_id=1, source_target_pairs={{0,2},{2,0},{4,6},{6,4},{8,10},{10,8},{12,14},{14,12},{1,3},{3,1},... | collective-permute-start | bytes 73736 | tf_op jit(solution)/shard_map/ppermute | solution.py:495
  36.3 1.3 %collective-permute-start.15 = (f32[16,1280]{1,0:T(8,128)S(1)}, f32[16,1280]{1,0:T(8,128)S(1)}, u32[]{:S(2)}, u32[]{:S(2)}) collective-permute-start(f32[16,1280]{1,0:T(8,128)S(1)} %collect.1.mine_ref), channel_id=1, source_target_pairs={{0,1},{1,0},{2,3},{3,2},{4,5},{5,4},{6,7},{7,6},{8,9},{9,8},{10,11... | collective-permute-start | bytes 245768 | tf_op jit(solution)/shard_map/ppermute | solution.py:491
  37.7 1.6 %copy-start.1 = (bf16[2,256,2048]{2,1,0:T(8,128)(2,1)S(1)}, bf16[2,256,2048]{2,1,0:T(8,128)(2,1)}, u32[]{:S(2)}) copy-start(bf16[2,256,2048]{2,1,0:T(8,128)(2,1)} %param.8) | copy-start | bytes 6291460
  42.2 4.4 %collective-permute-start.16 = (f16[16,2304]{1,0:T(8,128)(2,1)S(1)}, f16[16,2304]{1,0:T(8,128)(2,1)S(1)}, u32[]{:S(2)}, u32[]{:S(2)}) collective-permute-start(f16[16,2304]{1,0:T(8,128)(2,1)S(1)} %pad_maximum_fusion), channel_id=1, source_target_pairs={{0,2},{2,0},{4,6},{6,4},{8,10},{10,8},{12,14},{14,12},{1,3},{3,1},... | collective-permute-start | bytes 221192 | tf_op jit(solution)/shard_map/ppermute | solution.py:495
  47.3 8.0 %collective-permute-start.19 = (f16[16,2304]{1,0:T(8,128)(2,1)S(1)}, f16[16,2304]{1,0:T(8,128)(2,1)S(1)}, u32[]{:S(2)}, u32[]{:S(2)}) collective-permute-start(f16[16,2304]{1,0:T(8,128)(2,1)S(1)} %pad_maximum_fusion.1), channel_id=1, source_target_pairs={{0,8},{2,10},{4,12},{6,14},{8,0},{10,2},{12,4},{14,6},{1,9},{3,11}... | collective-permute-start | bytes 221192 | tf_op jit(solution)/shard_map/ppermute | solution.py:495
  48.5 7.0 %collective-permute-start.18 = (f16[16,2304]{1,0:T(8,128)(2,1)S(1)}, f16[16,2304]{1,0:T(8,128)(2,1)S(1)}, u32[]{:S(2)}, u32[]{:S(2)}) collective-permute-start(f16[16,2304]{1,0:T(8,128)(2,1)S(1)} %pad_maximum_fusion.1), channel_id=1, source_target_pairs={{0,12},{2,14},{4,8},{6,10},{8,4},{10,6},{12,0},{14,2},{1,13},{3,15... | collective-permute-start | bytes 221192 | tf_op jit(solution)/shard_map/ppermute | solution.py:495
  50.0 5.8 %collective-permute-start.17 = (f16[16,2304]{1,0:T(8,128)(2,1)S(1)}, f16[16,2304]{1,0:T(8,128)(2,1)S(1)}, u32[]{:S(2)}, u32[]{:S(2)}) collective-permute-start(f16[16,2304]{1,0:T(8,128)(2,1)S(1)} %pad_maximum_fusion.1), channel_id=1, source_target_pairs={{0,4},{2,6},{4,0},{6,2},{8,12},{10,14},{12,8},{14,10},{1,5},{3,7},... | collective-permute-start | bytes 221192 | tf_op jit(solution)/shard_map/ppermute | solution.py:495
